TPU v7x, 512 devices: a whole 4x8x8 slice. The times are simulated.
512 devices in a mesh: expert: 16 (over y, core), tensor: 8 (over z), dp: 4 (over x).
Axes of the slice: x: 4, y: 8, z: 8, core: 2. Of those that a mesh axis runs over, the one named last changes fastest.
Arguments:
- enc_tokens: bfloat16 [2048, 2048], P('expert', ('tensor', 'dp')), may hold values from -6 to 6
- enc_experts: int32 [2048, 2], P('expert'), may hold values from 0 to 15, all different within a row; in each aligned block of 128 rows (0 to 127, 128 to 255, ...) at most 32 rows name the same one
- enc_levels: int32 [2048, 2], P('expert'), may hold values from 1 to 255
- enc_w_in: bfloat16 [16, 2048, 8192], P('expert', None, ('tensor', 'dp')), may hold values from -0.125 to 0.125
- enc_w_out: bfloat16 [16, 8192, 2048], P('expert', ('tensor', 'dp')), may hold values from -0.125 to 0.125
- dec_tokens: bfloat16 [2304, 2048], P('expert', ('tensor', 'dp')), may hold values from -6 to 6
- dec_lengths: int32 [16, 16], P('expert'), may hold values from 1 to 16, as said below
- dec_language: int32 [256, 1], P('expert'), may hold values from 0 to 15, as said below
- dec_w_in: bfloat16 [16, 2048, 8192], P('expert', None, ('tensor', 'dp')), may hold values from -0.125 to 0.125
- dec_w_out: bfloat16 [16, 8192, 2048], P('expert', ('tensor', 'dp')), may hold values from -0.125 to 0.125
Outputs:
- enc_mixed: bfloat16 [2048, 2048], P('expert', ('tensor', 'dp'))
- dec_mixed: bfloat16 [2304, 2048], P('expert', ('tensor', 'dp'))
Inputs may be any that keep to these rules, and one draw needn't show every extreme that they name: `enc_experts`: the two experts of a token differ. Among the 256 assignments of one token group (aligned blocks of 128 rows), at most 32 name one expert, and in every draw some group gives some expert exactly 32. `dec_lengths`: each row sums to 144; exactly two entries of each row equal 16. `dec_language`: at most two of the 16 sentences of one token group (aligned blocks of 16 rows) go to one expert, so at most 32 of a group's decoder tokens reach one expert; in every draw some group sends exactly 32 tokens to one expert.
All inputs are finite; a program needn't handle non-finite values.
Results may differ from a plain program's by a relative error of at most 0.015.
Values may be sent and summed in bfloat16 or wider, within the bound.
No kernel may reach another device: no remote copies, remote signals or barrier semaphores. Data moves between devices by JAX's collectives and lax.ppermute only.
A program may use at most 64 MiB of HBM per device.

v0:
```python
import jax
import jax.numpy as jnp
from jax import lax
from jax.sharding import PartitionSpec as P


def expert_partial(row_block, weight_in, weight_out):
    hidden = jax.nn.relu(
        jnp.dot(row_block, weight_in[0], preferred_element_type=jnp.float32)
    ).astype(jnp.bfloat16)
    return jnp.dot(hidden, weight_out[0], preferred_element_type=jnp.float32).astype(jnp.bfloat16)


def route(tokens, chooser, senders):
    source = lax.all_gather(tokens, ("tensor", "dp"), axis=1, tiled=True)
    placed = jnp.dot(chooser, source, preferred_element_type=jnp.float32).astype(jnp.bfloat16)
    return placed.reshape(senders, -1, source.shape[1])


def experts_apply(placed, weight_in, weight_out):
    arrived = lax.all_to_all(placed, "expert", split_axis=0, concat_axis=0, tiled=True)
    sources, capacity, columns = arrived.shape
    partial_value = expert_partial(
        arrived.reshape(sources * capacity, columns), weight_in, weight_out
    )
    partial_value = partial_value.reshape(sources, capacity, columns)
    summed = lax.psum_scatter(
        partial_value.astype(jnp.float32).astype(jnp.bfloat16),
        ("tensor", "dp"),
        scatter_dimension=2,
        tiled=True,
    )
    return lax.all_to_all(summed, "expert", split_axis=0, concat_axis=0, tiled=True)


def collect(result, chooser):
    flattened = result.reshape(-1, result.shape[2])
    picked = jnp.einsum("pr,pd->rd", chooser, flattened, preferred_element_type=jnp.float32)
    return picked.astype(jnp.bfloat16)


def slot_targets(flattened, senders, capacity):
    span = flattened.shape[0]
    onehot = (flattened[:, None] == jnp.arange(senders, dtype=jnp.int32)[None, :]).astype(
        jnp.float32
    )
    lower = (jnp.arange(span)[:, None] > jnp.arange(span)[None, :]).astype(jnp.float32)
    earlier = jnp.dot(lower, onehot, precision=lax.Precision.HIGHEST)
    slot = jnp.sum(earlier * onehot, axis=1).astype(jnp.int32)
    return flattened * capacity + slot


def encoder_choosers(experts, senders, capacity):
    tok_count = experts.shape[0]
    target = slot_targets(experts.reshape(-1), senders, capacity).reshape(tok_count, 2)
    positions = jnp.arange(senders * capacity, dtype=jnp.int32)[:, None]
    first = (positions == target[None, :, 0]).astype(jnp.bfloat16)
    second = (positions == target[None, :, 1]).astype(jnp.bfloat16)
    return (first, second)


def decoder_chooser(lengths, languages, senders, capacity, tok_count):
    sentence_ends = jnp.cumsum(lengths[0])
    places = jnp.arange(tok_count, dtype=jnp.int32)
    member = (places[:, None] >= sentence_ends[None, :]).astype(jnp.int32)
    sentence = jnp.sum(member, axis=1)
    membership = (
        sentence[:, None] == jnp.arange(lengths.shape[1], dtype=jnp.int32)[None, :]
    ).astype(jnp.int32)
    expert_id = jnp.sum(membership * languages[:, 0][None, :], axis=1)
    target = slot_targets(expert_id, senders, capacity)
    positions = jnp.arange(senders * capacity, dtype=jnp.int32)[:, None]
    return (positions == target[None, :]).astype(jnp.bfloat16)


def shards(
    enc_tokens,
    enc_experts,
    enc_levels,
    enc_w_in,
    enc_w_out,
    dec_tokens,
    dec_lengths,
    dec_language,
    dec_w_in,
    dec_w_out,
):
    senders = lax.axis_size("expert")
    tok_count = enc_tokens.shape[0]
    capacity = 4 * tok_count // senders
    first, second = encoder_choosers(enc_experts, senders, capacity)
    placed = route(enc_tokens, first + second, senders)
    result = experts_apply(placed, enc_w_in, enc_w_out)
    both = collect(result, jnp.concatenate([first, second], axis=1))
    levels = enc_levels.astype(jnp.float32)
    gate = levels / jnp.sum(levels, axis=1, keepdims=True)
    enc_mixed = (
        enc_tokens.astype(jnp.float32)
        + gate[:, 0:1] * both[:tok_count]
        + gate[:, 1:2] * both[tok_count:]
    )
    dec_count = dec_tokens.shape[0]
    sentence_count = dec_lengths.shape[1]
    dec_capacity = 2 * (2 * dec_count // (sentence_count + 2))
    chooser = decoder_chooser(dec_lengths, dec_language, senders, dec_capacity, dec_count)
    dec_placed = route(dec_tokens, chooser, senders)
    dec_result = experts_apply(dec_placed, dec_w_in, dec_w_out)
    dec_rows = collect(dec_result, chooser)
    dec_mixed = dec_tokens.astype(jnp.float32) + dec_rows
    return (enc_mixed.astype(jnp.bfloat16), dec_mixed.astype(jnp.bfloat16))


def solution(mesh):
    return jax.shard_map(
        shards,
        mesh=mesh,
        in_specs=(
            P("expert", ("tensor", "dp")),
            P("expert", None),
            P("expert", None),
            P("expert", None, ("tensor", "dp")),
            P("expert", ("tensor", "dp"), None),
            P("expert", ("tensor", "dp")),
            P("expert", None),
            P("expert", None),
            P("expert", None, ("tensor", "dp")),
            P("expert", ("tensor", "dp"), None),
        ),
        out_specs=(P("expert", ("tensor", "dp")), P("expert", ("tensor", "dp"))),
        check_vma=False,
    )
```

profile of v0, /device:TPU:1, one launch (start us, length us, event | category | flops | bytes accessed | tf_op | source)
XLA Modules:
  0.0 629.7 jit_solution(10645354870724459388)
XLA Ops:
  7.2 44.9 %all_gather.7 = bf16[144,2048]{0,1:T(8,128)(2,1)S(1)} all-gather(bf16[144,64]{0,1:T(8,128)(2,1)} %param.15), channel_id=1, replica_groups=mesh['expert'=16,'tensor'=8,'dp'=4] {'tensor','dp'}, dimensions={1}, use_global_device_ids=true | all-gather | bytes 608256 | tf_op jit(solution)/shard_map/all_gather | solution.py:15
  53.9 2.1 convolution_convert_fusion.1
  56.1 20.2 %all-to-all-start.2 = ((bf16[16,32,2048]{2,1,0:T(8,128)(2,1)}), bf16[16,32,2048]{2,1,0:T(8,128)(2,1)S(1)}, u32[]{:S(2)}, u32[]{:S(2)}) async-start(bf16[16,32,2048]{2,1,0:T(8,128)(2,1)} %bitcast.48), calls=%async_computation.2 | async-start | bytes 4194304 | tf_op jit(solution)/shard_map/all_to_all | solution.py:21
  77.0 40.1 %all_gather.6 = bf16[128,2048]{0,1:T(8,128)(2,1)S(1)} all-gather(bf16[128,64]{0,1:T(8,128)(2,1)S(1)} %copy-done.2), channel_id=1, replica_groups=mesh['expert'=16,'tensor'=8,'dp'=4] {'tensor','dp'}, dimensions={1}, use_global_device_ids=true | all-gather | bytes 540672 | tf_op jit(solution)/shard_map/all_gather | solution.py:15
  117.0 2.1 convolution_convert_fusion.3
  119.1 6.1 all-to-all-done.2
  125.2 1.3 copy-done.1
  126.5 9.4 %all-to-all-start = ((bf16[16,32,2048]{2,1,0:T(8,128)(2,1)}), bf16[16,32,2048]{2,1,0:T(8,128)(2,1)}, u32[]{:S(2)}, u32[]{:S(2)}) async-start(bf16[16,32,2048]{2,1,0:T(8,128)(2,1)} %bitcast.47), calls=%async_computation | async-start | bytes 4194304 | tf_op jit(solution)/shard_map/all_to_all | solution.py:21
  136.0 4.2 convolution_convert_fusion
  140.2 8.6 %copy.34 = bf16[16,32,2048]{1,0,2:T(8,128)(2,1)} copy(bf16[16,32,2048]{2,1,0:T(8,128)(2,1)S(1)} %bitcast.44) | data formatting | bytes 4194304
  148.8 12.0 %reshape.82 = bf16[2048,512]{1,0:T(8,128)(2,1)} reshape(bf16[2048,16,32]{2,1,0:T(8,128)(2,1)} %bitcast.42) | data formatting | bytes 4194304
  161.0 24.0 %all-to-all-done = bf16[16,32,2048]{2,1,0:T(8,128)(2,1)} async-done(((bf16[16,32,2048]{2,1,0:T(8,128)(2,1)}), bf16[16,32,2048]{2,1,0:T(8,128)(2,1)}, u32[]{:S(2)}, u32[]{:S(2)}) %all-to-all-start) | async-done | bytes 2097184 | tf_op jit(solution)/shard_map/all_to_all | solution.py:21
  185.0 4.5 convolution_convert_fusion.2
  189.5 8.6 %copy.32 = bf16[16,32,2048]{1,0,2:T(8,128)(2,1)} copy(bf16[16,32,2048]{2,1,0:T(8,128)(2,1)S(1)} %bitcast.45) | data formatting | bytes 4194304
  198.1 12.0 %reshape.80 = bf16[2048,512]{1,0:T(8,128)(2,1)} reshape(bf16[2048,16,32]{2,1,0:T(8,128)(2,1)} %bitcast.43) | data formatting | bytes 4194304
  210.9 163.1 %reduce-scatter.9.cloned.1.call-done = bf16[64,512]{1,0:T(8,128)(2,1)} async-done(((bf16[2048,512]{1,0:T(8,128)(2,1)}), bf16[64,512]{1,0:T(8,128)(2,1)}) %reduce-scatter.9.cloned.1.call-update) | async-done | bytes 65552
  374.0 1.0 reshape.83
  376.1 12.8 %all-to-all-start.3 = ((bf16[16,2,1024]{2,1,0:T(2,128)(2,1)}), bf16[16,2,1024]{2,1,0:T(2,128)(2,1)S(1)}, u32[]{:S(2)}, u32[]{:S(2)}) async-start(bf16[16,2,1024]{2,1,0:T(2,128)(2,1)} %reshape.87), calls=%async_computation.3 | async-start | bytes 131072 | tf_op jit(solution)/shard_map/all_to_all | solution.py:33
  388.9 210.4 %reduce-scatter.7.cloned.1.call-done = bf16[64,512]{1,0:T(8,128)(2,1)} async-done(((bf16[2048,512]{1,0:T(8,128)(2,1)}), bf16[64,512]{1,0:T(8,128)(2,1)}) %reduce-scatter.7.cloned.1.call-update) | async-done | bytes 65552
  599.3 1.0 reshape.81
  600.6 0.8 reshape.85
  601.4 12.6 %all-to-all-start.1 = ((bf16[16,2,1024]{2,1,0:T(2,128)(2,1)}), bf16[16,2,1024]{2,1,0:T(2,128)(2,1)S(1)}, u32[]{:S(2)}, u32[]{:S(2)}) async-start(bf16[16,2,1024]{2,1,0:T(2,128)(2,1)} %reshape.85), calls=%async_computation.1 | async-start | bytes 131072 | tf_op jit(solution)/shard_map/all_to_all | solution.py:33
  614.2 0.9 fusion.4
  615.1 6.8 %all-to-all-done.1 = bf16[16,2,1024]{2,1,0:T(2,128)(2,1)S(1)} async-done(((bf16[16,2,1024]{2,1,0:T(2,128)(2,1)}), bf16[16,2,1024]{2,1,0:T(2,128)(2,1)S(1)}, u32[]{:S(2)}, u32[]{:S(2)}) %all-to-all-start.1) | async-done | bytes 65568 | tf_op jit(solution)/shard_map/all_to_all | solution.py:33
  (42 shorter events, 6.0 us)
Async XLA Ops:
  7.2 128.8 %copy-start = (bf16[1,256,2048]{2,1,0:T(8,128)(2,1)S(1)}, bf16[1,256,2048]{2,1,0:T(8,128)(2,1)}, u32[]{:S(2)}) copy-start(bf16[1,256,2048]{2,1,0:T(8,128)(2,1)} %param.19) | copy-start | bytes 3145732
  56.0 20.2 %copy-start.4 = (s32[128,2]{0,1:T(2,128)S(1)}, s32[128,2]{0,1:T(2,128)}, u32[]{:S(2)}) copy-start(s32[128,2]{0,1:T(2,128)} %param.11) | copy-start | bytes 3076
  56.1 20.9 %copy-start.2 = (bf16[128,64]{0,1:T(8,128)(2,1)S(1)}, bf16[128,64]{0,1:T(8,128)(2,1)}, u32[]{:S(2)}) copy-start(bf16[128,64]{0,1:T(8,128)(2,1)} %param.10) | copy-start | bytes 49156
  56.1 69.2 %all-to-all-start.2 = ((bf16[16,32,2048]{2,1,0:T(8,128)(2,1)}), bf16[16,32,2048]{2,1,0:T(8,128)(2,1)S(1)}, u32[]{:S(2)}, u32[]{:S(2)}) async-start(bf16[16,32,2048]{2,1,0:T(8,128)(2,1)} %bitcast.48), calls=%async_computation.2 | async-start | bytes 4194304 | tf_op jit(solution)/shard_map/all_to_all | solution.py:21
  125.2 1.3 copy-start.1
  126.5 58.5 %all-to-all-start = ((bf16[16,32,2048]{2,1,0:T(8,128)(2,1)}), bf16[16,32,2048]{2,1,0:T(8,128)(2,1)}, u32[]{:S(2)}, u32[]{:S(2)}) async-start(bf16[16,32,2048]{2,1,0:T(8,128)(2,1)} %bitcast.47), calls=%async_computation | async-start | bytes 4194304 | tf_op jit(solution)/shard_map/all_to_all | solution.py:21
  135.9 238.1 %reduce-scatter.9.cloned.1.call-start = ((), (), s32[]{:S(2)}) async-start(), calls=%async_computation.7 | async-start | bytes 2162688
  160.8 438.5 %reduce-scatter.7.cloned.1.call-start = ((), (), s32[]{:S(2)}) async-start(), calls=%async_computation.6 | async-start | bytes 2162688
  210.1 0.7 copy-start.5
  210.1 404.1 %copy-start.3 = (bf16[144,64]{0,1:T(8,128)(2,1)S(1)}, bf16[144,64]{0,1:T(8,128)(2,1)}, u32[]{:S(2)}) copy-start(bf16[144,64]{0,1:T(8,128)(2,1)} %param.15) | copy-start | bytes 55300
  376.1 225.3 %all-to-all-start.3 = ((bf16[16,2,1024]{2,1,0:T(2,128)(2,1)}), bf16[16,2,1024]{2,1,0:T(2,128)(2,1)S(1)}, u32[]{:S(2)}, u32[]{:S(2)}) async-start(bf16[16,2,1024]{2,1,0:T(2,128)(2,1)} %reshape.87), calls=%async_computation.3 | async-start | bytes 131072 | tf_op jit(solution)/shard_map/all_to_all | solution.py:33
  601.4 20.4 %all-to-all-start.1 = ((bf16[16,2,1024]{2,1,0:T(2,128)(2,1)}), bf16[16,2,1024]{2,1,0:T(2,128)(2,1)S(1)}, u32[]{:S(2)}, u32[]{:S(2)}) async-start(bf16[16,2,1024]{2,1,0:T(2,128)(2,1)} %reshape.85), calls=%async_computation.1 | async-start | bytes 131072 | tf_op jit(solution)/shard_map/all_to_all | solution.py:33
Sparse Core Ops, SparseCore 0:
  160.9 213.0 reduce-scatter.8
  379.0 220.2 reduce-scatter.6
where the time goes:
time: 631 us; the launch traced here: 630 us
  waiting for transfers between devices  410 us (65%)
  blocking collectives  84.9 us (13%)
  starting transfers between devices  55.3 us (9%)
  local copies, waits for them, and re-layouts  48.8 us (8%)
  matrix products  14.3 us (2%)
  between operations  14.2 us (2%)
    unnamed x4, waiting for transfers between devices  374 us
    all_gather x2, blocking collectives, route(): source = lax.all_gather(tokens, ('tensor', 'dp'), axis=1, tiled=True)  84.9 us
    unnamed x25, local copies, waits for them, and re-layouts  47.7 us
    all_to_all x2, waiting for transfers between devices, experts_apply(): lax.all_to_all(placed, 'expert', split_axis=0, concat_axis=0, tiled=True)  30.1 us
    all_to_all x2, starting transfers between devices, experts_apply(): lax.all_to_all(placed, 'expert', split_axis=0, concat_axis=0, tiled=True)  29.6 us
    all_to_all x2, starting transfers between devices, experts_apply(): lax.all_to_all(summed, 'expert', split_axis=0, concat_axis=0, tiled=True)  25.4 us
  transfers between devices with their start and end apart: 6, of which 5 were waited for; matrix products, arithmetic and copies ran while one was open for 9% of the time, Pallas kernels for 0%

commit v1 on v0

v1 whole, which is shorter than its diff:
```python
import jax
import jax.numpy as jnp
from jax import lax
from jax.experimental import pallas as pl
from jax.experimental.pallas import tpu as pltpu
from jax.sharding import PartitionSpec as P

BF = jnp.bfloat16
F32 = jnp.float32
EXPERTS = 16
CAP = 32
ROWS = EXPERTS * CAP
FEATS = 64
T = 8
DP = 4
UNITS = 256
VMEM = pl.BlockSpec(memory_space=pltpu.VMEM)
SMEM = pl.BlockSpec(memory_space=pltpu.SMEM)


def call(body, out_shape, n_in, *, smem=(), flops=0, moved=0):
    many = isinstance(out_shape, (tuple, list))
    return pl.pallas_call(
        body,
        out_shape=out_shape,
        in_specs=[SMEM if i in smem else VMEM for i in range(n_in)],
        out_specs=[VMEM] * len(out_shape) if many else VMEM,
        compiler_params=pltpu.CompilerParams(vmem_limit_bytes=32 * 1024 * 1024),
        cost_estimate=pl.CostEstimate(flops=flops, bytes_accessed=moved, transcendentals=0),
    )


def shape(dims, dtype=BF):
    return jax.ShapeDtypeStruct(dims, dtype)


def nt(a, b):
    return lax.dot_general(a, b, (((1,), (1,)), ((), ())), preferred_element_type=F32)


def nn(a, b):
    return lax.dot_general(a, b, (((1,), (0,)), ((), ())), preferred_element_type=F32)


def iota(dims, axis):
    return lax.broadcasted_iota(jnp.int32, dims, axis)


def pick(target):
    span = target.shape[1]
    return (iota((ROWS, span), 0) == target).astype(F32).astype(BF)


def slots(onehots):
    total = sum(onehots)
    span = total.shape[1]
    before = (iota((span, span), 0) < iota((span, span), 1)).astype(F32).astype(BF)
    earlier = nn(total.astype(BF), before)
    return [jnp.sum(o * earlier, axis=0, keepdims=True).astype(jnp.int32) for o in onehots]


def place_body(experts, lengths, languages, enc, dec, sent, enc_at, dec_at):
    enc_count = enc.shape[1]
    dec_count = dec.shape[1]
    rank = iota((EXPERTS, enc_count), 0)
    named = [experts[k : k + 1, :] for k in range(2)]
    found = slots([(rank == e).astype(F32) for e in named])
    targets = [e * CAP + s for e, s in zip(named, found)]
    for k in range(2):
        enc_at[k : k + 1, :] = targets[k]

    sents = lengths.shape[1]
    square = (sents, sents)
    upto = iota(square, 1) <= iota(square, 0)
    same = iota(square, 1) == iota(square, 0)
    length = jnp.broadcast_to(lengths[...], square)
    language = jnp.broadcast_to(languages[...], square)
    ends = jnp.sum(jnp.where(upto, length, 0), axis=1, keepdims=True)
    begins = ends - jnp.sum(jnp.where(same, length, 0), axis=1, keepdims=True)
    spoken = jnp.sum(jnp.where(same, language, 0), axis=1, keepdims=True)
    places = iota((sents, dec_count), 1)
    member = (places >= begins) & (places < ends)
    chosen = jnp.sum(jnp.where(member, spoken, 0), axis=0, keepdims=True)
    (dec_slot,) = slots([(iota((EXPERTS, dec_count), 0) == chosen).astype(F32)])
    dec_target = chosen * CAP + dec_slot
    dec_at[...] = dec_target

    zeros_enc = jnp.zeros((FEATS, enc_count), BF)
    zeros_dec = jnp.zeros((FEATS, dec_count), BF)
    wide_enc = jnp.concatenate([enc[...], zeros_enc], axis=0)
    wide_dec = jnp.concatenate([zeros_dec, dec[...]], axis=0)
    enc_pick = pick(targets[0]) + pick(targets[1])
    rows = nt(enc_pick, wide_enc) + nt(pick(dec_target), wide_dec)
    sent[...] = rows.astype(BF).reshape(EXPERTS, CAP, 2 * FEATS)


def spread_body(got, enc, dec):
    turned = got[...].reshape(ROWS, 2 * FEATS).astype(F32).T.astype(BF)
    for t in range(T):
        enc[t] = turned[:FEATS]
        dec[t] = turned[FEATS:]


def turn_body(w_in, w_out, in_turned, out_turned):
    for d in range(DP):
        cut = [(t * DP + d) * FEATS for t in range(T)]
        block = jnp.concatenate([w_in[c : c + FEATS, :] for c in cut], axis=0)
        in_turned[d] = block.T
    for c in range(16):
        turned = w_out[:, c * 128 : (c + 1) * 128].T
        for half in range(2):
            b = c * 2 + half
            t, d = b // DP, b % DP
            out_turned[d, t * FEATS : (t + 1) * FEATS, :] = turned[half * FEATS : (half + 1) * FEATS]


def expert_body(me, x0, x1, x2, x3, w_in, w_out, p0, p1, p2, p3):
    d = me[0]
    hidden = None
    for k, x in enumerate((x0, x1, x2, x3)):
        source = lax.rem(d - k + DP, DP)
        term = nn(w_in[source], x[...])
        hidden = term if hidden is None else hidden + term
    hidden = jnp.maximum(hidden, 0.0).astype(BF)
    for k, p in enumerate((p0, p1, p2, p3)):
        goal = lax.rem(d + k, DP)
        p[...] = nn(w_out[goal], hidden).astype(BF)


def add_body(a, b, c, d, out):
    total = (a[...].astype(F32) + b[...].astype(F32)) + (c[...].astype(F32) + d[...].astype(F32))
    out[...] = total.astype(BF)


def pack_body(enc, dec, sent):
    def total(ref):
        acc = ref[0].astype(F32)
        for t in range(1, T):
            acc = acc + ref[t].astype(F32)
        return acc.astype(BF).astype(F32)

    both = jnp.concatenate([total(enc), total(dec)], axis=0)
    sent[...] = both.T.astype(BF).reshape(EXPERTS, CAP, 2 * FEATS)


def mix_body(got, enc_at, dec_at, levels, enc, dec, enc_out, dec_out):
    turned = got[...].reshape(ROWS, 2 * FEATS).astype(F32).T.astype(BF)
    level = levels[...].astype(F32)
    whole = level[0:1] + level[1:2]
    mixed = enc[...].astype(F32)
    for k in range(2):
        rows = nn(turned[:FEATS], pick(enc_at[k : k + 1, :]))
        mixed = mixed + (level[k : k + 1] / whole) * rows
    enc_out[...] = mixed.astype(BF)
    rows = nn(turned[FEATS:], pick(dec_at[...]))
    dec_out[...] = (dec[...].astype(F32) + rows).astype(BF)


def shift(value, k):
    return lax.ppermute(value, "dp", [(i, (i + k) % DP) for i in range(DP)])


def gather(block, turned, me):
    over_t = lax.all_to_all(block, "tensor", split_axis=0, concat_axis=0, tiled=True)
    own = over_t.reshape(T * FEATS, ROWS)
    return [own] + [shift(own, k) for k in (1, 2, 3)]


def expert(blocks, turned, me):
    part = shape((T * FEATS, ROWS))
    work = 4 * ROWS * UNITS * T * DP * FEATS
    return call(expert_body, [part] * 4, 7, smem=(0,), flops=work, moved=6 << 20)(me, *blocks, *turned)


def scatter(parts):
    sums = [parts[0]] + [shift(parts[k], k) for k in (1, 2, 3)]
    total = call(add_body, shape((T * FEATS, ROWS)), 4, moved=5 << 19)(*sums)
    total = total.reshape(T, FEATS, ROWS)
    return lax.all_to_all(total, "tensor", split_axis=0, concat_axis=0, tiled=True)


def shards(
    enc_tokens,
    enc_experts,
    enc_levels,
    enc_w_in,
    enc_w_out,
    dec_tokens,
    dec_lengths,
    dec_language,
    dec_w_in,
    dec_w_out,
):
    me = lax.axis_index("dp").astype(jnp.int32).reshape(1)
    enc = enc_tokens.T
    dec = dec_tokens.T
    packed = shape((EXPERTS, CAP, 2 * FEATS))
    sent, enc_at, dec_at = call(
        place_body,
        [packed, shape((2, enc.shape[1]), jnp.int32), shape((1, dec.shape[1]), jnp.int32)],
        5,
        moved=1 << 18,
    )(enc_experts.T, dec_lengths, dec_language.T, enc, dec)
    got = lax.all_to_all(sent, "expert", split_axis=0, concat_axis=0, tiled=True)

    def turn(w_in, w_out):
        out = [shape((DP, UNITS, T * FEATS)), shape((DP, T * FEATS, UNITS))]
        return call(turn_body, out, 2, moved=4 << 20)(w_in[0], w_out[0])

    enc_turned = turn(enc_w_in, enc_w_out)
    dec_turned = turn(dec_w_in, dec_w_out)
    block = shape((T, FEATS, ROWS))
    enc_block, dec_block = call(spread_body, [block, block], 1, moved=1 << 20)(got)

    enc_x = gather(enc_block, enc_turned, me)
    dec_x = gather(dec_block, dec_turned, me)
    enc_sums = scatter(expert(enc_x, enc_turned, me))
    dec_sums = scatter(expert(dec_x, dec_turned, me))

    back = call(pack_body, packed, 2, moved=1 << 20)(enc_sums, dec_sums)
    got = lax.all_to_all(back, "expert", split_axis=0, concat_axis=0, tiled=True)
    enc_out, dec_out = call(
        mix_body, [shape(enc.shape), shape(dec.shape)], 6, moved=1 << 18
    )(got, enc_at, dec_at, enc_levels.T, enc, dec)
    return enc_out.T, dec_out.T


def solution(mesh):
    return jax.shard_map(
        shards,
        mesh=mesh,
        in_specs=(
            P("expert", ("tensor", "dp")),
            P("expert", None),
            P("expert", None),
            P("expert", None, ("tensor", "dp")),
            P("expert", ("tensor", "dp"), None),
            P("expert", ("tensor", "dp")),
            P("expert", None),
            P("expert", None),
            P("expert", None, ("tensor", "dp")),
            P("expert", ("tensor", "dp"), None),
        ),
        out_specs=(P("expert", ("tensor", "dp")), P("expert", ("tensor", "dp"))),
        check_vma=False,
    )
```

time: 631 us -> 204 us (0.32)
  waiting for transfers between devices: 410 us -> 56.5 us
  local copies, waits for them, and re-layouts: 48.8 us -> 4.7 us
  matrix products: 14.3 us -> 0 us
  between operations: 14.2 us -> 0.92 us
  Pallas kernels: 0 us -> 10.6 us
  blocking collectives: 84.9 us -> 78.2 us
    unnamed x4 -> x0, waiting for transfers between devices: 374 us -> none
    all_gather x2 -> x0, blocking collectives: 84.9 us -> none  [route(): source = lax.all_gather(tokens, ('tensor', 'dp'), axis=1, tiled=True)]
    all_to_all x0 -> x4, blocking collectives: none -> 78.2 us  [the longest x1 27.2 us: gather(): lax.all_to_all(block, 'tensor', split_axis=0, concat_axis=0, tiled=True)]
    ppermute x0 -> x12, waiting for transfers between devices: none -> 56.5 us  [shift(): return lax.ppermute(value, 'dp', [(i, (i + k) % DP) for i in range(DP)])]
    all_to_all x4 -> x2, starting transfers between devices: 55.1 us -> 7.13 us  [the longest x1 3.62 us: scatter(): lax.all_to_all(total, 'tensor', split_axis=0, concat_axis=0, tiled=True)]
    ppermute x0 -> x12, starting transfers between devices: none -> 43.5 us  [shift(): return lax.ppermute(value, 'dp', [(i, (i + k) % DP) for i in range(DP)])]
    unnamed x25 -> x30, local copies, waits for them, and re-layouts: 47.7 us -> 4.7 us
    all_to_all x4 -> x2, waiting for transfers between devices: 36.9 us -> 0.01 us  [the longest x1 0.01 us: gather(): lax.all_to_all(block, 'tensor', split_axis=0, concat_axis=0, tiled=True)]
  transfers between devices with their start and end apart: 6 -> 14, of which waited for: 5 -> 10; matrix products, arithmetic and copies ran while one was open for 9% -> 0% of each run, Pallas kernels for 0% -> 4%
where the time goes in v1:
time: 204 us; the launch traced here: 202 us
  blocking collectives  78.2 us (38%)
  waiting for transfers between devices  56.5 us (28%)
  starting transfers between devices  50.6 us (25%)
  Pallas kernels  10.6 us (5%)
  local copies, waits for them, and re-layouts  4.7 us (2%)
    ppermute x12, waiting for transfers between devices, shift(): return lax.ppermute(value, 'dp', [(i, (i + k) % DP) for i in range(DP)])  56.5 us
    ppermute x12, starting transfers between devices, shift(): return lax.ppermute(value, 'dp', [(i, (i + k) % DP) for i in range(DP)])  43.5 us
    all_to_all x1, blocking collectives, gather(): lax.all_to_all(block, 'tensor', split_axis=0, concat_axis=0, tiled=True)  27.2 us
    all_to_all x1, blocking collectives, shards(): lax.all_to_all(sent, 'expert', split_axis=0, concat_axis=0, tiled=True)  18.5 us
    all_to_all x1, blocking collectives, scatter(): lax.all_to_all(total, 'tensor', split_axis=0, concat_axis=0, tiled=True)  17.7 us
    all_to_all x1, blocking collectives, shards(): lax.all_to_all(back, 'expert', split_axis=0, concat_axis=0, tiled=True)  14.8 us
    pallas_call x2, Pallas kernels, expert(): call(expert_body, [part] * 4, 7, smem=(0,), flops=work, moved=6 << 20)  6.36 us
    unnamed x30, local copies, waits for them, and re-layouts  4.7 us
  transfers between devices with their start and end apart: 14, of which 10 were waited for; matrix products, arithmetic and copies ran while one was open for 0% of the time, Pallas kernels for 4%

profile of v1, /device:TPU:1, one launch (start us, length us, event | category | flops | bytes accessed | tf_op | source)
XLA Modules:
  0.0 201.5 jit_solution(16556842459770068606)
XLA Ops:
  3.3 18.5 %all_to_all.30.got = bf16[16,32,128]{2,1,0:T(8,128)(2,1)S(1)} all-to-all(bf16[16,32,128]{2,1,0:T(8,128)(2,1)S(1)} %get-tuple-element.21), channel_id=1, replica_groups=mesh['expert'=16,'tensor'=8,'dp'=4] {'expert'}, dimensions={0} | all-to-all | bytes 262144 | tf_op jit(solution)/shard_map/all_to_all | solution.py:204
  22.0 27.2 %all_to_all.31 = bf16[8,64,512]{2,1,0:T(8,128)(2,1)S(1)} all-to-all(bf16[8,64,512]{2,1,0:T(8,128)(2,1)S(1)} %get-tuple-element.29), channel_id=1, replica_groups=mesh['expert'=16,'tensor'=8,'dp'=4] {'tensor'}, dimensions={0} | all-to-all | bytes 1048576 | tf_op jit(solution)/shard_map/all_to_all | solution.py:164
  49.2 3.1 %collective-permute-start.6 = (bf16[512,512]{1,0:T(8,128)(2,1)S(1)}, bf16[512,512]{1,0:T(8,128)(2,1)}, u32[]{:S(2)}, u32[]{:S(2)}) collective-permute-start(bf16[512,512]{1,0:T(8,128)(2,1)S(1)} %bitcast.20), channel_id=1, source_target_pairs={{0,1},{1,2},{2,3},{3,0},{4,5},{5,6},{6,7},{7,4},{8,9},{9,10},{10,1... | collective-permute-start | bytes 1572872 | tf_op jit(solution)/shard_map/ppermute | solution.py:160
  52.3 4.4 %collective-permute-start.7 = (bf16[512,512]{1,0:T(8,128)(2,1)S(1)}, bf16[512,512]{1,0:T(8,128)(2,1)}, u32[]{:S(2)}, u32[]{:S(2)}) collective-permute-start(bf16[512,512]{1,0:T(8,128)(2,1)S(1)} %bitcast.21), channel_id=1, source_target_pairs={{0,2},{1,3},{2,0},{3,1},{4,6},{5,7},{6,4},{7,5},{8,10},{9,11},{10,... | collective-permute-start | bytes 1572872 | tf_op jit(solution)/shard_map/ppermute | solution.py:160
  56.6 3.1 %collective-permute-start.8 = (bf16[512,512]{1,0:T(8,128)(2,1)S(1)}, bf16[512,512]{1,0:T(8,128)(2,1)}, u32[]{:S(2)}, u32[]{:S(2)}) collective-permute-start(bf16[512,512]{1,0:T(8,128)(2,1)S(1)} %bitcast.22), channel_id=1, source_target_pairs={{0,3},{1,0},{2,1},{3,2},{4,7},{5,4},{6,5},{7,6},{8,11},{9,8},{10,9... | collective-permute-start | bytes 1572872 | tf_op jit(solution)/shard_map/ppermute | solution.py:160
  59.7 3.5 %all-to-all-start.1 = ((bf16[8,64,512]{2,1,0:T(8,128)(2,1)}), bf16[8,64,512]{2,1,0:T(8,128)(2,1)S(1)}, u32[]{:S(2)}, u32[]{:S(2)}) async-start(bf16[8,64,512]{2,1,0:T(8,128)(2,1)} %copy-done.6), calls=%async_computation.1 | async-start | bytes 1048576 | tf_op jit(solution)/shard_map/all_to_all | solution.py:164
  65.4 12.2 %collective-permute-done.7.x2 = bf16[512,512]{1,0:T(8,128)(2,1)} collective-permute-done((bf16[512,512]{1,0:T(8,128)(2,1)S(1)}, bf16[512,512]{1,0:T(8,128)(2,1)}, u32[]{:S(2)}, u32[]{:S(2)}) %collective-permute-start.7) | collective-permute-done | bytes 524320 | tf_op jit(solution)/shard_map/ppermute | solution.py:160
  78.9 3.6 %shard_map.119 = (bf16[512,512]{1,0:T(8,128)(2,1)S(1)}, bf16[512,512]{1,0:T(8,128)(2,1)S(1)}, bf16[512,512]{1,0:T(8,128)(2,1)}, bf16[512,512]{1,0:T(8,128)(2,1)}) custom-call(s32[1]{0:T(128)} %bitcast.me, bf16[512,512]{1,0:T(8,128)(2,1)S(1)} %bitcast.23, bf16[512,512]{1,0:T(8,128)(2,1)} %collective-permute-done.6.x1, ...), custom_call_target="tpu_custom_call" | custom-call | flops 1073741824 | bytes 6291456 | tf_op jit(solution)/shard_map/pallas_call | solution.py:172
  82.5 4.6 %collective-permute-start.10 = (bf16[512,512]{1,0:T(8,128)(2,1)}, bf16[512,512]{1,0:T(8,128)(2,1)S(1)}, u32[]{:S(2)}, u32[]{:S(2)}) collective-permute-start(bf16[512,512]{1,0:T(8,128)(2,1)} %get-tuple-element.34), channel_id=1, source_target_pairs={{0,2},{1,3},{2,0},{3,1},{4,6},{5,7},{6,4},{7,5},{8,10},{9,11},{10,... | collective-permute-start | bytes 1572872 | tf_op jit(solution)/shard_map/ppermute | solution.py:160
  87.1 4.7 %collective-permute-start.11 = (bf16[512,512]{1,0:T(8,128)(2,1)}, bf16[512,512]{1,0:T(8,128)(2,1)S(1)}, u32[]{:S(2)}, u32[]{:S(2)}) collective-permute-start(bf16[512,512]{1,0:T(8,128)(2,1)} %get-tuple-element.35), channel_id=1, source_target_pairs={{0,3},{1,0},{2,1},{3,2},{4,7},{5,4},{6,5},{7,6},{8,11},{9,8},{10,9... | collective-permute-start | bytes 1572872 | tf_op jit(solution)/shard_map/ppermute | solution.py:160
  95.8 5.7 %collective-permute-start.1 = (bf16[512,512]{1,0:T(8,128)(2,1)S(1)}, bf16[512,512]{1,0:T(8,128)(2,1)}, u32[]{:S(2)}, u32[]{:S(2)}) collective-permute-start(bf16[512,512]{1,0:T(8,128)(2,1)S(1)} %bitcast.17), channel_id=1, source_target_pairs={{0,2},{1,3},{2,0},{3,1},{4,6},{5,7},{6,4},{7,5},{8,10},{9,11},{10,... | collective-permute-start | bytes 1572872 | tf_op jit(solution)/shard_map/ppermute | solution.py:160
  101.5 3.0 %collective-permute-start.2 = (bf16[512,512]{1,0:T(8,128)(2,1)S(1)}, bf16[512,512]{1,0:T(8,128)(2,1)}, u32[]{:S(2)}, u32[]{:S(2)}) collective-permute-start(bf16[512,512]{1,0:T(8,128)(2,1)S(1)} %bitcast.18), channel_id=1, source_target_pairs={{0,3},{1,0},{2,1},{3,2},{4,7},{5,4},{6,5},{7,6},{8,11},{9,8},{10,9... | collective-permute-start | bytes 1572872 | tf_op jit(solution)/shard_map/ppermute | solution.py:160
  104.5 7.1 %collective-permute-done.11.d = bf16[512,512]{1,0:T(8,128)(2,1)S(1)} collective-permute-done((bf16[512,512]{1,0:T(8,128)(2,1)}, bf16[512,512]{1,0:T(8,128)(2,1)S(1)}, u32[]{:S(2)}, u32[]{:S(2)}) %collective-permute-start.11) | collective-permute-done | bytes 524320 | tf_op jit(solution)/shard_map/ppermute | solution.py:160
  114.5 3.6 %all-to-all-start.4 = ((bf16[8,64,512]{2,1,0:T(8,128)(2,1)}), bf16[8,64,512]{2,1,0:T(8,128)(2,1)S(1)}, u32[]{:S(2)}, u32[]{:S(2)}) async-start(bf16[8,64,512]{2,1,0:T(8,128)(2,1)} %bitcast.12), calls=%async_computation.4 | async-start | bytes 1048576 | tf_op jit(solution)/shard_map/all_to_all | solution.py:179
  118.8 4.5 %collective-permute-done.x1 = bf16[512,512]{1,0:T(8,128)(2,1)} collective-permute-done((bf16[512,512]{1,0:T(8,128)(2,1)S(1)}, bf16[512,512]{1,0:T(8,128)(2,1)}, u32[]{:S(2)}, u32[]{:S(2)}) %collective-permute-start) | collective-permute-done | bytes 524320 | tf_op jit(solution)/shard_map/ppermute | solution.py:160
  123.3 8.4 %collective-permute-done.1.x2 = bf16[512,512]{1,0:T(8,128)(2,1)} collective-permute-done((bf16[512,512]{1,0:T(8,128)(2,1)S(1)}, bf16[512,512]{1,0:T(8,128)(2,1)}, u32[]{:S(2)}, u32[]{:S(2)}) %collective-permute-start.1) | collective-permute-done | bytes 524320 | tf_op jit(solution)/shard_map/ppermute | solution.py:160
  134.0 2.7 %shard_map.116 = (bf16[512,512]{1,0:T(8,128)(2,1)S(1)}, bf16[512,512]{1,0:T(8,128)(2,1)S(1)}, bf16[512,512]{1,0:T(8,128)(2,1)S(1)}, bf16[512,512]{1,0:T(8,128)(2,1)S(1)}) custom-call(s32[1]{0:T(128)} %bitcast.me, bf16[512,512]{1,0:T(8,128)(2,1)S(1)} %bitcast.19, bf16[512,512]{1,0:T(8,128)(2,1)} %collective-permute-done.x1, ...), custom_call_target="tpu_custom_call" | custom-call | flops 1073741824 | bytes 6291456 | tf_op jit(solution)/shard_map/pallas_call | solution.py:172
  136.8 4.8 %collective-permute-start.3 = (bf16[512,512]{1,0:T(8,128)(2,1)S(1)}, bf16[512,512]{1,0:T(8,128)(2,1)S(1)}, u32[]{:S(2)}, u32[]{:S(2)}) collective-permute-start(bf16[512,512]{1,0:T(8,128)(2,1)S(1)} %get-tuple-element.26), channel_id=1, source_target_pairs={{0,1},{1,2},{2,3},{3,0},{4,5},{5,6},{6,7},{7,4},{8,9},{9,10},{10,1... | collective-permute-start | bytes 1572872 | tf_op jit(solution)/shard_map/ppermute | solution.py:160
  141.6 3.3 %collective-permute-start.4 = (bf16[512,512]{1,0:T(8,128)(2,1)S(1)}, bf16[512,512]{1,0:T(8,128)(2,1)S(1)}, u32[]{:S(2)}, u32[]{:S(2)}) collective-permute-start(bf16[512,512]{1,0:T(8,128)(2,1)S(1)} %get-tuple-element.27), channel_id=1, source_target_pairs={{0,2},{1,3},{2,0},{3,1},{4,6},{5,7},{6,4},{7,5},{8,10},{9,11},{10,... | collective-permute-start | bytes 1572872 | tf_op jit(solution)/shard_map/ppermute | solution.py:160
  145.0 2.9 %collective-permute-start.5 = (bf16[512,512]{1,0:T(8,128)(2,1)S(1)}, bf16[512,512]{1,0:T(8,128)(2,1)S(1)}, u32[]{:S(2)}, u32[]{:S(2)}) collective-permute-start(bf16[512,512]{1,0:T(8,128)(2,1)S(1)} %get-tuple-element.28), channel_id=1, source_target_pairs={{0,3},{1,0},{2,1},{3,2},{4,7},{5,4},{6,5},{7,6},{8,11},{9,8},{10,9... | collective-permute-start | bytes 1572872 | tf_op jit(solution)/shard_map/ppermute | solution.py:160
  147.8 5.1 %collective-permute-done.3.b = bf16[512,512]{1,0:T(8,128)(2,1)S(1)} collective-permute-done((bf16[512,512]{1,0:T(8,128)(2,1)S(1)}, bf16[512,512]{1,0:T(8,128)(2,1)S(1)}, u32[]{:S(2)}, u32[]{:S(2)}) %collective-permute-start.3) | collective-permute-done | bytes 524320 | tf_op jit(solution)/shard_map/ppermute | solution.py:160
  153.0 12.8 %collective-permute-done.4.c = bf16[512,512]{1,0:T(8,128)(2,1)S(1)} collective-permute-done((bf16[512,512]{1,0:T(8,128)(2,1)S(1)}, bf16[512,512]{1,0:T(8,128)(2,1)S(1)}, u32[]{:S(2)}, u32[]{:S(2)}) %collective-permute-start.4) | collective-permute-done | bytes 524320 | tf_op jit(solution)/shard_map/ppermute | solution.py:160
  167.2 17.7 %all_to_all.32.enc = bf16[8,64,512]{2,1,0:T(8,128)(2,1)S(1)} all-to-all(bf16[8,64,512]{2,1,0:T(8,128)(2,1)S(1)} %bitcast.24), channel_id=1, replica_groups=mesh['expert'=16,'tensor'=8,'dp'=4] {'tensor'}, dimensions={0} | all-to-all | bytes 1048576 | tf_op jit(solution)/shard_map/all_to_all | solution.py:179
  185.1 14.8 %all_to_all.33.got = bf16[16,32,128]{2,1,0:T(8,128)(2,1)S(1)} all-to-all(bf16[16,32,128]{2,1,0:T(8,128)(2,1)S(1)} %shard_map.121), channel_id=1, replica_groups=mesh['expert'=16,'tensor'=8,'dp'=4] {'expert'}, dimensions={0} | all-to-all | bytes 262144 | tf_op jit(solution)/shard_map/all_to_all | solution.py:221
  (48 shorter events, 19.1 us)
Async XLA Ops:
  1.3 0.8 copy-start.7
  21.9 37.8 %copy-start.6 = (bf16[8,64,512]{2,1,0:T(8,128)(2,1)}, bf16[8,64,512]{2,1,0:T(8,128)(2,1)S(1)}, u32[]{:S(2)}) copy-start(bf16[8,64,512]{2,1,0:T(8,128)(2,1)S(1)} %get-tuple-element.22) | copy-start | bytes 1572868
  21.9 41.3 %copy-start = (bf16[1,2048,256]{2,1,0:T(8,128)(2,1)S(1)}, bf16[1,2048,256]{2,1,0:T(8,128)(2,1)}, u32[]{:S(2)}) copy-start(bf16[1,2048,256]{2,1,0:T(8,128)(2,1)} %param.18) | copy-start | bytes 3145732
  22.0 41.3 %copy-start.1 = (bf16[1,256,2048]{2,1,0:T(8,128)(2,1)S(1)}, bf16[1,256,2048]{2,1,0:T(8,128)(2,1)}, u32[]{:S(2)}) copy-start(bf16[1,256,2048]{2,1,0:T(8,128)(2,1)} %param.19) | copy-start | bytes 3145732
  49.2 16.3 %collective-permute-start.6 = (bf16[512,512]{1,0:T(8,128)(2,1)S(1)}, bf16[512,512]{1,0:T(8,128)(2,1)}, u32[]{:S(2)}, u32[]{:S(2)}) collective-permute-start(bf16[512,512]{1,0:T(8,128)(2,1)S(1)} %bitcast.20), channel_id=1, source_target_pairs={{0,1},{1,2},{2,3},{3,0},{4,5},{5,6},{6,7},{7,4},{8,9},{9,10},{10,1... | collective-permute-start | bytes 1572872 | tf_op jit(solution)/shard_map/ppermute | solution.py:160
  52.3 25.4 %collective-permute-start.7 = (bf16[512,512]{1,0:T(8,128)(2,1)S(1)}, bf16[512,512]{1,0:T(8,128)(2,1)}, u32[]{:S(2)}, u32[]{:S(2)}) collective-permute-start(bf16[512,512]{1,0:T(8,128)(2,1)S(1)} %bitcast.21), channel_id=1, source_target_pairs={{0,2},{1,3},{2,0},{3,1},{4,6},{5,7},{6,4},{7,5},{8,10},{9,11},{10,... | collective-permute-start | bytes 1572872 | tf_op jit(solution)/shard_map/ppermute | solution.py:160
  56.6 22.2 %collective-permute-start.8 = (bf16[512,512]{1,0:T(8,128)(2,1)S(1)}, bf16[512,512]{1,0:T(8,128)(2,1)}, u32[]{:S(2)}, u32[]{:S(2)}) collective-permute-start(bf16[512,512]{1,0:T(8,128)(2,1)S(1)} %bitcast.22), channel_id=1, source_target_pairs={{0,3},{1,0},{2,1},{3,2},{4,7},{5,4},{6,5},{7,6},{8,11},{9,8},{10,9... | collective-permute-start | bytes 1572872 | tf_op jit(solution)/shard_map/ppermute | solution.py:160
  59.7 34.1 %all-to-all-start.1 = ((bf16[8,64,512]{2,1,0:T(8,128)(2,1)}), bf16[8,64,512]{2,1,0:T(8,128)(2,1)S(1)}, u32[]{:S(2)}, u32[]{:S(2)}) async-start(bf16[8,64,512]{2,1,0:T(8,128)(2,1)} %copy-done.6), calls=%async_computation.1 | async-start | bytes 1048576 | tf_op jit(solution)/shard_map/all_to_all | solution.py:164
  82.5 19.0 %collective-permute-start.10 = (bf16[512,512]{1,0:T(8,128)(2,1)}, bf16[512,512]{1,0:T(8,128)(2,1)S(1)}, u32[]{:S(2)}, u32[]{:S(2)}) collective-permute-start(bf16[512,512]{1,0:T(8,128)(2,1)} %get-tuple-element.34), channel_id=1, source_target_pairs={{0,2},{1,3},{2,0},{3,1},{4,6},{5,7},{6,4},{7,5},{8,10},{9,11},{10,... | collective-permute-start | bytes 1572872 | tf_op jit(solution)/shard_map/ppermute | solution.py:160
  87.1 24.5 %collective-permute-start.11 = (bf16[512,512]{1,0:T(8,128)(2,1)}, bf16[512,512]{1,0:T(8,128)(2,1)S(1)}, u32[]{:S(2)}, u32[]{:S(2)}) collective-permute-start(bf16[512,512]{1,0:T(8,128)(2,1)} %get-tuple-element.35), channel_id=1, source_target_pairs={{0,3},{1,0},{2,1},{3,2},{4,7},{5,4},{6,5},{7,6},{8,11},{9,8},{10,9... | collective-permute-start | bytes 1572872 | tf_op jit(solution)/shard_map/ppermute | solution.py:160
  91.9 19.7 %collective-permute-start.9 = (bf16[512,512]{1,0:T(8,128)(2,1)S(1)}, bf16[512,512]{1,0:T(8,128)(2,1)S(1)}, u32[]{:S(2)}, u32[]{:S(2)}) collective-permute-start(bf16[512,512]{1,0:T(8,128)(2,1)S(1)} %get-tuple-element.33), channel_id=1, source_target_pairs={{0,1},{1,2},{2,3},{3,0},{4,5},{5,6},{6,7},{7,4},{8,9},{9,10},{10,1... | collective-permute-start | bytes 1572872 | tf_op jit(solution)/shard_map/ppermute | solution.py:160
  93.8 29.5 %collective-permute-start = (bf16[512,512]{1,0:T(8,128)(2,1)S(1)}, bf16[512,512]{1,0:T(8,128)(2,1)}, u32[]{:S(2)}, u32[]{:S(2)}) collective-permute-start(bf16[512,512]{1,0:T(8,128)(2,1)S(1)} %bitcast.16), channel_id=1, source_target_pairs={{0,1},{1,2},{2,3},{3,0},{4,5},{5,6},{6,7},{7,4},{8,9},{9,10},{10,1... | collective-permute-start | bytes 1572872 | tf_op jit(solution)/shard_map/ppermute | solution.py:160
  95.8 36.0 %collective-permute-start.1 = (bf16[512,512]{1,0:T(8,128)(2,1)S(1)}, bf16[512,512]{1,0:T(8,128)(2,1)}, u32[]{:S(2)}, u32[]{:S(2)}) collective-permute-start(bf16[512,512]{1,0:T(8,128)(2,1)S(1)} %bitcast.17), channel_id=1, source_target_pairs={{0,2},{1,3},{2,0},{3,1},{4,6},{5,7},{6,4},{7,5},{8,10},{9,11},{10,... | collective-permute-start | bytes 1572872 | tf_op jit(solution)/shard_map/ppermute | solution.py:160
  101.5 32.5 %collective-permute-start.2 = (bf16[512,512]{1,0:T(8,128)(2,1)S(1)}, bf16[512,512]{1,0:T(8,128)(2,1)}, u32[]{:S(2)}, u32[]{:S(2)}) collective-permute-start(bf16[512,512]{1,0:T(8,128)(2,1)S(1)} %bitcast.18), channel_id=1, source_target_pairs={{0,3},{1,0},{2,1},{3,2},{4,7},{5,4},{6,5},{7,6},{8,11},{9,8},{10,9... | collective-permute-start | bytes 1572872 | tf_op jit(solution)/shard_map/ppermute | solution.py:160
  111.6 0.8 copy-start.4
  112.4 1.0 copy-start.5
  113.5 4.7 %copy-start.3 = (bf16[1,256,2048]{2,1,0:T(8,128)(2,1)S(1)}, bf16[1,256,2048]{2,1,0:T(8,128)(2,1)}, u32[]{:S(2)}) copy-start(bf16[1,256,2048]{2,1,0:T(8,128)(2,1)} %param.14) | copy-start | bytes 3145732
  114.5 3.6 %copy-start.2 = (bf16[1,2048,256]{2,1,0:T(8,128)(2,1)S(1)}, bf16[1,2048,256]{2,1,0:T(8,128)(2,1)}, u32[]{:S(2)}) copy-start(bf16[1,2048,256]{2,1,0:T(8,128)(2,1)} %param.13) | copy-start | bytes 3145732
  114.5 52.7 %all-to-all-start.4 = ((bf16[8,64,512]{2,1,0:T(8,128)(2,1)}), bf16[8,64,512]{2,1,0:T(8,128)(2,1)S(1)}, u32[]{:S(2)}, u32[]{:S(2)}) async-start(bf16[8,64,512]{2,1,0:T(8,128)(2,1)} %bitcast.12), calls=%async_computation.4 | async-start | bytes 1048576 | tf_op jit(solution)/shard_map/all_to_all | solution.py:179
  136.8 16.2 %collective-permute-start.3 = (bf16[512,512]{1,0:T(8,128)(2,1)S(1)}, bf16[512,512]{1,0:T(8,128)(2,1)S(1)}, u32[]{:S(2)}, u32[]{:S(2)}) collective-permute-start(bf16[512,512]{1,0:T(8,128)(2,1)S(1)} %get-tuple-element.26), channel_id=1, source_target_pairs={{0,1},{1,2},{2,3},{3,0},{4,5},{5,6},{6,7},{7,4},{8,9},{9,10},{10,1... | collective-permute-start | bytes 1572872 | tf_op jit(solution)/shard_map/ppermute | solution.py:160
  141.6 24.2 %collective-permute-start.4 = (bf16[512,512]{1,0:T(8,128)(2,1)S(1)}, bf16[512,512]{1,0:T(8,128)(2,1)S(1)}, u32[]{:S(2)}, u32[]{:S(2)}) collective-permute-start(bf16[512,512]{1,0:T(8,128)(2,1)S(1)} %get-tuple-element.27), channel_id=1, source_target_pairs={{0,2},{1,3},{2,0},{3,1},{4,6},{5,7},{6,4},{7,5},{8,10},{9,11},{10,... | collective-permute-start | bytes 1572872 | tf_op jit(solution)/shard_map/ppermute | solution.py:160
  145.0 22.0 %collective-permute-start.5 = (bf16[512,512]{1,0:T(8,128)(2,1)S(1)}, bf16[512,512]{1,0:T(8,128)(2,1)S(1)}, u32[]{:S(2)}, u32[]{:S(2)}) collective-permute-start(bf16[512,512]{1,0:T(8,128)(2,1)S(1)} %get-tuple-element.28), channel_id=1, source_target_pairs={{0,3},{1,0},{2,1},{3,2},{4,7},{5,4},{6,5},{7,6},{8,11},{9,8},{10,9... | collective-permute-start | bytes 1572872 | tf_op jit(solution)/shard_map/ppermute | solution.py:160
  185.1 14.8 %copy-start.8 = (bf16[144,64]{0,1:T(8,128)(2,1)S(1)}, bf16[144,64]{0,1:T(8,128)(2,1)}, u32[]{:S(2)}) copy-start(bf16[144,64]{0,1:T(8,128)(2,1)} %param.15) | copy-start | bytes 55300
  185.1 14.8 %copy-start.10 = (bf16[128,64]{0,1:T(8,128)(2,1)S(1)}, bf16[128,64]{0,1:T(8,128)(2,1)}, u32[]{:S(2)}) copy-start(bf16[128,64]{0,1:T(8,128)(2,1)} %param.10) | copy-start | bytes 49156
  (5 other events, 3.4 us)

commit v2 on v1

--- a/solution.py
+++ b/solution.py
@@ -11,6 +11,8 @@
 CAP = 32
 ROWS = EXPERTS * CAP
 FEATS = 64
+HELD = 256
+LINES = CAP + 16
 T = 8
 DP = 4
 UNITS = 256
@@ -18,13 +20,14 @@
 SMEM = pl.BlockSpec(memory_space=pltpu.SMEM)
 
 
-def call(body, out_shape, n_in, *, smem=(), flops=0, moved=0):
+def call(body, out_shape, n_in, *, smem=(), smem_out=(), flops=0, moved=0):
     many = isinstance(out_shape, (tuple, list))
+    outs = [SMEM if i in smem_out else VMEM for i in range(len(out_shape))] if many else VMEM
     return pl.pallas_call(
         body,
         out_shape=out_shape,
         in_specs=[SMEM if i in smem else VMEM for i in range(n_in)],
-        out_specs=[VMEM] * len(out_shape) if many else VMEM,
+        out_specs=outs,
         compiler_params=pltpu.CompilerParams(vmem_limit_bytes=32 * 1024 * 1024),
         cost_estimate=pl.CostEstimate(flops=flops, bytes_accessed=moved, transcendentals=0),
     )
@@ -46,9 +49,9 @@
     return lax.broadcasted_iota(jnp.int32, dims, axis)
 
 
-def pick(target):
+def pick(target, rows=ROWS, first=0):
     span = target.shape[1]
-    return (iota((ROWS, span), 0) == target).astype(F32).astype(BF)
+    return (iota((rows, span), 0) + first == target).astype(F32).astype(BF)
 
 
 def slots(onehots):
@@ -81,7 +84,8 @@
     places = iota((sents, dec_count), 1)
     member = (places >= begins) & (places < ends)
     chosen = jnp.sum(jnp.where(member, spoken, 0), axis=0, keepdims=True)
-    (dec_slot,) = slots([(iota((EXPERTS, dec_count), 0) == chosen).astype(F32)])
+    dec_onehot = (iota((EXPERTS, dec_count), 0) == chosen).astype(F32)
+    (dec_slot,) = slots([dec_onehot])
     dec_target = chosen * CAP + dec_slot
     dec_at[...] = dec_target
 
@@ -91,14 +95,34 @@
     wide_dec = jnp.concatenate([zeros_dec, dec[...]], axis=0)
     enc_pick = pick(targets[0]) + pick(targets[1])
     rows = nt(enc_pick, wide_enc) + nt(pick(dec_target), wide_dec)
-    sent[...] = rows.astype(BF).reshape(EXPERTS, CAP, 2 * FEATS)
-
-
-def spread_body(got, enc, dec):
-    turned = got[...].reshape(ROWS, 2 * FEATS).astype(F32).T.astype(BF)
+    sent[:, :CAP, :] = rows.astype(BF).reshape(EXPERTS, CAP, 2 * FEATS)
+    wide = (EXPERTS, 2 * FEATS)
+    counts = jnp.broadcast_to(jnp.sum(dec_onehot, axis=1, keepdims=True), wide)
+    on_lanes = jnp.sum(jnp.where(iota(wide, 0) == iota(wide, 1), counts, 0.0), axis=0, keepdims=True)
+    for e in range(EXPERTS):
+        line = iota((LINES - CAP, 2 * FEATS), 0)
+        here = jnp.where(line == 0, on_lanes, jnp.where(line == 1, counts[e : e + 1], 0.0))
+        sent[e, CAP:, :] = here.astype(BF)
+
+
+def spread_body(got, enc, dec, rest, dec_at, most):
+    turned = got[:, :CAP, :].reshape(ROWS, 2 * FEATS).astype(F32).T.astype(BF)
+    tail = got[:, CAP:, :].astype(F32)
+    totals = jnp.sum(tail[:, 0, :], axis=0, keepdims=True)
+    most[0] = jnp.max(totals).astype(jnp.int32)
+    counts = tail[:, 1, 0:1]
+    group = iota((EXPERTS, ROWS), 1) // CAP
+    own = jnp.sum(jnp.where(group == iota((EXPERTS, ROWS), 0), counts, 0.0), axis=0, keepdims=True)
+    ahead = jnp.sum(jnp.where(group > iota((EXPERTS, ROWS), 0), counts, 0.0), axis=0, keepdims=True)
+    slot = iota((1, ROWS), 1) % CAP
+    at = jnp.where(slot < own.astype(jnp.int32), ahead.astype(jnp.int32) + slot, -1)
+    dec_at[...] = at
+    near = nt(turned[FEATS:], pick(at, HELD)).astype(BF)
+    far = nt(turned[FEATS:], pick(at, ROWS - HELD, HELD)).astype(BF)
     for t in range(T):
         enc[t] = turned[:FEATS]
-        dec[t] = turned[FEATS:]
+        dec[t] = near
+        rest[t] = far
 
 
 def turn_body(w_in, w_out, in_turned, out_turned):
@@ -132,14 +156,17 @@
     out[...] = total.astype(BF)
 
 
-def pack_body(enc, dec, sent):
-    def total(ref):
-        acc = ref[0].astype(F32)
-        for t in range(1, T):
-            acc = acc + ref[t].astype(F32)
-        return acc.astype(BF).astype(F32)
-
-    both = jnp.concatenate([total(enc), total(dec)], axis=0)
+def total(ref):
+    acc = ref[0].astype(F32)
+    for t in range(1, T):
+        acc = acc + ref[t].astype(F32)
+    return acc.astype(BF)
+
+
+def pack_body(enc, dec, rest, dec_at, sent):
+    at = dec_at[...]
+    back = nn(total(dec), pick(at, HELD)) + nn(total(rest), pick(at, ROWS - HELD, HELD))
+    both = jnp.concatenate([total(enc).astype(F32), back], axis=0)
     sent[...] = both.T.astype(BF).reshape(EXPERTS, CAP, 2 * FEATS)
 
 
@@ -160,23 +187,31 @@
     return lax.ppermute(value, "dp", [(i, (i + k) % DP) for i in range(DP)])
 
 
-def gather(block, turned, me):
-    over_t = lax.all_to_all(block, "tensor", split_axis=0, concat_axis=0, tiled=True)
-    own = over_t.reshape(T * FEATS, ROWS)
+def over_tensor(block):
+    return lax.all_to_all(block, "tensor", split_axis=0, concat_axis=0, tiled=True)
+
+
+def gather(over_t):
+    own = over_t.reshape(T * FEATS, over_t.shape[2])
     return [own] + [shift(own, k) for k in (1, 2, 3)]
 
 
 def expert(blocks, turned, me):
-    part = shape((T * FEATS, ROWS))
-    work = 4 * ROWS * UNITS * T * DP * FEATS
+    rows = blocks[0].shape[1]
+    part = shape((T * FEATS, rows))
+    work = 4 * rows * UNITS * T * DP * FEATS
     return call(expert_body, [part] * 4, 7, smem=(0,), flops=work, moved=6 << 20)(me, *blocks, *turned)
 
 
 def scatter(parts):
+    rows = parts[0].shape[1]
     sums = [parts[0]] + [shift(parts[k], k) for k in (1, 2, 3)]
-    total = call(add_body, shape((T * FEATS, ROWS)), 4, moved=5 << 19)(*sums)
-    total = total.reshape(T, FEATS, ROWS)
-    return lax.all_to_all(total, "tensor", split_axis=0, concat_axis=0, tiled=True)
+    added = call(add_body, shape((T * FEATS, rows)), 4, moved=5 << 19)(*sums)
+    return over_tensor(added.reshape(T, FEATS, rows))
+
+
+def through(block, turned, me):
+    return scatter(expert(gather(over_tensor(block)), turned, me))
 
 
 def shards(
@@ -194,7 +229,7 @@
     me = lax.axis_index("dp").astype(jnp.int32).reshape(1)
     enc = enc_tokens.T
     dec = dec_tokens.T
-    packed = shape((EXPERTS, CAP, 2 * FEATS))
+    packed = shape((EXPERTS, LINES, 2 * FEATS))
     sent, enc_at, dec_at = call(
         place_body,
         [packed, shape((2, enc.shape[1]), jnp.int32), shape((1, dec.shape[1]), jnp.int32)],
@@ -209,15 +244,33 @@
 
     enc_turned = turn(enc_w_in, enc_w_out)
     dec_turned = turn(dec_w_in, dec_w_out)
-    block = shape((T, FEATS, ROWS))
-    enc_block, dec_block = call(spread_body, [block, block], 1, moved=1 << 20)(got)
-
-    enc_x = gather(enc_block, enc_turned, me)
-    dec_x = gather(dec_block, dec_turned, me)
+    near = shape((T, FEATS, HELD))
+    far = shape((T, FEATS, ROWS - HELD))
+    enc_block, dec_block, rest_block, moved_to, most = call(
+        spread_body,
+        [shape((T, FEATS, ROWS)), near, far, shape((1, ROWS), jnp.int32), shape((1,), jnp.int32)],
+        1,
+        smem_out=(4,),
+        moved=1 << 20,
+    )(got)
+
+    enc_t = over_tensor(enc_block)
+    dec_block, enc_t = lax.optimization_barrier((dec_block, enc_t))
+    dec_t = over_tensor(dec_block)
+    enc_x = gather(enc_t)
+    dec_x = gather(dec_t)
     enc_sums = scatter(expert(enc_x, enc_turned, me))
     dec_sums = scatter(expert(dec_x, dec_turned, me))
-
-    back = call(pack_body, packed, 2, moved=1 << 20)(enc_sums, dec_sums)
+    rest_sums = lax.cond(
+        most[0] > HELD,
+        lambda b, w: through(b, w, me),
+        lambda b, w: jnp.zeros_like(b),
+        rest_block,
+        dec_turned,
+    )
+
+    packed = shape((EXPERTS, CAP, 2 * FEATS))
+    back = call(pack_body, packed, 4, moved=1 << 20)(enc_sums, dec_sums, rest_sums, moved_to)
     got = lax.all_to_all(back, "expert", split_axis=0, concat_axis=0, tiled=True)
     enc_out, dec_out = call(
         mix_body, [shape(enc.shape), shape(dec.shape)], 6, moved=1 << 18

time: 204 us -> 195 us (0.956)
  blocking collectives: 78.2 us -> 93.9 us
  waiting for transfers between devices: 56.5 us -> 41.6 us
  starting transfers between devices: 50.6 us -> 42.6 us
    ppermute x12, waiting for transfers between devices: 56.5 us -> 41.6 us  [shift(): return lax.ppermute(value, 'dp', [(i, (i + k) % DP) for i in range(DP)])]
    all_to_all x2 -> x3, blocking collectives: 44.9 us -> 59.4 us  [over_tensor(): lax.all_to_all(block, 'tensor', split_axis=0, concat_axis=0, tiled=True)]
    ppermute x12, starting transfers between devices: 43.5 us -> 39.2 us  [shift(): return lax.ppermute(value, 'dp', [(i, (i + k) % DP) for i in range(DP)])]
    all_to_all x2 -> x1, starting transfers between devices: 7.13 us -> 3.41 us  [over_tensor(): lax.all_to_all(block, 'tensor', split_axis=0, concat_axis=0, tiled=True)]
    unnamed x30 -> x24, local copies, waits for them, and re-layouts: 4.7 us -> 2.86 us
  transfers between devices with their start and end apart: 14 -> 13, of which waited for: 10 -> 5; matrix products, arithmetic and copies ran while one was open for 0% -> 0% of each run, Pallas kernels for 4% -> 5%
where the time goes in v2:
time: 195 us; the launch traced here: 194 us
  blocking collectives  93.9 us (48%)
  starting transfers between devices  42.6 us (22%)
  waiting for transfers between devices  41.6 us (21%)
  Pallas kernels  11.7 us (6%)
  local copies, waits for them, and re-layouts  2.88 us (1%)
    all_to_all x3, blocking collectives, over_tensor(): lax.all_to_all(block, 'tensor', split_axis=0, concat_axis=0, tiled=True)  59.4 us
    ppermute x12, waiting for transfers between devices, shift(): return lax.ppermute(value, 'dp', [(i, (i + k) % DP) for i in range(DP)])  41.6 us
    ppermute x12, starting transfers between devices, shift(): return lax.ppermute(value, 'dp', [(i, (i + k) % DP) for i in range(DP)])  39.2 us
    all_to_all x1, blocking collectives, shards(): lax.all_to_all(sent, 'expert', split_axis=0, concat_axis=0, tiled=True)  19.8 us
    all_to_all x1, blocking collectives, shards(): lax.all_to_all(back, 'expert', split_axis=0, concat_axis=0, tiled=True)  14.7 us
    pallas_call x2, Pallas kernels, expert(): call(expert_body, [part] * 4, 7, smem=(0,), flops=work, moved=6 << 20)  5.27 us
  transfers between devices with their start and end apart: 13, of which 5 were waited for; matrix products, arithmetic and copies ran while one was open for 0% of the time, Pallas kernels for 5%

profile of v2, /device:TPU:1, one launch (start us, length us, event | category | flops | bytes accessed | tf_op | source)
XLA Modules:
  0.0 194.2 jit_solution(14626621468724951486)
XLA Ops:
  3.3 19.8 %all_to_all.40.got = bf16[16,48,128]{2,1,0:T(8,128)(2,1)S(1)} all-to-all(bf16[16,48,128]{2,1,0:T(8,128)(2,1)S(1)} %get-tuple-element.45), channel_id=1, replica_groups=mesh['expert'=16,'tensor'=8,'dp'=4] {'expert'}, dimensions={0} | all-to-all | bytes 393216 | tf_op jit(solution)/shard_map/all_to_all | solution.py:239
  24.3 26.9 %all_to_all.41 = bf16[8,64,512]{2,1,0:T(8,128)(2,1)S(1)} all-to-all(bf16[8,64,512]{2,1,0:T(8,128)(2,1)S(1)} %get-tuple-element.47), channel_id=1, replica_groups=mesh['expert'=16,'tensor'=8,'dp'=4] {'tensor'}, dimensions={0} | all-to-all | bytes 1048576 | tf_op jit(solution)/shard_map/all_to_all | solution.py:191
  51.2 14.7 %all_to_all.42 = bf16[8,64,256]{2,1,0:T(8,128)(2,1)S(1)} all-to-all(bf16[8,64,256]{2,1,0:T(8,128)(2,1)S(1)} %get-tuple-element.55), channel_id=1, replica_groups=mesh['expert'=16,'tensor'=8,'dp'=4] {'tensor'}, dimensions={0} | all-to-all | bytes 524288 | tf_op jit(solution)/shard_map/all_to_all | solution.py:191
  65.8 3.1 %collective-permute-start.12 = (bf16[512,256]{1,0:T(8,128)(2,1)S(1)}, bf16[512,256]{1,0:T(8,128)(2,1)}, u32[]{:S(2)}, u32[]{:S(2)}) collective-permute-start(bf16[512,256]{1,0:T(8,128)(2,1)S(1)} %bitcast.29), channel_id=1, source_target_pairs={{0,1},{1,2},{2,3},{3,0},{4,5},{5,6},{6,7},{7,4},{8,9},{9,10},{10,1... | collective-permute-start | bytes 786440 | tf_op jit(solution)/shard_map/ppermute | solution.py:187
  69.0 3.1 %collective-permute-start.6 = (bf16[512,512]{1,0:T(8,128)(2,1)S(1)}, bf16[512,512]{1,0:T(8,128)(2,1)S(1)}, u32[]{:S(2)}, u32[]{:S(2)}) collective-permute-start(bf16[512,512]{1,0:T(8,128)(2,1)S(1)} %bitcast.19), channel_id=1, source_target_pairs={{0,1},{1,2},{2,3},{3,0},{4,5},{5,6},{6,7},{7,4},{8,9},{9,10},{10,1... | collective-permute-start | bytes 1572872 | tf_op jit(solution)/shard_map/ppermute | solution.py:187
  74.7 3.5 %collective-permute-start.7 = (bf16[512,512]{1,0:T(8,128)(2,1)S(1)}, bf16[512,512]{1,0:T(8,128)(2,1)S(1)}, u32[]{:S(2)}, u32[]{:S(2)}) collective-permute-start(bf16[512,512]{1,0:T(8,128)(2,1)S(1)} %bitcast.20), channel_id=1, source_target_pairs={{0,2},{1,3},{2,0},{3,1},{4,6},{5,7},{6,4},{7,5},{8,10},{9,11},{10,... | collective-permute-start | bytes 1572872 | tf_op jit(solution)/shard_map/ppermute | solution.py:187
  78.2 3.8 %collective-permute-start.8 = (bf16[512,512]{1,0:T(8,128)(2,1)S(1)}, bf16[512,512]{1,0:T(8,128)(2,1)S(1)}, u32[]{:S(2)}, u32[]{:S(2)}) collective-permute-start(bf16[512,512]{1,0:T(8,128)(2,1)S(1)} %bitcast.21), channel_id=1, source_target_pairs={{0,3},{1,0},{2,1},{3,2},{4,7},{5,4},{6,5},{7,6},{8,11},{9,8},{10,9... | collective-permute-start | bytes 1572872 | tf_op jit(solution)/shard_map/ppermute | solution.py:187
  82.0 2.4 %collective-permute-start.13 = (bf16[512,256]{1,0:T(8,128)(2,1)S(1)}, bf16[512,256]{1,0:T(8,128)(2,1)S(1)}, u32[]{:S(2)}, u32[]{:S(2)}) collective-permute-start(bf16[512,256]{1,0:T(8,128)(2,1)S(1)} %bitcast.30), channel_id=1, source_target_pairs={{0,2},{1,3},{2,0},{3,1},{4,6},{5,7},{6,4},{7,5},{8,10},{9,11},{10,... | collective-permute-start | bytes 786440 | tf_op jit(solution)/shard_map/ppermute | solution.py:187
  84.4 3.4 %collective-permute-start.14 = (bf16[512,256]{1,0:T(8,128)(2,1)S(1)}, bf16[512,256]{1,0:T(8,128)(2,1)S(1)}, u32[]{:S(2)}, u32[]{:S(2)}) collective-permute-start(bf16[512,256]{1,0:T(8,128)(2,1)S(1)} %bitcast.31), channel_id=1, source_target_pairs={{0,3},{1,0},{2,1},{3,2},{4,7},{5,4},{6,5},{7,6},{8,11},{9,8},{10,9... | collective-permute-start | bytes 786440 | tf_op jit(solution)/shard_map/ppermute | solution.py:187
  87.8 17.5 %collective-permute-done.13.x2 = bf16[512,256]{1,0:T(8,128)(2,1)S(1)} collective-permute-done((bf16[512,256]{1,0:T(8,128)(2,1)S(1)}, bf16[512,256]{1,0:T(8,128)(2,1)S(1)}, u32[]{:S(2)}, u32[]{:S(2)}) %collective-permute-start.13) | collective-permute-done | bytes 262176 | tf_op jit(solution)/shard_map/ppermute | solution.py:187
  105.3 7.3 %collective-permute-done.14.x3 = bf16[512,256]{1,0:T(8,128)(2,1)S(1)} collective-permute-done((bf16[512,256]{1,0:T(8,128)(2,1)S(1)}, bf16[512,256]{1,0:T(8,128)(2,1)S(1)}, u32[]{:S(2)}, u32[]{:S(2)}) %collective-permute-start.14) | collective-permute-done | bytes 262176 | tf_op jit(solution)/shard_map/ppermute | solution.py:187
  112.6 3.0 %shard_map.119 = (bf16[512,256]{1,0:T(8,128)(2,1)S(1)}, bf16[512,256]{1,0:T(8,128)(2,1)S(1)}, bf16[512,256]{1,0:T(8,128)(2,1)S(1)}, bf16[512,256]{1,0:T(8,128)(2,1)S(1)}) custom-call(s32[1]{0:T(128)} %bitcast.2.me, bf16[512,256]{1,0:T(8,128)(2,1)S(1)} %bitcast.32, bf16[512,256]{1,0:T(8,128)(2,1)} %collective-permute-done.12.x1, ...), custom_call_target="tpu_custom_call" | custom-call | flops 536870912 | bytes 6291456 | tf_op jit(solution)/shard_map/pallas_call | solution.py:203
  115.6 4.8 %collective-permute-start.15 = (bf16[512,256]{1,0:T(8,128)(2,1)S(1)}, bf16[512,256]{1,0:T(8,128)(2,1)S(1)}, u32[]{:S(2)}, u32[]{:S(2)}) collective-permute-start(bf16[512,256]{1,0:T(8,128)(2,1)S(1)} %get-tuple-element.59), channel_id=1, source_target_pairs={{0,1},{1,2},{2,3},{3,0},{4,5},{5,6},{6,7},{7,4},{8,9},{9,10},{10,1... | collective-permute-start | bytes 786440 | tf_op jit(solution)/shard_map/ppermute | solution.py:187
  120.3 3.6 %collective-permute-start.16 = (bf16[512,256]{1,0:T(8,128)(2,1)S(1)}, bf16[512,256]{1,0:T(8,128)(2,1)S(1)}, u32[]{:S(2)}, u32[]{:S(2)}) collective-permute-start(bf16[512,256]{1,0:T(8,128)(2,1)S(1)} %get-tuple-element.60), channel_id=1, source_target_pairs={{0,2},{1,3},{2,0},{3,1},{4,6},{5,7},{6,4},{7,5},{8,10},{9,11},{10,... | collective-permute-start | bytes 786440 | tf_op jit(solution)/shard_map/ppermute | solution.py:187
  124.0 2.6 %collective-permute-start.17 = (bf16[512,256]{1,0:T(8,128)(2,1)S(1)}, bf16[512,256]{1,0:T(8,128)(2,1)S(1)}, u32[]{:S(2)}, u32[]{:S(2)}) collective-permute-start(bf16[512,256]{1,0:T(8,128)(2,1)S(1)} %get-tuple-element.61), channel_id=1, source_target_pairs={{0,3},{1,0},{2,1},{3,2},{4,7},{5,4},{6,5},{7,6},{8,11},{9,8},{10,9... | collective-permute-start | bytes 786440 | tf_op jit(solution)/shard_map/ppermute | solution.py:187
  127.2 2.3 %shard_map.116 = (bf16[512,512]{1,0:T(8,128)(2,1)S(1)}, bf16[512,512]{1,0:T(8,128)(2,1)}, bf16[512,512]{1,0:T(8,128)(2,1)}, bf16[512,512]{1,0:T(8,128)(2,1)}) custom-call(s32[1]{0:T(128)} %bitcast.2.me, bf16[512,512]{1,0:T(8,128)(2,1)S(1)} %bitcast.22, bf16[512,512]{1,0:T(8,128)(2,1)S(1)} %collective-permute-done.6.x1, ...), custom_call_target="tpu_custom_call" | custom-call | flops 1073741824 | bytes 6291456 | tf_op jit(solution)/shard_map/pallas_call | solution.py:203
  129.5 2.7 %collective-permute-start.9 = (bf16[512,512]{1,0:T(8,128)(2,1)}, bf16[512,512]{1,0:T(8,128)(2,1)S(1)}, u32[]{:S(2)}, u32[]{:S(2)}) collective-permute-start(bf16[512,512]{1,0:T(8,128)(2,1)} %get-tuple-element.52), channel_id=1, source_target_pairs={{0,1},{1,2},{2,3},{3,0},{4,5},{5,6},{6,7},{7,4},{8,9},{9,10},{10,1... | collective-permute-start | bytes 1572872 | tf_op jit(solution)/shard_map/ppermute | solution.py:187
  132.2 3.1 %collective-permute-start.10 = (bf16[512,512]{1,0:T(8,128)(2,1)}, bf16[512,512]{1,0:T(8,128)(2,1)S(1)}, u32[]{:S(2)}, u32[]{:S(2)}) collective-permute-start(bf16[512,512]{1,0:T(8,128)(2,1)} %get-tuple-element.53), channel_id=1, source_target_pairs={{0,2},{1,3},{2,0},{3,1},{4,6},{5,7},{6,4},{7,5},{8,10},{9,11},{10,... | collective-permute-start | bytes 1572872 | tf_op jit(solution)/shard_map/ppermute | solution.py:187
  135.4 3.1 %collective-permute-start.11 = (bf16[512,512]{1,0:T(8,128)(2,1)}, bf16[512,512]{1,0:T(8,128)(2,1)S(1)}, u32[]{:S(2)}, u32[]{:S(2)}) collective-permute-start(bf16[512,512]{1,0:T(8,128)(2,1)} %get-tuple-element.54), channel_id=1, source_target_pairs={{0,3},{1,0},{2,1},{3,2},{4,7},{5,4},{6,5},{7,6},{8,11},{9,8},{10,9... | collective-permute-start | bytes 1572872 | tf_op jit(solution)/shard_map/ppermute | solution.py:187
  139.3 3.4 %all-to-all-start.6 = ((bf16[8,64,256]{2,1,0:T(8,128)(2,1)}), bf16[8,64,256]{2,1,0:T(8,128)(2,1)S(1)}, u32[]{:S(2)}, u32[]{:S(2)}) async-start(bf16[8,64,256]{2,1,0:T(8,128)(2,1)} %bitcast.14), calls=%async_computation.6 | async-start | bytes 524288 | tf_op jit(solution)/shard_map/all_to_all | solution.py:191
  144.8 10.7 %collective-permute-done.10.c = bf16[512,512]{1,0:T(8,128)(2,1)S(1)} collective-permute-done((bf16[512,512]{1,0:T(8,128)(2,1)}, bf16[512,512]{1,0:T(8,128)(2,1)S(1)}, u32[]{:S(2)}, u32[]{:S(2)}) %collective-permute-start.10) | collective-permute-done | bytes 524320 | tf_op jit(solution)/shard_map/ppermute | solution.py:187
  155.6 3.9 %collective-permute-done.11.d = bf16[512,512]{1,0:T(8,128)(2,1)S(1)} collective-permute-done((bf16[512,512]{1,0:T(8,128)(2,1)}, bf16[512,512]{1,0:T(8,128)(2,1)S(1)}, u32[]{:S(2)}, u32[]{:S(2)}) %collective-permute-start.11) | collective-permute-done | bytes 524320 | tf_op jit(solution)/shard_map/ppermute | solution.py:187
  159.8 17.8 %all_to_all.43.enc = bf16[8,64,512]{2,1,0:T(8,128)(2,1)S(1)} all-to-all(bf16[8,64,512]{2,1,0:T(8,128)(2,1)S(1)} %bitcast.23), channel_id=1, replica_groups=mesh['expert'=16,'tensor'=8,'dp'=4] {'tensor'}, dimensions={0} | all-to-all | bytes 1048576 | tf_op jit(solution)/shard_map/all_to_all | solution.py:191
  177.9 14.7 %all_to_all.44.got = bf16[16,32,128]{2,1,0:T(8,128)(2,1)S(1)} all-to-all(bf16[16,32,128]{2,1,0:T(8,128)(2,1)S(1)} %shard_map.121), channel_id=1, replica_groups=mesh['expert'=16,'tensor'=8,'dp'=4] {'expert'}, dimensions={0} | all-to-all | bytes 262144 | tf_op jit(solution)/shard_map/all_to_all | solution.py:274
  (43 shorter events, 11.4 us)
Async XLA Ops:
  0.6 0.7 copy-start.9
  0.7 0.7 copy-start.10
  1.3 0.8 copy-start.4
  2.1 0.7 copy-start.6
  3.3 68.8 %copy-start = (bf16[1,2048,256]{2,1,0:T(8,128)(2,1)S(1)}, bf16[1,2048,256]{2,1,0:T(8,128)(2,1)}, u32[]{:S(2)}) copy-start(bf16[1,2048,256]{2,1,0:T(8,128)(2,1)} %param.20) | copy-start | bytes 3145732
  3.3 68.8 %copy-start.1 = (bf16[1,256,2048]{2,1,0:T(8,128)(2,1)S(1)}, bf16[1,256,2048]{2,1,0:T(8,128)(2,1)}, u32[]{:S(2)}) copy-start(bf16[1,256,2048]{2,1,0:T(8,128)(2,1)} %param.21) | copy-start | bytes 3145732
  65.8 18.6 %collective-permute-start.12 = (bf16[512,256]{1,0:T(8,128)(2,1)S(1)}, bf16[512,256]{1,0:T(8,128)(2,1)}, u32[]{:S(2)}, u32[]{:S(2)}) collective-permute-start(bf16[512,256]{1,0:T(8,128)(2,1)S(1)} %bitcast.29), channel_id=1, source_target_pairs={{0,1},{1,2},{2,3},{3,0},{4,5},{5,6},{6,7},{7,4},{8,9},{9,10},{10,1... | collective-permute-start | bytes 786440 | tf_op jit(solution)/shard_map/ppermute | solution.py:187
  69.0 55.0 %collective-permute-start.6 = (bf16[512,512]{1,0:T(8,128)(2,1)S(1)}, bf16[512,512]{1,0:T(8,128)(2,1)S(1)}, u32[]{:S(2)}, u32[]{:S(2)}) collective-permute-start(bf16[512,512]{1,0:T(8,128)(2,1)S(1)} %bitcast.19), channel_id=1, source_target_pairs={{0,1},{1,2},{2,3},{3,0},{4,5},{5,6},{6,7},{7,4},{8,9},{9,10},{10,1... | collective-permute-start | bytes 1572872 | tf_op jit(solution)/shard_map/ppermute | solution.py:187
  74.7 51.9 %copy-start.2 = (bf16[1,2048,256]{2,1,0:T(8,128)(2,1)S(1)}, bf16[1,2048,256]{2,1,0:T(8,128)(2,1)}, u32[]{:S(2)}) copy-start(bf16[1,2048,256]{2,1,0:T(8,128)(2,1)} %param.15) | copy-start | bytes 3145732
  74.7 51.9 %copy-start.3 = (bf16[1,256,2048]{2,1,0:T(8,128)(2,1)S(1)}, bf16[1,256,2048]{2,1,0:T(8,128)(2,1)}, u32[]{:S(2)}) copy-start(bf16[1,256,2048]{2,1,0:T(8,128)(2,1)} %param.16) | copy-start | bytes 3145732
  74.7 52.5 %collective-permute-start.7 = (bf16[512,512]{1,0:T(8,128)(2,1)S(1)}, bf16[512,512]{1,0:T(8,128)(2,1)S(1)}, u32[]{:S(2)}, u32[]{:S(2)}) collective-permute-start(bf16[512,512]{1,0:T(8,128)(2,1)S(1)} %bitcast.20), channel_id=1, source_target_pairs={{0,2},{1,3},{2,0},{3,1},{4,6},{5,7},{6,4},{7,5},{8,10},{9,11},{10,... | collective-permute-start | bytes 1572872 | tf_op jit(solution)/shard_map/ppermute | solution.py:187
  78.2 49.0 %collective-permute-start.8 = (bf16[512,512]{1,0:T(8,128)(2,1)S(1)}, bf16[512,512]{1,0:T(8,128)(2,1)S(1)}, u32[]{:S(2)}, u32[]{:S(2)}) collective-permute-start(bf16[512,512]{1,0:T(8,128)(2,1)S(1)} %bitcast.21), channel_id=1, source_target_pairs={{0,3},{1,0},{2,1},{3,2},{4,7},{5,4},{6,5},{7,6},{8,11},{9,8},{10,9... | collective-permute-start | bytes 1572872 | tf_op jit(solution)/shard_map/ppermute | solution.py:187
  82.0 23.4 %collective-permute-start.13 = (bf16[512,256]{1,0:T(8,128)(2,1)S(1)}, bf16[512,256]{1,0:T(8,128)(2,1)S(1)}, u32[]{:S(2)}, u32[]{:S(2)}) collective-permute-start(bf16[512,256]{1,0:T(8,128)(2,1)S(1)} %bitcast.30), channel_id=1, source_target_pairs={{0,2},{1,3},{2,0},{3,1},{4,6},{5,7},{6,4},{7,5},{8,10},{9,11},{10,... | collective-permute-start | bytes 786440 | tf_op jit(solution)/shard_map/ppermute | solution.py:187
  84.4 28.2 %collective-permute-start.14 = (bf16[512,256]{1,0:T(8,128)(2,1)S(1)}, bf16[512,256]{1,0:T(8,128)(2,1)S(1)}, u32[]{:S(2)}, u32[]{:S(2)}) collective-permute-start(bf16[512,256]{1,0:T(8,128)(2,1)S(1)} %bitcast.31), channel_id=1, source_target_pairs={{0,3},{1,0},{2,1},{3,2},{4,7},{5,4},{6,5},{7,6},{8,11},{9,8},{10,9... | collective-permute-start | bytes 786440 | tf_op jit(solution)/shard_map/ppermute | solution.py:187
  115.6 19.8 %collective-permute-start.15 = (bf16[512,256]{1,0:T(8,128)(2,1)S(1)}, bf16[512,256]{1,0:T(8,128)(2,1)S(1)}, u32[]{:S(2)}, u32[]{:S(2)}) collective-permute-start(bf16[512,256]{1,0:T(8,128)(2,1)S(1)} %get-tuple-element.59), channel_id=1, source_target_pairs={{0,1},{1,2},{2,3},{3,0},{4,5},{5,6},{6,7},{7,4},{8,9},{9,10},{10,1... | collective-permute-start | bytes 786440 | tf_op jit(solution)/shard_map/ppermute | solution.py:187
  120.3 18.1 %collective-permute-start.16 = (bf16[512,256]{1,0:T(8,128)(2,1)S(1)}, bf16[512,256]{1,0:T(8,128)(2,1)S(1)}, u32[]{:S(2)}, u32[]{:S(2)}) collective-permute-start(bf16[512,256]{1,0:T(8,128)(2,1)S(1)} %get-tuple-element.60), channel_id=1, source_target_pairs={{0,2},{1,3},{2,0},{3,1},{4,6},{5,7},{6,4},{7,5},{8,10},{9,11},{10,... | collective-permute-start | bytes 786440 | tf_op jit(solution)/shard_map/ppermute | solution.py:187
  124.0 14.5 %collective-permute-start.17 = (bf16[512,256]{1,0:T(8,128)(2,1)S(1)}, bf16[512,256]{1,0:T(8,128)(2,1)S(1)}, u32[]{:S(2)}, u32[]{:S(2)}) collective-permute-start(bf16[512,256]{1,0:T(8,128)(2,1)S(1)} %get-tuple-element.61), channel_id=1, source_target_pairs={{0,3},{1,0},{2,1},{3,2},{4,7},{5,4},{6,5},{7,6},{8,11},{9,8},{10,9... | collective-permute-start | bytes 786440 | tf_op jit(solution)/shard_map/ppermute | solution.py:187
  129.5 15.3 %collective-permute-start.9 = (bf16[512,512]{1,0:T(8,128)(2,1)}, bf16[512,512]{1,0:T(8,128)(2,1)S(1)}, u32[]{:S(2)}, u32[]{:S(2)}) collective-permute-start(bf16[512,512]{1,0:T(8,128)(2,1)} %get-tuple-element.52), channel_id=1, source_target_pairs={{0,1},{1,2},{2,3},{3,0},{4,5},{5,6},{6,7},{7,4},{8,9},{9,10},{10,1... | collective-permute-start | bytes 1572872 | tf_op jit(solution)/shard_map/ppermute | solution.py:187
  132.2 23.3 %collective-permute-start.10 = (bf16[512,512]{1,0:T(8,128)(2,1)}, bf16[512,512]{1,0:T(8,128)(2,1)S(1)}, u32[]{:S(2)}, u32[]{:S(2)}) collective-permute-start(bf16[512,512]{1,0:T(8,128)(2,1)} %get-tuple-element.53), channel_id=1, source_target_pairs={{0,2},{1,3},{2,0},{3,1},{4,6},{5,7},{6,4},{7,5},{8,10},{9,11},{10,... | collective-permute-start | bytes 1572872 | tf_op jit(solution)/shard_map/ppermute | solution.py:187
  135.4 24.1 %collective-permute-start.11 = (bf16[512,512]{1,0:T(8,128)(2,1)}, bf16[512,512]{1,0:T(8,128)(2,1)S(1)}, u32[]{:S(2)}, u32[]{:S(2)}) collective-permute-start(bf16[512,512]{1,0:T(8,128)(2,1)} %get-tuple-element.54), channel_id=1, source_target_pairs={{0,3},{1,0},{2,1},{3,2},{4,7},{5,4},{6,5},{7,6},{8,11},{9,8},{10,9... | collective-permute-start | bytes 1572872 | tf_op jit(solution)/shard_map/ppermute | solution.py:187
  139.3 20.4 %all-to-all-start.6 = ((bf16[8,64,256]{2,1,0:T(8,128)(2,1)}), bf16[8,64,256]{2,1,0:T(8,128)(2,1)S(1)}, u32[]{:S(2)}, u32[]{:S(2)}) async-start(bf16[8,64,256]{2,1,0:T(8,128)(2,1)} %bitcast.14), calls=%async_computation.6 | async-start | bytes 524288 | tf_op jit(solution)/shard_map/all_to_all | solution.py:191
  177.5 15.1 %copy-start.7 = (bf16[128,64]{0,1:T(8,128)(2,1)S(1)}, bf16[128,64]{0,1:T(8,128)(2,1)}, u32[]{:S(2)}) copy-start(bf16[128,64]{0,1:T(8,128)(2,1)} %param.12) | copy-start | bytes 49156
  177.9 14.7 %copy-start.5 = (bf16[144,64]{0,1:T(8,128)(2,1)S(1)}, bf16[144,64]{0,1:T(8,128)(2,1)}, u32[]{:S(2)}) copy-start(bf16[144,64]{0,1:T(8,128)(2,1)} %param.17) | copy-start | bytes 55300
  192.6 0.7 copy-start.8
  (1 other events, 0.7 us)

commit v3 on v2

--- a/solution.py
+++ b/solution.py
@@ -105,7 +105,7 @@
         sent[e, CAP:, :] = here.astype(BF)
 
 
-def spread_body(got, enc, dec, rest, dec_at, most):
+def spread_body(got, enc_a, enc_b, dec, rest, dec_at, most):
     turned = got[:, :CAP, :].reshape(ROWS, 2 * FEATS).astype(F32).T.astype(BF)
     tail = got[:, CAP:, :].astype(F32)
     totals = jnp.sum(tail[:, 0, :], axis=0, keepdims=True)
@@ -120,7 +120,8 @@
     near = nt(turned[FEATS:], pick(at, HELD)).astype(BF)
     far = nt(turned[FEATS:], pick(at, ROWS - HELD, HELD)).astype(BF)
     for t in range(T):
-        enc[t] = turned[:FEATS]
+        enc_a[t] = turned[:FEATS, :HELD]
+        enc_b[t] = turned[:FEATS, HELD:]
         dec[t] = near
         rest[t] = far
 
@@ -163,10 +164,11 @@
     return acc.astype(BF)
 
 
-def pack_body(enc, dec, rest, dec_at, sent):
+def pack_body(enc_a, enc_b, dec, rest, dec_at, sent):
     at = dec_at[...]
     back = nn(total(dec), pick(at, HELD)) + nn(total(rest), pick(at, ROWS - HELD, HELD))
-    both = jnp.concatenate([total(enc).astype(F32), back], axis=0)
+    enc = jnp.concatenate([total(enc_a), total(enc_b)], axis=1).astype(F32)
+    both = jnp.concatenate([enc, back], axis=0)
     sent[...] = both.T.astype(BF).reshape(EXPERTS, CAP, 2 * FEATS)
 
 
@@ -246,21 +248,16 @@
     dec_turned = turn(dec_w_in, dec_w_out)
     near = shape((T, FEATS, HELD))
     far = shape((T, FEATS, ROWS - HELD))
-    enc_block, dec_block, rest_block, moved_to, most = call(
+    *blocks, rest_block, moved_to, most = call(
         spread_body,
-        [shape((T, FEATS, ROWS)), near, far, shape((1, ROWS), jnp.int32), shape((1,), jnp.int32)],
+        [near, far, near, far, shape((1, ROWS), jnp.int32), shape((1,), jnp.int32)],
         1,
-        smem_out=(4,),
+        smem_out=(5,),
         moved=1 << 20,
     )(got)
 
-    enc_t = over_tensor(enc_block)
-    dec_block, enc_t = lax.optimization_barrier((dec_block, enc_t))
-    dec_t = over_tensor(dec_block)
-    enc_x = gather(enc_t)
-    dec_x = gather(dec_t)
-    enc_sums = scatter(expert(enc_x, enc_turned, me))
-    dec_sums = scatter(expert(dec_x, dec_turned, me))
+    weights = [enc_turned, enc_turned, dec_turned]
+    sums = [through(block, turned, me) for block, turned in zip(blocks, weights)]
     rest_sums = lax.cond(
         most[0] > HELD,
         lambda b, w: through(b, w, me),
@@ -270,7 +267,7 @@
     )
 
     packed = shape((EXPERTS, CAP, 2 * FEATS))
-    back = call(pack_body, packed, 4, moved=1 << 20)(enc_sums, dec_sums, rest_sums, moved_to)
+    back = call(pack_body, packed, 5, moved=1 << 20)(*sums, rest_sums, moved_to)
     got = lax.all_to_all(back, "expert", split_axis=0, concat_axis=0, tiled=True)
     enc_out, dec_out = call(
         mix_body, [shape(enc.shape), shape(dec.shape)], 6, moved=1 << 18

time: 195 us -> 201 us (1.031)
  the two profiles are of different devices: /device:TPU:1 before, /device:TPU:3 now
where the time goes in v3:
time: 201 us; the launch traced here: 199 us
  starting transfers between devices  83.7 us (42%)
  blocking collectives  53.5 us (27%)
  waiting for transfers between devices  36.9 us (18%)
  Pallas kernels  15.9 us (8%)
  local copies, waits for them, and re-layouts  7.26 us (4%)
    ppermute x18, starting transfers between devices, shift(): return lax.ppermute(value, 'dp', [(i, (i + k) % DP) for i in range(DP)])  52.4 us
    all_to_all x2, blocking collectives, over_tensor(): lax.all_to_all(block, 'tensor', split_axis=0, concat_axis=0, tiled=True)  39.8 us
    ppermute x18, waiting for transfers between devices, shift(): return lax.ppermute(value, 'dp', [(i, (i + k) % DP) for i in range(DP)])  30.9 us
    all_to_all x4, starting transfers between devices, over_tensor(): lax.all_to_all(block, 'tensor', split_axis=0, concat_axis=0, tiled=True)  23.5 us
    all_to_all x1, blocking collectives, shards(): lax.all_to_all(back, 'expert', split_axis=0, concat_axis=0, tiled=True)  13.7 us
    pallas_call x3, Pallas kernels, expert(): call(expert_body, [part] * 4, 7, smem=(0,), flops=work, moved=6 << 20)  8.07 us
    all_to_all x1, starting transfers between devices, shards(): lax.all_to_all(sent, 'expert', split_axis=0, concat_axis=0, tiled=True)  7.78 us
    unnamed x32, local copies, waits for them, and re-layouts  7.23 us
  transfers between devices with their start and end apart: 23, of which 10 were waited for; matrix products, arithmetic and copies ran while one was open for 0% of the time, Pallas kernels for 6%

profile of v3, /device:TPU:3, one launch (start us, length us, event | category | flops | bytes accessed | tf_op | source)
XLA Modules:
  0.0 199.0 jit_solution(4117865626918307658)
XLA Ops:
  4.0 7.8 %all-to-all-start.2 = ((bf16[16,48,128]{2,1,0:T(8,128)(2,1)}), bf16[16,48,128]{2,1,0:T(8,128)(2,1)S(1)}, u32[]{:S(2)}, u32[]{:S(2)}) async-start(bf16[16,48,128]{2,1,0:T(8,128)(2,1)} %get-tuple-element.48), calls=%async_computation.2 | async-start | bytes 393216 | tf_op jit(solution)/shard_map/all_to_all | solution.py:241
  16.1 6.0 %all-to-all-done.2.got = bf16[16,48,128]{2,1,0:T(8,128)(2,1)S(1)} async-done(((bf16[16,48,128]{2,1,0:T(8,128)(2,1)}), bf16[16,48,128]{2,1,0:T(8,128)(2,1)S(1)}, u32[]{:S(2)}, u32[]{:S(2)}) %all-to-all-start.2) | async-done | bytes 196640 | tf_op jit(solution)/shard_map/all_to_all | solution.py:241
  23.9 22.5 %all_to_all.50 = bf16[8,64,256]{2,1,0:T(8,128)(2,1)} all-to-all(bf16[8,64,256]{2,1,0:T(8,128)(2,1)S(1)} %get-tuple-element.49), channel_id=1, replica_groups=mesh['expert'=16,'tensor'=8,'dp'=4] {'tensor'}, dimensions={0} | all-to-all | bytes 524288 | tf_op jit(solution)/shard_map/all_to_all | solution.py:193
  46.4 3.4 %all-to-all-start.5 = ((bf16[8,64,256]{2,1,0:T(8,128)(2,1)}), bf16[8,64,256]{2,1,0:T(8,128)(2,1)S(1)}, u32[]{:S(2)}, u32[]{:S(2)}) async-start(bf16[8,64,256]{2,1,0:T(8,128)(2,1)} %get-tuple-element.56), calls=%async_computation.5 | async-start | bytes 524288 | tf_op jit(solution)/shard_map/all_to_all | solution.py:193
  49.8 3.1 %collective-permute-start.6 = (bf16[512,256]{1,0:T(8,128)(2,1)}, bf16[512,256]{1,0:T(8,128)(2,1)S(1)}, u32[]{:S(2)}, u32[]{:S(2)}) collective-permute-start(bf16[512,256]{1,0:T(8,128)(2,1)} %bitcast.7.x0), channel_id=1, source_target_pairs={{0,1},{1,2},{2,3},{3,0},{4,5},{5,6},{6,7},{7,4},{8,9},{9,10},{10,1... | collective-permute-start | bytes 786440 | tf_op jit(solution)/shard_map/ppermute | solution.py:189
  53.0 2.7 %collective-permute-start.7 = (bf16[512,256]{1,0:T(8,128)(2,1)}, bf16[512,256]{1,0:T(8,128)(2,1)S(1)}, u32[]{:S(2)}, u32[]{:S(2)}) collective-permute-start(bf16[512,256]{1,0:T(8,128)(2,1)} %bitcast.7.x0), channel_id=1, source_target_pairs={{0,2},{1,3},{2,0},{3,1},{4,6},{5,7},{6,4},{7,5},{8,10},{9,11},{10,... | collective-permute-start | bytes 786440 | tf_op jit(solution)/shard_map/ppermute | solution.py:189
  55.7 3.8 %collective-permute-start.8 = (bf16[512,256]{1,0:T(8,128)(2,1)}, bf16[512,256]{1,0:T(8,128)(2,1)S(1)}, u32[]{:S(2)}, u32[]{:S(2)}) collective-permute-start(bf16[512,256]{1,0:T(8,128)(2,1)} %bitcast.7.x0), channel_id=1, source_target_pairs={{0,3},{1,0},{2,1},{3,2},{4,7},{5,4},{6,5},{7,6},{8,11},{9,8},{10,9... | collective-permute-start | bytes 786440 | tf_op jit(solution)/shard_map/ppermute | solution.py:189
  63.7 6.7 %collective-permute-done.8.x3 = bf16[512,256]{1,0:T(8,128)(2,1)S(1)} collective-permute-done((bf16[512,256]{1,0:T(8,128)(2,1)}, bf16[512,256]{1,0:T(8,128)(2,1)S(1)}, u32[]{:S(2)}, u32[]{:S(2)}) %collective-permute-start.8) | collective-permute-done | bytes 262176 | tf_op jit(solution)/shard_map/ppermute | solution.py:189
  70.4 2.7 %shard_map.116 = (bf16[512,256]{1,0:T(8,128)(2,1)S(1)}, bf16[512,256]{1,0:T(8,128)(2,1)}, bf16[512,256]{1,0:T(8,128)(2,1)S(1)}, bf16[512,256]{1,0:T(8,128)(2,1)S(1)}) custom-call(s32[1]{0:T(128)} %bitcast.2.me, bf16[512,256]{1,0:T(8,128)(2,1)} %bitcast.7.x0, bf16[512,256]{1,0:T(8,128)(2,1)S(1)} %collective-permute-done.6.x1, ...), custom_call_target="tpu_custom_call" | custom-call | flops 536870912 | bytes 6291456 | tf_op jit(solution)/shard_map/pallas_call | solution.py:205
  75.8 6.6 %all-to-all-start.7 = ((bf16[8,64,256]{2,1,0:T(8,128)(2,1)}), bf16[8,64,256]{2,1,0:T(8,128)(2,1)S(1)}, u32[]{:S(2)}, u32[]{:S(2)}) async-start(bf16[8,64,256]{2,1,0:T(8,128)(2,1)} %get-tuple-element.61), calls=%async_computation.7 | async-start | bytes 524288 | tf_op jit(solution)/shard_map/all_to_all | solution.py:193
  84.4 4.0 %collective-permute-start.11 = (bf16[512,256]{1,0:T(8,128)(2,1)}, bf16[512,256]{1,0:T(8,128)(2,1)S(1)}, u32[]{:S(2)}, u32[]{:S(2)}) collective-permute-start(bf16[512,256]{1,0:T(8,128)(2,1)} %copy-done.12), channel_id=1, source_target_pairs={{0,3},{1,0},{2,1},{3,2},{4,7},{5,4},{6,5},{7,6},{8,11},{9,8},{10,9... | collective-permute-start | bytes 786440 | tf_op jit(solution)/shard_map/ppermute | solution.py:189
  90.7 4.9 %collective-permute-start.13 = (bf16[512,256]{1,0:T(8,128)(2,1)S(1)}, bf16[512,256]{1,0:T(8,128)(2,1)}, u32[]{:S(2)}, u32[]{:S(2)}) collective-permute-start(bf16[512,256]{1,0:T(8,128)(2,1)S(1)} %bitcast.32), channel_id=1, source_target_pairs={{0,2},{1,3},{2,0},{3,1},{4,6},{5,7},{6,4},{7,5},{8,10},{9,11},{10,... | collective-permute-start | bytes 786440 | tf_op jit(solution)/shard_map/ppermute | solution.py:189
  97.8 3.7 %collective-permute-done.11.d = bf16[512,256]{1,0:T(8,128)(2,1)S(1)} collective-permute-done((bf16[512,256]{1,0:T(8,128)(2,1)}, bf16[512,256]{1,0:T(8,128)(2,1)S(1)}, u32[]{:S(2)}, u32[]{:S(2)}) %collective-permute-start.11) | collective-permute-done | bytes 262176 | tf_op jit(solution)/shard_map/ppermute | solution.py:189
  102.4 6.9 %all-to-all-start.4 = ((bf16[8,64,256]{2,1,0:T(8,128)(2,1)}), bf16[8,64,256]{2,1,0:T(8,128)(2,1)S(1)}, u32[]{:S(2)}, u32[]{:S(2)}) async-start(bf16[8,64,256]{2,1,0:T(8,128)(2,1)} %bitcast.10), calls=%async_computation.4 | async-start | bytes 524288 | tf_op jit(solution)/shard_map/all_to_all | solution.py:193
  117.6 4.0 %collective-permute-start.17 = (bf16[512,256]{1,0:T(8,128)(2,1)S(1)}, bf16[512,256]{1,0:T(8,128)(2,1)S(1)}, u32[]{:S(2)}, u32[]{:S(2)}) collective-permute-start(bf16[512,256]{1,0:T(8,128)(2,1)S(1)} %get-tuple-element.60), channel_id=1, source_target_pairs={{0,3},{1,0},{2,1},{3,2},{4,7},{5,4},{6,5},{7,6},{8,11},{9,8},{10,9... | collective-permute-start | bytes 786440 | tf_op jit(solution)/shard_map/ppermute | solution.py:189
  123.8 4.9 %collective-permute-start.19 = (bf16[512,256]{1,0:T(8,128)(2,1)S(1)}, bf16[512,256]{1,0:T(8,128)(2,1)S(1)}, u32[]{:S(2)}, u32[]{:S(2)}) collective-permute-start(bf16[512,256]{1,0:T(8,128)(2,1)S(1)} %bitcast.28), channel_id=1, source_target_pairs={{0,2},{1,3},{2,0},{3,1},{4,6},{5,7},{6,4},{7,5},{8,10},{9,11},{10,... | collective-permute-start | bytes 786440 | tf_op jit(solution)/shard_map/ppermute | solution.py:189
  130.9 3.4 %collective-permute-done.17.d = bf16[512,256]{1,0:T(8,128)(2,1)S(1)} collective-permute-done((bf16[512,256]{1,0:T(8,128)(2,1)S(1)}, bf16[512,256]{1,0:T(8,128)(2,1)S(1)}, u32[]{:S(2)}, u32[]{:S(2)}) %collective-permute-start.17) | collective-permute-done | bytes 262176 | tf_op jit(solution)/shard_map/ppermute | solution.py:189
  135.1 6.6 %all-to-all-start.6 = ((bf16[8,64,256]{2,1,0:T(8,128)(2,1)}), bf16[8,64,256]{2,1,0:T(8,128)(2,1)S(1)}, u32[]{:S(2)}, u32[]{:S(2)}) async-start(bf16[8,64,256]{2,1,0:T(8,128)(2,1)} %bitcast.12), calls=%async_computation.6 | async-start | bytes 524288 | tf_op jit(solution)/shard_map/all_to_all | solution.py:193
  143.8 2.9 %shard_map.121 = (bf16[512,256]{1,0:T(8,128)(2,1)S(1)}, bf16[512,256]{1,0:T(8,128)(2,1)S(1)}, bf16[512,256]{1,0:T(8,128)(2,1)S(1)}, bf16[512,256]{1,0:T(8,128)(2,1)S(1)}) custom-call(s32[1]{0:T(128)} %bitcast.2.me, bf16[512,256]{1,0:T(8,128)(2,1)S(1)} %bitcast.30, bf16[512,256]{1,0:T(8,128)(2,1)S(1)} %collective-permute-done.18.x1, ...), custom_call_target="tpu_custom_call" | custom-call | flops 536870912 | bytes 6291456 | tf_op jit(solution)/shard_map/pallas_call | solution.py:205
  150.8 4.0 %collective-permute-start.23 = (bf16[512,256]{1,0:T(8,128)(2,1)S(1)}, bf16[512,256]{1,0:T(8,128)(2,1)S(1)}, u32[]{:S(2)}, u32[]{:S(2)}) collective-permute-start(bf16[512,256]{1,0:T(8,128)(2,1)S(1)} %get-tuple-element.67), channel_id=1, source_target_pairs={{0,3},{1,0},{2,1},{3,2},{4,7},{5,4},{6,5},{7,6},{8,11},{9,8},{10,9... | collective-permute-start | bytes 786440 | tf_op jit(solution)/shard_map/ppermute | solution.py:189
  155.8 2.8 %collective-permute-done.22.c = bf16[512,256]{1,0:T(8,128)(2,1)S(1)} collective-permute-done((bf16[512,256]{1,0:T(8,128)(2,1)S(1)}, bf16[512,256]{1,0:T(8,128)(2,1)S(1)}, u32[]{:S(2)}, u32[]{:S(2)}) %collective-permute-start.22) | collective-permute-done | bytes 262176 | tf_op jit(solution)/shard_map/ppermute | solution.py:189
  158.6 7.2 %collective-permute-done.23.d = bf16[512,256]{1,0:T(8,128)(2,1)S(1)} collective-permute-done((bf16[512,256]{1,0:T(8,128)(2,1)S(1)}, bf16[512,256]{1,0:T(8,128)(2,1)S(1)}, u32[]{:S(2)}, u32[]{:S(2)}) %collective-permute-start.23) | collective-permute-done | bytes 262176 | tf_op jit(solution)/shard_map/ppermute | solution.py:189
  166.0 17.3 %all_to_all.51.dec = bf16[8,64,256]{2,1,0:T(8,128)(2,1)S(1)} all-to-all(bf16[8,64,256]{2,1,0:T(8,128)(2,1)S(1)} %bitcast.21), channel_id=1, replica_groups=mesh['expert'=16,'tensor'=8,'dp'=4] {'tensor'}, dimensions={0} | all-to-all | bytes 524288 | tf_op jit(solution)/shard_map/all_to_all | solution.py:193
  183.7 13.7 %all_to_all.52.got = bf16[16,32,128]{2,1,0:T(8,128)(2,1)S(1)} all-to-all(bf16[16,32,128]{2,1,0:T(8,128)(2,1)S(1)} %shard_map.123), channel_id=1, replica_groups=mesh['expert'=16,'tensor'=8,'dp'=4] {'expert'}, dimensions={0} | all-to-all | bytes 262144 | tf_op jit(solution)/shard_map/all_to_all | solution.py:271
  (71 shorter events, 45.8 us)
Async XLA Ops:
  4.0 18.1 %all-to-all-start.2 = ((bf16[16,48,128]{2,1,0:T(8,128)(2,1)}), bf16[16,48,128]{2,1,0:T(8,128)(2,1)S(1)}, u32[]{:S(2)}, u32[]{:S(2)}) async-start(bf16[16,48,128]{2,1,0:T(8,128)(2,1)} %get-tuple-element.48), calls=%async_computation.2 | async-start | bytes 393216 | tf_op jit(solution)/shard_map/all_to_all | solution.py:241
  23.9 35.6 %copy-start.2 = (bf16[1,2048,256]{2,1,0:T(8,128)(2,1)S(1)}, bf16[1,2048,256]{2,1,0:T(8,128)(2,1)}, u32[]{:S(2)}) copy-start(bf16[1,2048,256]{2,1,0:T(8,128)(2,1)} %param.15) | copy-start | bytes 3145732
  46.4 29.4 %all-to-all-start.5 = ((bf16[8,64,256]{2,1,0:T(8,128)(2,1)}), bf16[8,64,256]{2,1,0:T(8,128)(2,1)S(1)}, u32[]{:S(2)}, u32[]{:S(2)}) async-start(bf16[8,64,256]{2,1,0:T(8,128)(2,1)} %get-tuple-element.56), calls=%async_computation.5 | async-start | bytes 524288 | tf_op jit(solution)/shard_map/all_to_all | solution.py:193
  49.8 11.5 %collective-permute-start.6 = (bf16[512,256]{1,0:T(8,128)(2,1)}, bf16[512,256]{1,0:T(8,128)(2,1)S(1)}, u32[]{:S(2)}, u32[]{:S(2)}) collective-permute-start(bf16[512,256]{1,0:T(8,128)(2,1)} %bitcast.7.x0), channel_id=1, source_target_pairs={{0,1},{1,2},{2,3},{3,0},{4,5},{5,6},{6,7},{7,4},{8,9},{9,10},{10,1... | collective-permute-start | bytes 786440 | tf_op jit(solution)/shard_map/ppermute | solution.py:189
  53.0 10.8 %collective-permute-start.7 = (bf16[512,256]{1,0:T(8,128)(2,1)}, bf16[512,256]{1,0:T(8,128)(2,1)S(1)}, u32[]{:S(2)}, u32[]{:S(2)}) collective-permute-start(bf16[512,256]{1,0:T(8,128)(2,1)} %bitcast.7.x0), channel_id=1, source_target_pairs={{0,2},{1,3},{2,0},{3,1},{4,6},{5,7},{6,4},{7,5},{8,10},{9,11},{10,... | collective-permute-start | bytes 786440 | tf_op jit(solution)/shard_map/ppermute | solution.py:189
  55.7 14.7 %collective-permute-start.8 = (bf16[512,256]{1,0:T(8,128)(2,1)}, bf16[512,256]{1,0:T(8,128)(2,1)S(1)}, u32[]{:S(2)}, u32[]{:S(2)}) collective-permute-start(bf16[512,256]{1,0:T(8,128)(2,1)} %bitcast.7.x0), channel_id=1, source_target_pairs={{0,3},{1,0},{2,1},{3,2},{4,7},{5,4},{6,5},{7,6},{8,11},{9,8},{10,9... | collective-permute-start | bytes 786440 | tf_op jit(solution)/shard_map/ppermute | solution.py:189
  73.9 21.8 %collective-permute-start.9 = (bf16[512,256]{1,0:T(8,128)(2,1)}, bf16[512,256]{1,0:T(8,128)(2,1)S(1)}, u32[]{:S(2)}, u32[]{:S(2)}) collective-permute-start(bf16[512,256]{1,0:T(8,128)(2,1)} %get-tuple-element.53), channel_id=1, source_target_pairs={{0,1},{1,2},{2,3},{3,0},{4,5},{5,6},{6,7},{7,4},{8,9},{9,10},{10,1... | collective-permute-start | bytes 786440 | tf_op jit(solution)/shard_map/ppermute | solution.py:189
  75.8 26.6 %all-to-all-start.7 = ((bf16[8,64,256]{2,1,0:T(8,128)(2,1)}), bf16[8,64,256]{2,1,0:T(8,128)(2,1)S(1)}, u32[]{:S(2)}, u32[]{:S(2)}) async-start(bf16[8,64,256]{2,1,0:T(8,128)(2,1)} %get-tuple-element.61), calls=%async_computation.7 | async-start | bytes 524288 | tf_op jit(solution)/shard_map/all_to_all | solution.py:193
  82.4 15.5 %collective-permute-start.10 = (bf16[512,256]{1,0:T(8,128)(2,1)}, bf16[512,256]{1,0:T(8,128)(2,1)S(1)}, u32[]{:S(2)}, u32[]{:S(2)}) collective-permute-start(bf16[512,256]{1,0:T(8,128)(2,1)} %copy-done.13), channel_id=1, source_target_pairs={{0,2},{1,3},{2,0},{3,1},{4,6},{5,7},{6,4},{7,5},{8,10},{9,11},{10,... | collective-permute-start | bytes 786440 | tf_op jit(solution)/shard_map/ppermute | solution.py:189
  84.4 17.1 %collective-permute-start.11 = (bf16[512,256]{1,0:T(8,128)(2,1)}, bf16[512,256]{1,0:T(8,128)(2,1)S(1)}, u32[]{:S(2)}, u32[]{:S(2)}) collective-permute-start(bf16[512,256]{1,0:T(8,128)(2,1)} %copy-done.12), channel_id=1, source_target_pairs={{0,3},{1,0},{2,1},{3,2},{4,7},{5,4},{6,5},{7,6},{8,11},{9,8},{10,9... | collective-permute-start | bytes 786440 | tf_op jit(solution)/shard_map/ppermute | solution.py:189
  88.4 20.9 %collective-permute-start.12 = (bf16[512,256]{1,0:T(8,128)(2,1)S(1)}, bf16[512,256]{1,0:T(8,128)(2,1)}, u32[]{:S(2)}, u32[]{:S(2)}) collective-permute-start(bf16[512,256]{1,0:T(8,128)(2,1)S(1)} %bitcast.31), channel_id=1, source_target_pairs={{0,1},{1,2},{2,3},{3,0},{4,5},{5,6},{6,7},{7,4},{8,9},{9,10},{10,1... | collective-permute-start | bytes 786440 | tf_op jit(solution)/shard_map/ppermute | solution.py:189
  90.7 18.6 %collective-permute-start.13 = (bf16[512,256]{1,0:T(8,128)(2,1)S(1)}, bf16[512,256]{1,0:T(8,128)(2,1)}, u32[]{:S(2)}, u32[]{:S(2)}) collective-permute-start(bf16[512,256]{1,0:T(8,128)(2,1)S(1)} %bitcast.32), channel_id=1, source_target_pairs={{0,2},{1,3},{2,0},{3,1},{4,6},{5,7},{6,4},{7,5},{8,10},{9,11},{10,... | collective-permute-start | bytes 786440 | tf_op jit(solution)/shard_map/ppermute | solution.py:189
  95.7 15.4 %collective-permute-start.14 = (bf16[512,256]{1,0:T(8,128)(2,1)S(1)}, bf16[512,256]{1,0:T(8,128)(2,1)}, u32[]{:S(2)}, u32[]{:S(2)}) collective-permute-start(bf16[512,256]{1,0:T(8,128)(2,1)S(1)} %bitcast.33), channel_id=1, source_target_pairs={{0,3},{1,0},{2,1},{3,2},{4,7},{5,4},{6,5},{7,6},{8,11},{9,8},{10,9... | collective-permute-start | bytes 786440 | tf_op jit(solution)/shard_map/ppermute | solution.py:189
  102.4 32.7 %all-to-all-start.4 = ((bf16[8,64,256]{2,1,0:T(8,128)(2,1)}), bf16[8,64,256]{2,1,0:T(8,128)(2,1)S(1)}, u32[]{:S(2)}, u32[]{:S(2)}) async-start(bf16[8,64,256]{2,1,0:T(8,128)(2,1)} %bitcast.10), calls=%async_computation.4 | async-start | bytes 524288 | tf_op jit(solution)/shard_map/all_to_all | solution.py:193
  113.5 15.2 %collective-permute-start.15 = (bf16[512,256]{1,0:T(8,128)(2,1)S(1)}, bf16[512,256]{1,0:T(8,128)(2,1)S(1)}, u32[]{:S(2)}, u32[]{:S(2)}) collective-permute-start(bf16[512,256]{1,0:T(8,128)(2,1)S(1)} %get-tuple-element.58), channel_id=1, source_target_pairs={{0,1},{1,2},{2,3},{3,0},{4,5},{5,6},{6,7},{7,4},{8,9},{9,10},{10,1... | collective-permute-start | bytes 786440 | tf_op jit(solution)/shard_map/ppermute | solution.py:189
  115.4 15.5 %collective-permute-start.16 = (bf16[512,256]{1,0:T(8,128)(2,1)S(1)}, bf16[512,256]{1,0:T(8,128)(2,1)S(1)}, u32[]{:S(2)}, u32[]{:S(2)}) collective-permute-start(bf16[512,256]{1,0:T(8,128)(2,1)S(1)} %get-tuple-element.59), channel_id=1, source_target_pairs={{0,2},{1,3},{2,0},{3,1},{4,6},{5,7},{6,4},{7,5},{8,10},{9,11},{10,... | collective-permute-start | bytes 786440 | tf_op jit(solution)/shard_map/ppermute | solution.py:189
  117.6 16.7 %collective-permute-start.17 = (bf16[512,256]{1,0:T(8,128)(2,1)S(1)}, bf16[512,256]{1,0:T(8,128)(2,1)S(1)}, u32[]{:S(2)}, u32[]{:S(2)}) collective-permute-start(bf16[512,256]{1,0:T(8,128)(2,1)S(1)} %get-tuple-element.60), channel_id=1, source_target_pairs={{0,3},{1,0},{2,1},{3,2},{4,7},{5,4},{6,5},{7,6},{8,11},{9,8},{10,9... | collective-permute-start | bytes 786440 | tf_op jit(solution)/shard_map/ppermute | solution.py:189
  121.6 20.2 %collective-permute-start.18 = (bf16[512,256]{1,0:T(8,128)(2,1)S(1)}, bf16[512,256]{1,0:T(8,128)(2,1)S(1)}, u32[]{:S(2)}, u32[]{:S(2)}) collective-permute-start(bf16[512,256]{1,0:T(8,128)(2,1)S(1)} %bitcast.27), channel_id=1, source_target_pairs={{0,1},{1,2},{2,3},{3,0},{4,5},{5,6},{6,7},{7,4},{8,9},{9,10},{10,1... | collective-permute-start | bytes 786440 | tf_op jit(solution)/shard_map/ppermute | solution.py:189
  123.8 18.0 %collective-permute-start.19 = (bf16[512,256]{1,0:T(8,128)(2,1)S(1)}, bf16[512,256]{1,0:T(8,128)(2,1)S(1)}, u32[]{:S(2)}, u32[]{:S(2)}) collective-permute-start(bf16[512,256]{1,0:T(8,128)(2,1)S(1)} %bitcast.28), channel_id=1, source_target_pairs={{0,2},{1,3},{2,0},{3,1},{4,6},{5,7},{6,4},{7,5},{8,10},{9,11},{10,... | collective-permute-start | bytes 786440 | tf_op jit(solution)/shard_map/ppermute | solution.py:189
  128.7 15.0 %collective-permute-start.20 = (bf16[512,256]{1,0:T(8,128)(2,1)S(1)}, bf16[512,256]{1,0:T(8,128)(2,1)S(1)}, u32[]{:S(2)}, u32[]{:S(2)}) collective-permute-start(bf16[512,256]{1,0:T(8,128)(2,1)S(1)} %bitcast.29), channel_id=1, source_target_pairs={{0,3},{1,0},{2,1},{3,2},{4,7},{5,4},{6,5},{7,6},{8,11},{9,8},{10,9... | collective-permute-start | bytes 786440 | tf_op jit(solution)/shard_map/ppermute | solution.py:189
  135.1 30.9 %all-to-all-start.6 = ((bf16[8,64,256]{2,1,0:T(8,128)(2,1)}), bf16[8,64,256]{2,1,0:T(8,128)(2,1)S(1)}, u32[]{:S(2)}, u32[]{:S(2)}) async-start(bf16[8,64,256]{2,1,0:T(8,128)(2,1)} %bitcast.12), calls=%async_computation.6 | async-start | bytes 524288 | tf_op jit(solution)/shard_map/all_to_all | solution.py:193
  146.7 9.2 %collective-permute-start.21 = (bf16[512,256]{1,0:T(8,128)(2,1)S(1)}, bf16[512,256]{1,0:T(8,128)(2,1)S(1)}, u32[]{:S(2)}, u32[]{:S(2)}) collective-permute-start(bf16[512,256]{1,0:T(8,128)(2,1)S(1)} %get-tuple-element.65), channel_id=1, source_target_pairs={{0,1},{1,2},{2,3},{3,0},{4,5},{5,6},{6,7},{7,4},{8,9},{9,10},{10,1... | collective-permute-start | bytes 786440 | tf_op jit(solution)/shard_map/ppermute | solution.py:189
  148.6 10.0 %collective-permute-start.22 = (bf16[512,256]{1,0:T(8,128)(2,1)S(1)}, bf16[512,256]{1,0:T(8,128)(2,1)S(1)}, u32[]{:S(2)}, u32[]{:S(2)}) collective-permute-start(bf16[512,256]{1,0:T(8,128)(2,1)S(1)} %get-tuple-element.66), channel_id=1, source_target_pairs={{0,2},{1,3},{2,0},{3,1},{4,6},{5,7},{6,4},{7,5},{8,10},{9,11},{10,... | collective-permute-start | bytes 786440 | tf_op jit(solution)/shard_map/ppermute | solution.py:189
  150.8 15.0 %collective-permute-start.23 = (bf16[512,256]{1,0:T(8,128)(2,1)S(1)}, bf16[512,256]{1,0:T(8,128)(2,1)S(1)}, u32[]{:S(2)}, u32[]{:S(2)}) collective-permute-start(bf16[512,256]{1,0:T(8,128)(2,1)S(1)} %get-tuple-element.67), channel_id=1, source_target_pairs={{0,3},{1,0},{2,1},{3,2},{4,7},{5,4},{6,5},{7,6},{8,11},{9,8},{10,9... | collective-permute-start | bytes 786440 | tf_op jit(solution)/shard_map/ppermute | solution.py:189
  (15 other events, 78.9 us)

commit v4 on v2

--- a/solution.py
+++ b/solution.py
@@ -119,9 +119,9 @@
     dec_at[...] = at
     near = nt(turned[FEATS:], pick(at, HELD)).astype(BF)
     far = nt(turned[FEATS:], pick(at, ROWS - HELD, HELD)).astype(BF)
+    dec[...] = near
     for t in range(T):
         enc[t] = turned[:FEATS]
-        dec[t] = near
         rest[t] = far
 
 
@@ -163,9 +163,10 @@
     return acc.astype(BF)
 
 
-def pack_body(enc, dec, rest, dec_at, sent):
+def pack_body(enc, dec_a, dec_b, dec_c, dec_d, rest, dec_at, sent):
     at = dec_at[...]
-    back = nn(total(dec), pick(at, HELD)) + nn(total(rest), pick(at, ROWS - HELD, HELD))
+    dec = sum(ref[...].astype(F32) for ref in (dec_a, dec_b, dec_c, dec_d)).astype(BF)
+    back = nn(dec, pick(at, HELD)) + nn(total(rest), pick(at, ROWS - HELD, HELD))
     both = jnp.concatenate([total(enc).astype(F32), back], axis=0)
     sent[...] = both.T.astype(BF).reshape(EXPERTS, CAP, 2 * FEATS)
 
@@ -203,15 +204,56 @@
     return call(expert_body, [part] * 4, 7, smem=(0,), flops=work, moved=6 << 20)(me, *blocks, *turned)
 
 
-def scatter(parts):
+def arrive(parts):
+    return [parts[0]] + [shift(parts[k], k) for k in (1, 2, 3)]
+
+
+def settle(parts):
     rows = parts[0].shape[1]
-    sums = [parts[0]] + [shift(parts[k], k) for k in (1, 2, 3)]
-    added = call(add_body, shape((T * FEATS, rows)), 4, moved=5 << 19)(*sums)
+    added = call(add_body, shape((T * FEATS, rows)), 4, moved=5 << 19)(*parts)
     return over_tensor(added.reshape(T, FEATS, rows))
 
 
 def through(block, turned, me):
-    return scatter(expert(gather(over_tensor(block)), turned, me))
+    return settle(arrive(expert(gather(over_tensor(block)), turned, me)))
+
+
+def tie(values, others):
+    done = lax.optimization_barrier((list(values), list(others)))
+    return done[0], done[1]
+
+
+def copies_body(a, b, c, d, out):
+    for t in range(T):
+        for k, ref in enumerate((a, b, c, d)):
+            out[t, k] = ref[...]
+
+
+def crossed_body(me, x, w_in, w_out, part):
+    d = me[0]
+    rows = x.shape[3]
+    hidden = None
+    for k in range(DP):
+        block = x[:, k].reshape(T * FEATS, rows)
+        term = nn(w_in[lax.rem(d - k + DP, DP)], block)
+        hidden = term if hidden is None else hidden + term
+    hidden = jnp.maximum(hidden, 0.0).astype(BF)
+    for k in range(DP):
+        block = nn(w_out[lax.rem(d + k, DP)], hidden).astype(BF)
+        part[:, k] = block.reshape(T, FEATS, rows)
+
+
+def crossed_sum_body(got, a, b, c, d):
+    for k, ref in enumerate((a, b, c, d)):
+        acc = got[0, k].astype(F32)
+        for t in range(1, T):
+            acc = acc + got[t, k].astype(F32)
+        ref[...] = acc.astype(BF)
+
+
+def expert_crossed(x, turned, me):
+    work = 4 * x.shape[3] * UNITS * T * DP * FEATS
+    return call(crossed_body, shape(x.shape), 4, smem=(0,), flops=work, moved=4 << 20)(me, x, *turned)
 
 
 def shards(
@@ -244,23 +286,29 @@
 
     enc_turned = turn(enc_w_in, enc_w_out)
     dec_turned = turn(dec_w_in, dec_w_out)
-    near = shape((T, FEATS, HELD))
     far = shape((T, FEATS, ROWS - HELD))
     enc_block, dec_block, rest_block, moved_to, most = call(
         spread_body,
-        [shape((T, FEATS, ROWS)), near, far, shape((1, ROWS), jnp.int32), shape((1,), jnp.int32)],
+        [shape((T, FEATS, ROWS)), shape((FEATS, HELD)), far, shape((1, ROWS), jnp.int32), shape((1,), jnp.int32)],
         1,
         smem_out=(4,),
         moved=1 << 20,
     )(got)
 
+    near_x = [dec_block] + [shift(dec_block, k) for k in (1, 2, 3)]
+    dec_x = call(copies_body, shape((T, DP, FEATS, HELD)), 4, moved=1 << 20)(*near_x)
     enc_t = over_tensor(enc_block)
-    dec_block, enc_t = lax.optimization_barrier((dec_block, enc_t))
-    dec_t = over_tensor(dec_block)
+    (dec_x,), (enc_t,) = tie([dec_x], [enc_t])
     enc_x = gather(enc_t)
-    dec_x = gather(dec_t)
-    enc_sums = scatter(expert(enc_x, enc_turned, me))
-    dec_sums = scatter(expert(dec_x, dec_turned, me))
+    dec_x = over_tensor(dec_x)
+    (dec_x,), enc_x = tie([dec_x], enc_x)
+    dec_parts = expert_crossed(dec_x, dec_turned, me)
+    enc_got = arrive(expert(enc_x, enc_turned, me))
+    dec_parts = over_tensor(dec_parts)
+    (dec_parts,), (enc_got[0],) = tie([dec_parts], [enc_got[0]])
+    dec_parts = call(crossed_sum_body, [shape((FEATS, HELD))] * 4, 1, moved=1 << 20)(dec_parts)
+    dec_sums = arrive(dec_parts)
+    enc_sums = settle(enc_got)
     rest_sums = lax.cond(
         most[0] > HELD,
         lambda b, w: through(b, w, me),
@@ -270,7 +318,7 @@
     )
 
     packed = shape((EXPERTS, CAP, 2 * FEATS))
-    back = call(pack_body, packed, 4, moved=1 << 20)(enc_sums, dec_sums, rest_sums, moved_to)
+    back = call(pack_body, packed, 7, moved=1 << 20)(enc_sums, *dec_sums, rest_sums, moved_to)
     got = lax.all_to_all(back, "expert", split_axis=0, concat_axis=0, tiled=True)
     enc_out, dec_out = call(
         mix_body, [shape(enc.shape), shape(dec.shape)], 6, moved=1 << 18

time: 195 us -> 176 us (0.903)
  blocking collectives: 93.9 us -> 14.1 us
  starting transfers between devices: 42.6 us -> 72.8 us
  waiting for transfers between devices: 41.6 us -> 63.6 us
  local copies, waits for them, and re-layouts: 2.88 us -> 8.7 us
  Pallas kernels: 11.7 us -> 14.2 us
    all_to_all x4 -> x0, blocking collectives: 79.2 us -> none  [the longest x3 59.4 us: over_tensor(): lax.all_to_all(block, 'tensor', split_axis=0, concat_axis=0, tiled=True)]
    all_to_all x1 -> x4, waiting for transfers between devices: 0.01 us -> 23.1 us  [over_tensor(): lax.all_to_all(block, 'tensor', split_axis=0, concat_axis=0, tiled=True)]
    all_to_all x1 -> x4, starting transfers between devices: 3.41 us -> 25.3 us  [over_tensor(): lax.all_to_all(block, 'tensor', split_axis=0, concat_axis=0, tiled=True)]
    all_to_all x0 -> x1, starting transfers between devices: none -> 10.2 us  [shards(): lax.all_to_all(sent, 'expert', split_axis=0, concat_axis=0, tiled=True)]
    ppermute x12, waiting for transfers between devices: 41.6 us -> 34.4 us  [shift(): return lax.ppermute(value, 'dp', [(i, (i + k) % DP) for i in range(DP)])]
    all_to_all x0 -> x1, waiting for transfers between devices: none -> 6.09 us  [shards(): lax.all_to_all(sent, 'expert', split_axis=0, concat_axis=0, tiled=True)]
    unnamed x24 -> x32, local copies, waits for them, and re-layouts: 2.86 us -> 8.68 us
    pallas_call x4 -> x6, Pallas kernels: 2.55 us -> 7.4 us  [the longest x1 3.86 us: expert_crossed(): call(crossed_body, shape(x.shape), 4, smem=(0,), flops=work, moved=4 << 20)]
  transfers between devices with their start and end apart: 13 -> 17, of which waited for: 5 -> 12; matrix products, arithmetic and copies ran while one was open for 0% -> 0% of each run, Pallas kernels for 5% -> 3%
where the time goes in v4:
time: 176 us; the launch traced here: 175 us
  starting transfers between devices  72.8 us (41%)
  waiting for transfers between devices  63.6 us (36%)
  Pallas kernels  14.2 us (8%)
  blocking collectives  14.1 us (8%)
  local copies, waits for them, and re-layouts  8.7 us (5%)
    ppermute x12, starting transfers between devices, shift(): return lax.ppermute(value, 'dp', [(i, (i + k) % DP) for i in range(DP)])  37.3 us
    ppermute x12, waiting for transfers between devices, shift(): return lax.ppermute(value, 'dp', [(i, (i + k) % DP) for i in range(DP)])  34.4 us
    all_to_all x4, starting transfers between devices, over_tensor(): lax.all_to_all(block, 'tensor', split_axis=0, concat_axis=0, tiled=True)  25.3 us
    all_to_all x4, waiting for transfers between devices, over_tensor(): lax.all_to_all(block, 'tensor', split_axis=0, concat_axis=0, tiled=True)  23.1 us
    all_to_all x1, blocking collectives, shards(): lax.all_to_all(back, 'expert', split_axis=0, concat_axis=0, tiled=True)  14.1 us
    all_to_all x1, starting transfers between devices, shards(): lax.all_to_all(sent, 'expert', split_axis=0, concat_axis=0, tiled=True)  10.2 us
    unnamed x32, local copies, waits for them, and re-layouts  8.68 us
    all_to_all x1, waiting for transfers between devices, shards(): lax.all_to_all(sent, 'expert', split_axis=0, concat_axis=0, tiled=True)  6.09 us
  transfers between devices with their start and end apart: 17, of which 12 were waited for; matrix products, arithmetic and copies ran while one was open for 0% of the time, Pallas kernels for 3%

profile of v4, /device:TPU:1, one launch (start us, length us, event | category | flops | bytes accessed | tf_op | source)
XLA Modules:
  0.0 174.9 jit_solution(4768966753785798447)
XLA Ops:
  4.0 10.2 %all-to-all-start.2 = ((bf16[16,48,128]{2,1,0:T(8,128)(2,1)}), bf16[16,48,128]{2,1,0:T(8,128)(2,1)S(1)}, u32[]{:S(2)}, u32[]{:S(2)}) async-start(bf16[16,48,128]{2,1,0:T(8,128)(2,1)} %get-tuple-element.52), calls=%async_computation.2 | async-start | bytes 393216 | tf_op jit(solution)/shard_map/all_to_all | solution.py:281
  18.5 6.1 %all-to-all-done.2.got = bf16[16,48,128]{2,1,0:T(8,128)(2,1)S(1)} async-done(((bf16[16,48,128]{2,1,0:T(8,128)(2,1)}), bf16[16,48,128]{2,1,0:T(8,128)(2,1)S(1)}, u32[]{:S(2)}, u32[]{:S(2)}) %all-to-all-start.2) | async-done | bytes 196640 | tf_op jit(solution)/shard_map/all_to_all | solution.py:281
  26.3 8.4 %all-to-all-start.3 = ((bf16[8,64,512]{2,1,0:T(8,128)(2,1)}), bf16[8,64,512]{2,1,0:T(8,128)(2,1)S(1)}, u32[]{:S(2)}, u32[]{:S(2)}) async-start(bf16[8,64,512]{2,1,0:T(8,128)(2,1)} %get-tuple-element.54), calls=%async_computation.3 | async-start | bytes 1048576 | tf_op jit(solution)/shard_map/all_to_all | solution.py:192
  34.7 4.4 %collective-permute-start.8 = (bf16[64,256]{1,0:T(8,128)(2,1)S(1)}, bf16[64,256]{1,0:T(8,128)(2,1)S(1)}, u32[]{:S(2)}, u32[]{:S(2)}) collective-permute-start(bf16[64,256]{1,0:T(8,128)(2,1)S(1)} %get-tuple-element.53.a), channel_id=1, source_target_pairs={{0,3},{1,0},{2,1},{3,2},{4,7},{5,4},{6,5},{7,6},{8,11},{9,8},{10,9... | collective-permute-start | bytes 98312 | tf_op jit(solution)/shard_map/ppermute | solution.py:188
  41.5 2.5 %collective-permute-start.6 = (bf16[64,256]{1,0:T(8,128)(2,1)S(1)}, bf16[64,256]{1,0:T(8,128)(2,1)S(1)}, u32[]{:S(2)}, u32[]{:S(2)}) collective-permute-start(bf16[64,256]{1,0:T(8,128)(2,1)S(1)} %get-tuple-element.53.a), channel_id=1, source_target_pairs={{0,1},{1,2},{2,3},{3,0},{4,5},{5,6},{6,7},{7,4},{8,9},{9,10},{10,1... | collective-permute-start | bytes 98312 | tf_op jit(solution)/shard_map/ppermute | solution.py:188
  48.4 4.3 %all-to-all-done.3 = bf16[8,64,512]{2,1,0:T(8,128)(2,1)S(1)} async-done(((bf16[8,64,512]{2,1,0:T(8,128)(2,1)}), bf16[8,64,512]{2,1,0:T(8,128)(2,1)S(1)}, u32[]{:S(2)}, u32[]{:S(2)}) %all-to-all-start.3) | async-done | bytes 524320 | tf_op jit(solution)/shard_map/all_to_all | solution.py:192
  52.7 3.6 %all-to-all-start.4 = ((bf16[8,4,64,256]{3,2,1,0:T(8,128)(2,1)}), bf16[8,4,64,256]{3,2,1,0:T(8,128)(2,1)S(1)}, u32[]{:S(2)}, u32[]{:S(2)}) async-start(bf16[8,4,64,256]{3,2,1,0:T(8,128)(2,1)} %shard_map.115), calls=%async_computation.4 | async-start | bytes 2097152 | tf_op jit(solution)/shard_map/all_to_all | solution.py:192
  56.3 4.4 %collective-permute-start.11 = (bf16[512,512]{1,0:T(8,128)(2,1)S(1)}, bf16[512,512]{1,0:T(8,128)(2,1)S(1)}, u32[]{:S(2)}, u32[]{:S(2)}) collective-permute-start(bf16[512,512]{1,0:T(8,128)(2,1)S(1)} %bitcast.17), channel_id=1, source_target_pairs={{0,3},{1,0},{2,1},{3,2},{4,7},{5,4},{6,5},{7,6},{8,11},{9,8},{10,9... | collective-permute-start | bytes 1572872 | tf_op jit(solution)/shard_map/ppermute | solution.py:188
  63.1 2.5 %collective-permute-start.9 = (bf16[512,512]{1,0:T(8,128)(2,1)S(1)}, bf16[512,512]{1,0:T(8,128)(2,1)S(1)}, u32[]{:S(2)}, u32[]{:S(2)}) collective-permute-start(bf16[512,512]{1,0:T(8,128)(2,1)S(1)} %bitcast.19), channel_id=1, source_target_pairs={{0,1},{1,2},{2,3},{3,0},{4,5},{5,6},{6,7},{7,4},{8,9},{9,10},{10,1... | collective-permute-start | bytes 1572872 | tf_op jit(solution)/shard_map/ppermute | solution.py:188
  65.7 7.3 %collective-permute-done.11.x3 = bf16[512,512]{1,0:T(8,128)(2,1)S(1)} collective-permute-done((bf16[512,512]{1,0:T(8,128)(2,1)S(1)}, bf16[512,512]{1,0:T(8,128)(2,1)S(1)}, u32[]{:S(2)}, u32[]{:S(2)}) %collective-permute-start.11) | collective-permute-done | bytes 524320 | tf_op jit(solution)/shard_map/ppermute | solution.py:188
  72.9 3.9 %collective-permute-done.10.x2 = bf16[512,512]{1,0:T(8,128)(2,1)S(1)} collective-permute-done((bf16[512,512]{1,0:T(8,128)(2,1)S(1)}, bf16[512,512]{1,0:T(8,128)(2,1)S(1)}, u32[]{:S(2)}, u32[]{:S(2)}) %collective-permute-start.10) | collective-permute-done | bytes 524320 | tf_op jit(solution)/shard_map/ppermute | solution.py:188
  77.7 11.5 %collective-permute-done.9.x1 = bf16[512,512]{1,0:T(8,128)(2,1)S(1)} collective-permute-done((bf16[512,512]{1,0:T(8,128)(2,1)S(1)}, bf16[512,512]{1,0:T(8,128)(2,1)S(1)}, u32[]{:S(2)}, u32[]{:S(2)}) %collective-permute-start.9) | collective-permute-done | bytes 524320 | tf_op jit(solution)/shard_map/ppermute | solution.py:188
  90.0 3.9 %shard_map.117 = bf16[8,4,64,256]{3,2,1,0:T(8,128)(2,1)} custom-call(s32[1]{0:T(128)} %bitcast.2.me, bf16[8,4,64,256]{3,2,1,0:T(8,128)(2,1)S(1)} %all-to-all-done.4.x, bf16[4,256,512]{2,1,0:T(8,128)(2,1)} %get-tuple-element.58.w_in, bf16[4,512,256]{2,1,0:T(8,128)(2,1)} %get-tuple-element.59.w_out), custom_call_target="tpu_custom_call" | custom-call | flops 536870912 | bytes 4194304 | tf_op jit(solution)/shard_map/pallas_call | solution.py:256
  93.8 6.7 %all-to-all-start.5 = ((bf16[8,4,64,256]{3,2,1,0:T(8,128)(2,1)}), bf16[8,4,64,256]{3,2,1,0:T(8,128)(2,1)S(1)}, u32[]{:S(2)}, u32[]{:S(2)}) async-start(bf16[8,4,64,256]{3,2,1,0:T(8,128)(2,1)} %shard_map.117), calls=%async_computation.5 | async-start | bytes 2097152 | tf_op jit(solution)/shard_map/all_to_all | solution.py:192
  109.6 4.1 %collective-permute-start.14 = (bf16[512,512]{1,0:T(8,128)(2,1)}, bf16[512,512]{1,0:T(8,128)(2,1)S(1)}, u32[]{:S(2)}, u32[]{:S(2)}) collective-permute-start(bf16[512,512]{1,0:T(8,128)(2,1)} %get-tuple-element.70), channel_id=1, source_target_pairs={{0,3},{1,0},{2,1},{3,2},{4,7},{5,4},{6,5},{7,6},{8,11},{9,8},{10,9... | collective-permute-start | bytes 1572872 | tf_op jit(solution)/shard_map/ppermute | solution.py:188
  113.6 16.1 %all-to-all-done.5.got = bf16[8,4,64,256]{3,2,1,0:T(8,128)(2,1)S(1)} async-done(((bf16[8,4,64,256]{3,2,1,0:T(8,128)(2,1)}), bf16[8,4,64,256]{3,2,1,0:T(8,128)(2,1)S(1)}, u32[]{:S(2)}, u32[]{:S(2)}) %all-to-all-start.5) | async-done | bytes 1048608 | tf_op jit(solution)/shard_map/all_to_all | solution.py:192
  129.7 2.7 %collective-permute-done.12.b = bf16[512,512]{1,0:T(8,128)(2,1)S(1)} collective-permute-done((bf16[512,512]{1,0:T(8,128)(2,1)}, bf16[512,512]{1,0:T(8,128)(2,1)S(1)}, u32[]{:S(2)}, u32[]{:S(2)}) %collective-permute-start.12) | collective-permute-done | bytes 524320 | tf_op jit(solution)/shard_map/ppermute | solution.py:188
  132.4 2.8 %collective-permute-done.14.d = bf16[512,512]{1,0:T(8,128)(2,1)S(1)} collective-permute-done((bf16[512,512]{1,0:T(8,128)(2,1)}, bf16[512,512]{1,0:T(8,128)(2,1)S(1)}, u32[]{:S(2)}, u32[]{:S(2)}) %collective-permute-start.14) | collective-permute-done | bytes 524320 | tf_op jit(solution)/shard_map/ppermute | solution.py:188
  136.2 6.6 %all-to-all-start.6 = ((bf16[8,64,512]{2,1,0:T(8,128)(2,1)}), bf16[8,64,512]{2,1,0:T(8,128)(2,1)S(1)}, u32[]{:S(2)}, u32[]{:S(2)}) async-start(bf16[8,64,512]{2,1,0:T(8,128)(2,1)} %bitcast.12), calls=%async_computation.6 | async-start | bytes 1048576 | tf_op jit(solution)/shard_map/all_to_all | solution.py:192
  143.0 2.8 %collective-permute-start.15 = (bf16[64,256]{1,0:T(8,128)(2,1)S(1)}, bf16[64,256]{1,0:T(8,128)(2,1)S(1)}, u32[]{:S(2)}, u32[]{:S(2)}) collective-permute-start(bf16[64,256]{1,0:T(8,128)(2,1)S(1)} %get-tuple-element.73), channel_id=1, source_target_pairs={{0,1},{1,2},{2,3},{3,0},{4,5},{5,6},{6,7},{7,4},{8,9},{9,10},{10,1... | collective-permute-start | bytes 98312 | tf_op jit(solution)/shard_map/ppermute | solution.py:188
  145.9 5.5 %collective-permute-start.16 = (bf16[64,256]{1,0:T(8,128)(2,1)S(1)}, bf16[64,256]{1,0:T(8,128)(2,1)S(1)}, u32[]{:S(2)}, u32[]{:S(2)}) collective-permute-start(bf16[64,256]{1,0:T(8,128)(2,1)S(1)} %get-tuple-element.74), channel_id=1, source_target_pairs={{0,2},{1,3},{2,0},{3,1},{4,6},{5,7},{6,4},{7,5},{8,10},{9,11},{10,... | collective-permute-start | bytes 98312 | tf_op jit(solution)/shard_map/ppermute | solution.py:188
  153.3 2.9 %collective-permute-done.17.dec_d = bf16[64,256]{1,0:T(8,128)(2,1)S(1)} collective-permute-done((bf16[64,256]{1,0:T(8,128)(2,1)S(1)}, bf16[64,256]{1,0:T(8,128)(2,1)S(1)}, u32[]{:S(2)}, u32[]{:S(2)}) %collective-permute-start.17) | collective-permute-done | bytes 32800 | tf_op jit(solution)/shard_map/ppermute | solution.py:188
  156.1 2.7 %all-to-all-done.6.enc = bf16[8,64,512]{2,1,0:T(8,128)(2,1)S(1)} async-done(((bf16[8,64,512]{2,1,0:T(8,128)(2,1)}), bf16[8,64,512]{2,1,0:T(8,128)(2,1)S(1)}, u32[]{:S(2)}, u32[]{:S(2)}) %all-to-all-start.6) | async-done | bytes 524320 | tf_op jit(solution)/shard_map/all_to_all | solution.py:192
  159.2 14.1 %all_to_all.40.got = bf16[16,32,128]{2,1,0:T(8,128)(2,1)S(1)} all-to-all(bf16[16,32,128]{2,1,0:T(8,128)(2,1)S(1)} %shard_map.122), channel_id=1, replica_groups=mesh['expert'=16,'tensor'=8,'dp'=4] {'expert'}, dimensions={0} | all-to-all | bytes 262144 | tf_op jit(solution)/shard_map/all_to_all | solution.py:322
  (56 shorter events, 33.6 us)
Async XLA Ops:
  4.0 20.6 %all-to-all-start.2 = ((bf16[16,48,128]{2,1,0:T(8,128)(2,1)}), bf16[16,48,128]{2,1,0:T(8,128)(2,1)S(1)}, u32[]{:S(2)}, u32[]{:S(2)}) async-start(bf16[16,48,128]{2,1,0:T(8,128)(2,1)} %get-tuple-element.52), calls=%async_computation.2 | async-start | bytes 393216 | tf_op jit(solution)/shard_map/all_to_all | solution.py:281
  14.2 1.2 copy-start
  15.4 1.2 copy-start.1
  26.3 26.5 %all-to-all-start.3 = ((bf16[8,64,512]{2,1,0:T(8,128)(2,1)}), bf16[8,64,512]{2,1,0:T(8,128)(2,1)S(1)}, u32[]{:S(2)}, u32[]{:S(2)}) async-start(bf16[8,64,512]{2,1,0:T(8,128)(2,1)} %get-tuple-element.54), calls=%async_computation.3 | async-start | bytes 1048576 | tf_op jit(solution)/shard_map/all_to_all | solution.py:192
  34.7 9.3 %collective-permute-start.8 = (bf16[64,256]{1,0:T(8,128)(2,1)S(1)}, bf16[64,256]{1,0:T(8,128)(2,1)S(1)}, u32[]{:S(2)}, u32[]{:S(2)}) collective-permute-start(bf16[64,256]{1,0:T(8,128)(2,1)S(1)} %get-tuple-element.53.a), channel_id=1, source_target_pairs={{0,3},{1,0},{2,1},{3,2},{4,7},{5,4},{6,5},{7,6},{8,11},{9,8},{10,9... | collective-permute-start | bytes 98312 | tf_op jit(solution)/shard_map/ppermute | solution.py:188
  39.1 6.5 %collective-permute-start.7 = (bf16[64,256]{1,0:T(8,128)(2,1)S(1)}, bf16[64,256]{1,0:T(8,128)(2,1)S(1)}, u32[]{:S(2)}, u32[]{:S(2)}) collective-permute-start(bf16[64,256]{1,0:T(8,128)(2,1)S(1)} %get-tuple-element.53.a), channel_id=1, source_target_pairs={{0,2},{1,3},{2,0},{3,1},{4,6},{5,7},{6,4},{7,5},{8,10},{9,11},{10,... | collective-permute-start | bytes 98312 | tf_op jit(solution)/shard_map/ppermute | solution.py:188
  41.5 5.9 %collective-permute-start.6 = (bf16[64,256]{1,0:T(8,128)(2,1)S(1)}, bf16[64,256]{1,0:T(8,128)(2,1)S(1)}, u32[]{:S(2)}, u32[]{:S(2)}) collective-permute-start(bf16[64,256]{1,0:T(8,128)(2,1)S(1)} %get-tuple-element.53.a), channel_id=1, source_target_pairs={{0,1},{1,2},{2,3},{3,0},{4,5},{5,6},{6,7},{7,4},{8,9},{9,10},{10,1... | collective-permute-start | bytes 98312 | tf_op jit(solution)/shard_map/ppermute | solution.py:188
  52.7 37.2 %all-to-all-start.4 = ((bf16[8,4,64,256]{3,2,1,0:T(8,128)(2,1)}), bf16[8,4,64,256]{3,2,1,0:T(8,128)(2,1)S(1)}, u32[]{:S(2)}, u32[]{:S(2)}) async-start(bf16[8,4,64,256]{3,2,1,0:T(8,128)(2,1)} %shard_map.115), calls=%async_computation.4 | async-start | bytes 2097152 | tf_op jit(solution)/shard_map/all_to_all | solution.py:192
  56.3 16.6 %collective-permute-start.11 = (bf16[512,512]{1,0:T(8,128)(2,1)S(1)}, bf16[512,512]{1,0:T(8,128)(2,1)S(1)}, u32[]{:S(2)}, u32[]{:S(2)}) collective-permute-start(bf16[512,512]{1,0:T(8,128)(2,1)S(1)} %bitcast.17), channel_id=1, source_target_pairs={{0,3},{1,0},{2,1},{3,2},{4,7},{5,4},{6,5},{7,6},{8,11},{9,8},{10,9... | collective-permute-start | bytes 1572872 | tf_op jit(solution)/shard_map/ppermute | solution.py:188
  60.7 16.2 %collective-permute-start.10 = (bf16[512,512]{1,0:T(8,128)(2,1)S(1)}, bf16[512,512]{1,0:T(8,128)(2,1)S(1)}, u32[]{:S(2)}, u32[]{:S(2)}) collective-permute-start(bf16[512,512]{1,0:T(8,128)(2,1)S(1)} %bitcast.18), channel_id=1, source_target_pairs={{0,2},{1,3},{2,0},{3,1},{4,6},{5,7},{6,4},{7,5},{8,10},{9,11},{10,... | collective-permute-start | bytes 1572872 | tf_op jit(solution)/shard_map/ppermute | solution.py:188
  63.1 26.0 %collective-permute-start.9 = (bf16[512,512]{1,0:T(8,128)(2,1)S(1)}, bf16[512,512]{1,0:T(8,128)(2,1)S(1)}, u32[]{:S(2)}, u32[]{:S(2)}) collective-permute-start(bf16[512,512]{1,0:T(8,128)(2,1)S(1)} %bitcast.19), channel_id=1, source_target_pairs={{0,1},{1,2},{2,3},{3,0},{4,5},{5,6},{6,7},{7,4},{8,9},{9,10},{10,1... | collective-permute-start | bytes 1572872 | tf_op jit(solution)/shard_map/ppermute | solution.py:188
  93.8 6.7 %copy-start.2 = (bf16[1,2048,256]{2,1,0:T(8,128)(2,1)S(1)}, bf16[1,2048,256]{2,1,0:T(8,128)(2,1)}, u32[]{:S(2)}) copy-start(bf16[1,2048,256]{2,1,0:T(8,128)(2,1)} %param.15) | copy-start | bytes 3145732
  93.8 35.9 %all-to-all-start.5 = ((bf16[8,4,64,256]{3,2,1,0:T(8,128)(2,1)}), bf16[8,4,64,256]{3,2,1,0:T(8,128)(2,1)S(1)}, u32[]{:S(2)}, u32[]{:S(2)}) async-start(bf16[8,4,64,256]{3,2,1,0:T(8,128)(2,1)} %shard_map.117), calls=%async_computation.5 | async-start | bytes 2097152 | tf_op jit(solution)/shard_map/all_to_all | solution.py:192
  100.5 1.2 copy-start.3
  101.7 1.2 copy-start.7
  105.2 27.2 %collective-permute-start.12 = (bf16[512,512]{1,0:T(8,128)(2,1)}, bf16[512,512]{1,0:T(8,128)(2,1)S(1)}, u32[]{:S(2)}, u32[]{:S(2)}) collective-permute-start(bf16[512,512]{1,0:T(8,128)(2,1)} %get-tuple-element.68), channel_id=1, source_target_pairs={{0,1},{1,2},{2,3},{3,0},{4,5},{5,6},{6,7},{7,4},{8,9},{9,10},{10,1... | collective-permute-start | bytes 1572872 | tf_op jit(solution)/shard_map/ppermute | solution.py:188
  107.1 25.3 %collective-permute-start.13 = (bf16[512,512]{1,0:T(8,128)(2,1)}, bf16[512,512]{1,0:T(8,128)(2,1)S(1)}, u32[]{:S(2)}, u32[]{:S(2)}) collective-permute-start(bf16[512,512]{1,0:T(8,128)(2,1)} %get-tuple-element.69), channel_id=1, source_target_pairs={{0,2},{1,3},{2,0},{3,1},{4,6},{5,7},{6,4},{7,5},{8,10},{9,11},{10,... | collective-permute-start | bytes 1572872 | tf_op jit(solution)/shard_map/ppermute | solution.py:188
  109.6 25.6 %collective-permute-start.14 = (bf16[512,512]{1,0:T(8,128)(2,1)}, bf16[512,512]{1,0:T(8,128)(2,1)S(1)}, u32[]{:S(2)}, u32[]{:S(2)}) collective-permute-start(bf16[512,512]{1,0:T(8,128)(2,1)} %get-tuple-element.70), channel_id=1, source_target_pairs={{0,3},{1,0},{2,1},{3,2},{4,7},{5,4},{6,5},{7,6},{8,11},{9,8},{10,9... | collective-permute-start | bytes 1572872 | tf_op jit(solution)/shard_map/ppermute | solution.py:188
  136.2 22.6 %all-to-all-start.6 = ((bf16[8,64,512]{2,1,0:T(8,128)(2,1)}), bf16[8,64,512]{2,1,0:T(8,128)(2,1)S(1)}, u32[]{:S(2)}, u32[]{:S(2)}) async-start(bf16[8,64,512]{2,1,0:T(8,128)(2,1)} %bitcast.12), calls=%async_computation.6 | async-start | bytes 1048576 | tf_op jit(solution)/shard_map/all_to_all | solution.py:192
  143.0 10.3 %collective-permute-start.15 = (bf16[64,256]{1,0:T(8,128)(2,1)S(1)}, bf16[64,256]{1,0:T(8,128)(2,1)S(1)}, u32[]{:S(2)}, u32[]{:S(2)}) collective-permute-start(bf16[64,256]{1,0:T(8,128)(2,1)S(1)} %get-tuple-element.73), channel_id=1, source_target_pairs={{0,1},{1,2},{2,3},{3,0},{4,5},{5,6},{6,7},{7,4},{8,9},{9,10},{10,1... | collective-permute-start | bytes 98312 | tf_op jit(solution)/shard_map/ppermute | solution.py:188
  145.9 7.4 %collective-permute-start.16 = (bf16[64,256]{1,0:T(8,128)(2,1)S(1)}, bf16[64,256]{1,0:T(8,128)(2,1)S(1)}, u32[]{:S(2)}, u32[]{:S(2)}) collective-permute-start(bf16[64,256]{1,0:T(8,128)(2,1)S(1)} %get-tuple-element.74), channel_id=1, source_target_pairs={{0,2},{1,3},{2,0},{3,1},{4,6},{5,7},{6,4},{7,5},{8,10},{9,11},{10,... | collective-permute-start | bytes 98312 | tf_op jit(solution)/shard_map/ppermute | solution.py:188
  151.3 4.8 %collective-permute-start.17 = (bf16[64,256]{1,0:T(8,128)(2,1)S(1)}, bf16[64,256]{1,0:T(8,128)(2,1)S(1)}, u32[]{:S(2)}, u32[]{:S(2)}) collective-permute-start(bf16[64,256]{1,0:T(8,128)(2,1)S(1)} %get-tuple-element.75), channel_id=1, source_target_pairs={{0,3},{1,0},{2,1},{3,2},{4,7},{5,4},{6,5},{7,6},{8,11},{9,8},{10,9... | collective-permute-start | bytes 98312 | tf_op jit(solution)/shard_map/ppermute | solution.py:188
  158.8 14.5 %copy-start.11 = (bf16[128,64]{0,1:T(8,128)(2,1)S(1)}, bf16[128,64]{0,1:T(8,128)(2,1)}, u32[]{:S(2)}) copy-start(bf16[128,64]{0,1:T(8,128)(2,1)} %param.12) | copy-start | bytes 49156
  159.2 14.1 %copy-start.9 = (bf16[144,64]{0,1:T(8,128)(2,1)S(1)}, bf16[144,64]{0,1:T(8,128)(2,1)}, u32[]{:S(2)}) copy-start(bf16[144,64]{0,1:T(8,128)(2,1)} %param.17) | copy-start | bytes 55300
  (9 other events, 6.8 us)

commit v5 on v4

--- a/solution.py
+++ b/solution.py
@@ -18,17 +18,24 @@
 UNITS = 256
 VMEM = pl.BlockSpec(memory_space=pltpu.VMEM)
 SMEM = pl.BlockSpec(memory_space=pltpu.SMEM)
-
-
-def call(body, out_shape, n_in, *, smem=(), smem_out=(), flops=0, moved=0):
+ANY = pl.BlockSpec(memory_space=pl.ANY)
+
+
+def call(body, out_shape, n_in, *, smem=(), smem_out=(), limit=32, flops=0, moved=0, after=0, far=(), far_out=False, scratch=()):
+    def timed(*refs):
+        body(*refs[:n_in], *refs[n_in + after :])
+
     many = isinstance(out_shape, (tuple, list))
-    outs = [SMEM if i in smem_out else VMEM for i in range(len(out_shape))] if many else VMEM
+    whole = pl.BlockSpec() if limit > 32 else VMEM
+    place = ANY if far_out else whole
+    outs = [SMEM if i in smem_out else place for i in range(len(out_shape))] if many else place
     return pl.pallas_call(
-        body,
+        timed,
         out_shape=out_shape,
-        in_specs=[SMEM if i in smem else VMEM for i in range(n_in)],
+        in_specs=[SMEM if i in smem else ANY if i in far else whole for i in range(n_in)] + [ANY] * after,
+        scratch_shapes=list(scratch),
         out_specs=outs,
-        compiler_params=pltpu.CompilerParams(vmem_limit_bytes=32 * 1024 * 1024),
+        compiler_params=pltpu.CompilerParams(vmem_limit_bytes=limit * 1024 * 1024),
         cost_estimate=pl.CostEstimate(flops=flops, bytes_accessed=moved, transcendentals=0),
     )
 
@@ -125,7 +132,8 @@
         rest[t] = far
 
 
-def turn_body(w_in, w_out, in_turned, out_turned):
+def turn_body(w_in, w_out, in_turned, out_turned, ready):
+    ready[...] = jnp.zeros_like(ready)
     for d in range(DP):
         cut = [(t * DP + d) * FEATS for t in range(T)]
         block = jnp.concatenate([w_in[c : c + FEATS, :] for c in cut], axis=0)
@@ -138,17 +146,51 @@
             out_turned[d, t * FEATS : (t + 1) * FEATS, :] = turned[half * FEATS : (half + 1) * FEATS]
 
 
-def expert_body(me, x0, x1, x2, x3, w_in, w_out, p0, p1, p2, p3):
+def turn_near_body(me, w_in, w_out, in_turned, out_turned, ready):
+    ready[...] = jnp.zeros_like(ready)
+    span = DP * FEATS
+    for t in range(T):
+        for k in range(DP):
+            at = pl.multiple_of((t * DP + lax.rem(me[0] - k + DP, DP)) * FEATS, FEATS)
+            to = t * span + k * FEATS
+            out_turned[to : to + FEATS, :] = w_in[pl.ds(at, FEATS), :]
+    ordered = out_turned[...]
+    in_turned[...] = ordered.T
+    for t in range(T):
+        block = w_out[:, t * span : (t + 1) * span].T
+        for k in range(DP):
+            to = pl.multiple_of(t * span + lax.rem(k - me[0] + DP, DP) * FEATS, FEATS)
+            out_turned[pl.ds(to, FEATS), :] = block[k * FEATS : (k + 1) * FEATS]
+
+
+def expert_body(me, x0, x1, x2, x3, w_in, w_out, p0, p1, p2, p3, xs, ins, outs, ps, sems):
     d = me[0]
-    hidden = None
+    near = []
     for k, x in enumerate((x0, x1, x2, x3)):
         source = lax.rem(d - k + DP, DP)
-        term = nn(w_in[source], x[...])
+        near.append(pltpu.make_async_copy(w_in.at[source], ins.at[k], sems.at[k]))
+        near.append(pltpu.make_async_copy(x, xs.at[k], sems.at[DP + k]))
+    far = {}
+    for k in (2, 1, 3, 0):
+        goal = lax.rem(d + k, DP)
+        far[k] = pltpu.make_async_copy(w_out.at[goal], outs.at[k], sems.at[2 * DP + k])
+    for copy in near + list(far.values()):
+        copy.start()
+    hidden = None
+    for k in range(DP):
+        near[2 * k].wait()
+        near[2 * k + 1].wait()
+        term = nn(ins[k], xs[k])
         hidden = term if hidden is None else hidden + term
     hidden = jnp.maximum(hidden, 0.0).astype(BF)
-    for k, p in enumerate((p0, p1, p2, p3)):
-        goal = lax.rem(d + k, DP)
-        p[...] = nn(w_out[goal], hidden).astype(BF)
+    gone = []
+    for k in (2, 1, 3, 0):
+        far[k].wait()
+        ps[k] = nn(outs[k], hidden).astype(BF)
+        gone.append(pltpu.make_async_copy(ps.at[k], (p0, p1, p2, p3)[k], sems.at[3 * DP + k]))
+        gone[-1].start()
+    for copy in gone:
+        copy.wait()
 
 
 def add_body(a, b, c, d, out):
@@ -201,16 +243,30 @@
     rows = blocks[0].shape[1]
     part = shape((T * FEATS, rows))
     work = 4 * rows * UNITS * T * DP * FEATS
-    return call(expert_body, [part] * 4, 7, smem=(0,), flops=work, moved=6 << 20)(me, *blocks, *turned)
+    held = pltpu.VMEM((DP, T * FEATS, rows), BF)
+    return call(
+        expert_body,
+        [part] * 4,
+        7,
+        smem=(0,),
+        far=range(1, 7),
+        far_out=True,
+        scratch=[held, *(pltpu.VMEM(w.shape, BF) for w in turned), held, pltpu.SemaphoreType.DMA((4 * DP,))],
+        limit=60,
+        flops=work,
+        moved=6 << 20,
+    )(me, *blocks, *turned)
 
 
 def arrive(parts):
     return [parts[0]] + [shift(parts[k], k) for k in (1, 2, 3)]
 
 
-def settle(parts):
+def settle(parts, later=()):
     rows = parts[0].shape[1]
-    added = call(add_body, shape((T * FEATS, rows)), 4, moved=5 << 19)(*parts)
+    added = call(
+        add_body, shape((T * FEATS, rows)), 4, moved=5 << 19, after=len(later)
+    )(*parts, *later)
     return over_tensor(added.reshape(T, FEATS, rows))
 
 
@@ -229,18 +285,33 @@
             out[t, k] = ref[...]
 
 
-def crossed_body(me, x, w_in, w_out, part):
-    d = me[0]
-    rows = x.shape[3]
+def crossed_body(x, w_in, w_out, part, xs, ins, outs, ps, sems):
+    span = T * FEATS
+    first = pltpu.make_async_copy(w_in, ins, sems.at[0])
+    near = []
+    far = []
+    for k in range(DP):
+        cut = pl.ds(k * span, span)
+        near.append(pltpu.make_async_copy(x.at[cut], xs.at[cut], sems.at[1 + k]))
+        far.append(pltpu.make_async_copy(w_out.at[cut], outs.at[cut], sems.at[1 + DP + k]))
+    for copy in [first] + near + far:
+        copy.start()
+    first.wait()
     hidden = None
     for k in range(DP):
-        block = x[:, k].reshape(T * FEATS, rows)
-        term = nn(w_in[lax.rem(d - k + DP, DP)], block)
+        near[k].wait()
+        term = nn(ins[:, k * span : (k + 1) * span], xs[k * span : (k + 1) * span, :])
         hidden = term if hidden is None else hidden + term
     hidden = jnp.maximum(hidden, 0.0).astype(BF)
+    gone = []
     for k in range(DP):
-        block = nn(w_out[lax.rem(d + k, DP)], hidden).astype(BF)
-        part[:, k] = block.reshape(T, FEATS, rows)
+        far[k].wait()
+        cut = pl.ds(k * span, span)
+        ps[k * span : (k + 1) * span, :] = nn(outs[k * span : (k + 1) * span, :], hidden).astype(BF)
+        gone.append(pltpu.make_async_copy(ps.at[cut], part.at[cut], sems.at[1 + 2 * DP + k]))
+        gone[-1].start()
+    for copy in gone:
+        copy.wait()
 
 
 def crossed_sum_body(got, a, b, c, d):
@@ -251,9 +322,24 @@
         ref[...] = acc.astype(BF)
 
 
-def expert_crossed(x, turned, me):
-    work = 4 * x.shape[3] * UNITS * T * DP * FEATS
-    return call(crossed_body, shape(x.shape), 4, smem=(0,), flops=work, moved=4 << 20)(me, x, *turned)
+def expert_crossed(x, turned, later):
+    rows = x.shape[3]
+    flat = x.reshape(T * DP * FEATS, rows)
+    work = 4 * rows * UNITS * T * DP * FEATS
+    held = pltpu.VMEM(flat.shape, BF)
+    part = call(
+        crossed_body,
+        shape(flat.shape),
+        3,
+        far=range(3),
+        far_out=True,
+        scratch=[held, *(pltpu.VMEM(w.shape, BF) for w in turned), held, pltpu.SemaphoreType.DMA((1 + 3 * DP,))],
+        limit=60,
+        flops=work,
+        moved=4 << 20,
+        after=len(later),
+    )(flat, *turned, *later)
+    return part.reshape(x.shape)
 
 
 def shards(
@@ -276,16 +362,18 @@
         place_body,
         [packed, shape((2, enc.shape[1]), jnp.int32), shape((1, dec.shape[1]), jnp.int32)],
         5,
+        limit=60,
         moved=1 << 18,
     )(enc_experts.T, dec_lengths, dec_language.T, enc, dec)
     got = lax.all_to_all(sent, "expert", split_axis=0, concat_axis=0, tiled=True)
 
     def turn(w_in, w_out):
-        out = [shape((DP, UNITS, T * FEATS)), shape((DP, T * FEATS, UNITS))]
-        return call(turn_body, out, 2, moved=4 << 20)(w_in[0], w_out[0])
-
-    enc_turned = turn(enc_w_in, enc_w_out)
-    dec_turned = turn(dec_w_in, dec_w_out)
+        out = [shape((DP, UNITS, T * FEATS)), shape((DP, T * FEATS, UNITS)), shape((16, 128))]
+        return call(turn_body, out, 2, limit=60, moved=4 << 20)(w_in[0], w_out[0])
+
+    *enc_turned, enc_ready = turn(enc_w_in, enc_w_out)
+    out = [shape((UNITS, T * DP * FEATS)), shape((T * DP * FEATS, UNITS)), shape((16, 128))]
+    *near_turned, dec_ready = call(turn_near_body, out, 3, smem=(0,), limit=60, moved=4 << 20)(me, dec_w_in[0], dec_w_out[0])
     far = shape((T, FEATS, ROWS - HELD))
     enc_block, dec_block, rest_block, moved_to, most = call(
         spread_body,
@@ -293,7 +381,8 @@
         1,
         smem_out=(4,),
         moved=1 << 20,
-    )(got)
+        after=2,
+    )(got, enc_ready, dec_ready)
 
     near_x = [dec_block] + [shift(dec_block, k) for k in (1, 2, 3)]
     dec_x = call(copies_body, shape((T, DP, FEATS, HELD)), 4, moved=1 << 20)(*near_x)
@@ -301,20 +390,18 @@
     (dec_x,), (enc_t,) = tie([dec_x], [enc_t])
     enc_x = gather(enc_t)
     dec_x = over_tensor(dec_x)
-    (dec_x,), enc_x = tie([dec_x], enc_x)
-    dec_parts = expert_crossed(dec_x, dec_turned, me)
+    dec_parts = expert_crossed(dec_x, near_turned, enc_x[1:])
     enc_got = arrive(expert(enc_x, enc_turned, me))
     dec_parts = over_tensor(dec_parts)
-    (dec_parts,), (enc_got[0],) = tie([dec_parts], [enc_got[0]])
-    dec_parts = call(crossed_sum_body, [shape((FEATS, HELD))] * 4, 1, moved=1 << 20)(dec_parts)
-    dec_sums = arrive(dec_parts)
-    enc_sums = settle(enc_got)
+    dec_halves = call(crossed_sum_body, [shape((FEATS, HELD))] * 4, 1, moved=1 << 20)(dec_parts)
+    dec_sums = arrive(dec_halves)
+    enc_sums = settle(enc_got, [dec_parts])
     rest_sums = lax.cond(
         most[0] > HELD,
-        lambda b, w: through(b, w, me),
+        lambda b, w: through(b, turn(*w)[:2], me),
         lambda b, w: jnp.zeros_like(b),
         rest_block,
-        dec_turned,
+        (dec_w_in, dec_w_out),
     )
 
     packed = shape((EXPERTS, CAP, 2 * FEATS))

time: 176 us -> 173 us (0.983)
  waiting for transfers between devices: 63.6 us -> 54.7 us
  Pallas kernels: 14.2 us -> 20.2 us
  local copies, waits for them, and re-layouts: 8.7 us -> 3.43 us
  starting transfers between devices: 72.8 us -> 77.1 us
    all_to_all x4, waiting for transfers between devices: 23.1 us -> 7.91 us  [over_tensor(): lax.all_to_all(block, 'tensor', split_axis=0, concat_axis=0, tiled=True)]
    ppermute x12, waiting for transfers between devices: 34.4 us -> 41.7 us  [shift(): return lax.ppermute(value, 'dp', [(i, (i + k) % DP) for i in range(DP)])]
    unnamed x32 -> x30, local copies, waits for them, and re-layouts: 8.68 us -> 3.41 us
    pallas_call x5, Pallas kernels: 9.61 us -> 14.7 us  [the longest x1 4.31 us: expert(): call(expert_body, [part] * 4, 7, smem=(0,), far=range(1, 7), far_out=True...]
    ppermute x12, starting transfers between devices: 37.3 us -> 42.2 us  [shift(): return lax.ppermute(value, 'dp', [(i, (i + k) % DP) for i in range(DP)])]
  transfers between devices with their start and end apart: 17 -> 17, of which waited for: 12 -> 13; matrix products, arithmetic and copies ran while one was open for 0% -> 0% of each run, Pallas kernels for 3% -> 6%
where the time goes in v5:
time: 173 us; the launch traced here: 171 us
  starting transfers between devices  77.1 us (45%)
  waiting for transfers between devices  54.7 us (32%)
  Pallas kernels  20.2 us (12%)
  blocking collectives  14.1 us (8%)
  local copies, waits for them, and re-layouts  3.43 us (2%)
    ppermute x12, starting transfers between devices, shift(): return lax.ppermute(value, 'dp', [(i, (i + k) % DP) for i in range(DP)])  42.2 us
    ppermute x12, waiting for transfers between devices, shift(): return lax.ppermute(value, 'dp', [(i, (i + k) % DP) for i in range(DP)])  41.7 us
    all_to_all x4, starting transfers between devices, over_tensor(): lax.all_to_all(block, 'tensor', split_axis=0, concat_axis=0, tiled=True)  24.7 us
    all_to_all x1, blocking collectives, shards(): lax.all_to_all(back, 'expert', split_axis=0, concat_axis=0, tiled=True)  14.1 us
    all_to_all x1, starting transfers between devices, shards(): lax.all_to_all(sent, 'expert', split_axis=0, concat_axis=0, tiled=True)  10.2 us
    all_to_all x4, waiting for transfers between devices, over_tensor(): lax.all_to_all(block, 'tensor', split_axis=0, concat_axis=0, tiled=True)  7.91 us
    all_to_all x1, waiting for transfers between devices, shards(): lax.all_to_all(sent, 'expert', split_axis=0, concat_axis=0, tiled=True)  5.09 us
    pallas_call x1, Pallas kernels, expert(): call(expert_body, [part] * 4, 7, smem=(0,), far=range(1, 7), far_out=True...  4.31 us
  transfers between devices with their start and end apart: 17, of which 13 were waited for; matrix products, arithmetic and copies ran while one was open for 0% of the time, Pallas kernels for 6%

profile of v5, /device:TPU:1, one launch (start us, length us, event | category | flops | bytes accessed | tf_op | source)
XLA Modules:
  0.0 171.0 jit_solution(5724801277020163701)
XLA Ops:
  2.6 10.2 %all-to-all-start.2 = ((bf16[16,48,128]{2,1,0:T(8,128)(2,1)}), bf16[16,48,128]{2,1,0:T(8,128)(2,1)S(1)}, u32[]{:S(2)}, u32[]{:S(2)}) async-start(bf16[16,48,128]{2,1,0:T(8,128)(2,1)} %get-tuple-element.49), calls=%async_computation.2 | async-start | bytes 393216 | tf_op jit(solution)/shard_map/all_to_all | solution.py:368
  12.8 3.4 %shard_map.114 = (bf16[4,256,512]{2,1,0:T(8,128)(2,1)}, bf16[4,512,256]{2,1,0:T(8,128)(2,1)}, bf16[16,128]{1,0:T(8,128)(2,1)}) custom-call(bf16[2048,256]{1,0:T(8,128)(2,1)} %bitcast.37, bf16[256,2048]{1,0:T(8,128)(2,1)} %bitcast.38), custom_call_target="tpu_custom_call" | custom-call | bytes 4194304 | tf_op jit(solution)/shard_map/pallas_call | solution.py:372
  18.1 5.1 %all-to-all-done.2.refs_0_ = bf16[16,48,128]{2,1,0:T(8,128)(2,1)S(1)} async-done(((bf16[16,48,128]{2,1,0:T(8,128)(2,1)}), bf16[16,48,128]{2,1,0:T(8,128)(2,1)S(1)}, u32[]{:S(2)}, u32[]{:S(2)}) %all-to-all-start.2) | async-done | bytes 196640 | tf_op jit(solution)/shard_map/all_to_all | solution.py:368
  25.6 8.4 %all-to-all-start.3 = ((bf16[8,64,512]{2,1,0:T(8,128)(2,1)}), bf16[8,64,512]{2,1,0:T(8,128)(2,1)S(1)}, u32[]{:S(2)}, u32[]{:S(2)}) async-start(bf16[8,64,512]{2,1,0:T(8,128)(2,1)} %get-tuple-element.53), calls=%async_computation.3 | async-start | bytes 1048576 | tf_op jit(solution)/shard_map/all_to_all | solution.py:234
  34.0 3.1 %collective-permute-start.6 = (bf16[64,256]{1,0:T(8,128)(2,1)S(1)}, bf16[64,256]{1,0:T(8,128)(2,1)S(1)}, u32[]{:S(2)}, u32[]{:S(2)}) collective-permute-start(bf16[64,256]{1,0:T(8,128)(2,1)S(1)} %get-tuple-element.52.refs_0_), channel_id=1, source_target_pairs={{0,1},{1,2},{2,3},{3,0},{4,5},{5,6},{6,7},{7,4},{8,9},{9,10},{10,1... | collective-permute-start | bytes 98312 | tf_op jit(solution)/shard_map/ppermute | solution.py:230
  37.1 4.4 %collective-permute-start.7 = (bf16[64,256]{1,0:T(8,128)(2,1)S(1)}, bf16[64,256]{1,0:T(8,128)(2,1)S(1)}, u32[]{:S(2)}, u32[]{:S(2)}) collective-permute-start(bf16[64,256]{1,0:T(8,128)(2,1)S(1)} %get-tuple-element.52.refs_0_), channel_id=1, source_target_pairs={{0,2},{1,3},{2,0},{3,1},{4,6},{5,7},{6,4},{7,5},{8,10},{9,11},{10,... | collective-permute-start | bytes 98312 | tf_op jit(solution)/shard_map/ppermute | solution.py:230
  41.5 3.1 %collective-permute-start.8 = (bf16[64,256]{1,0:T(8,128)(2,1)S(1)}, bf16[64,256]{1,0:T(8,128)(2,1)S(1)}, u32[]{:S(2)}, u32[]{:S(2)}) collective-permute-start(bf16[64,256]{1,0:T(8,128)(2,1)S(1)} %get-tuple-element.52.refs_0_), channel_id=1, source_target_pairs={{0,3},{1,0},{2,1},{3,2},{4,7},{5,4},{6,5},{7,6},{8,11},{9,8},{10,9... | collective-permute-start | bytes 98312 | tf_op jit(solution)/shard_map/ppermute | solution.py:230
  47.5 4.6 %all-to-all-done.3 = bf16[8,64,512]{2,1,0:T(8,128)(2,1)S(1)} async-done(((bf16[8,64,512]{2,1,0:T(8,128)(2,1)}), bf16[8,64,512]{2,1,0:T(8,128)(2,1)S(1)}, u32[]{:S(2)}, u32[]{:S(2)}) %all-to-all-start.3) | async-done | bytes 524320 | tf_op jit(solution)/shard_map/all_to_all | solution.py:234
  52.1 3.6 %all-to-all-start.4 = ((bf16[8,4,64,256]{3,2,1,0:T(8,128)(2,1)}), bf16[8,4,64,256]{3,2,1,0:T(8,128)(2,1)S(1)}, u32[]{:S(2)}, u32[]{:S(2)}) async-start(bf16[8,4,64,256]{3,2,1,0:T(8,128)(2,1)} %shard_map.117), calls=%async_computation.4 | async-start | bytes 2097152 | tf_op jit(solution)/shard_map/all_to_all | solution.py:234
  55.7 4.7 %collective-permute-start.10 = (bf16[512,512]{1,0:T(8,128)(2,1)S(1)}, bf16[512,512]{1,0:T(8,128)(2,1)S(1)}, u32[]{:S(2)}, u32[]{:S(2)}) collective-permute-start(bf16[512,512]{1,0:T(8,128)(2,1)S(1)} %bitcast.33), channel_id=1, source_target_pairs={{0,2},{1,3},{2,0},{3,1},{4,6},{5,7},{6,4},{7,5},{8,10},{9,11},{10,... | collective-permute-start | bytes 1572872 | tf_op jit(solution)/shard_map/ppermute | solution.py:230
  65.6 6.5 %collective-permute-done.10.refs_3_.refs_4_ = bf16[512,512]{1,0:T(8,128)(2,1)S(1)} collective-permute-done((bf16[512,512]{1,0:T(8,128)(2,1)S(1)}, bf16[512,512]{1,0:T(8,128)(2,1)S(1)}, u32[]{:S(2)}, u32[]{:S(2)}) %collective-permute-start.10) | collective-permute-done | bytes 524320 | tf_op jit(solution)/shard_map/ppermute | solution.py:230
  72.1 11.4 %collective-permute-done.11.refs_4_.refs_5_ = bf16[512,512]{1,0:T(8,128)(2,1)S(1)} collective-permute-done((bf16[512,512]{1,0:T(8,128)(2,1)S(1)}, bf16[512,512]{1,0:T(8,128)(2,1)S(1)}, u32[]{:S(2)}, u32[]{:S(2)}) %collective-permute-start.11) | collective-permute-done | bytes 524320 | tf_op jit(solution)/shard_map/ppermute | solution.py:230
  85.8 4.1 %shard_map.119 = bf16[2048,256]{1,0:T(8,128)(2,1)} custom-call(bf16[2048,256]{1,0:T(8,128)(2,1)} %bitcast.32, bf16[256,2048]{1,0:T(8,128)(2,1)} %get-tuple-element.62.refs_1_, bf16[2048,256]{1,0:T(8,128)(2,1)} %get-tuple-element.63.refs_2_, bf16[512,512]{1,0:T(8,128)(2,1)} %copy-done.15, bf16[512,512]{1,0:T(8,128)(2,1)} %copy-done.13, ...), custom_call_target="tpu_custom_call" | custom-call | flops 536870912 | bytes 4194304 | tf_op jit(solution)/shard_map/pallas_call | solution.py:330
  89.9 6.1 %all-to-all-start.5 = ((bf16[8,4,64,256]{3,2,1,0:T(8,128)(2,1)}), bf16[8,4,64,256]{3,2,1,0:T(8,128)(2,1)S(1)}, u32[]{:S(2)}, u32[]{:S(2)}) async-start(bf16[8,4,64,256]{3,2,1,0:T(8,128)(2,1)} %bitcast.31), calls=%async_computation.5 | async-start | bytes 2097152 | tf_op jit(solution)/shard_map/all_to_all | solution.py:234
  95.9 4.3 %shard_map.118 = (bf16[512,512]{1,0:T(8,128)(2,1)}, bf16[512,512]{1,0:T(8,128)(2,1)}, bf16[512,512]{1,0:T(8,128)(2,1)}, bf16[512,512]{1,0:T(8,128)(2,1)}) custom-call(s32[1]{0:T(128)} %bitcast.4.refs_0_, bf16[512,512]{1,0:T(8,128)(2,1)} %bitcast.36, bf16[512,512]{1,0:T(8,128)(2,1)} %copy-done.15, bf16[512,512]{1,0:T(8,128)(2,1)} %copy-done.13, ...), custom_call_target="tpu_custom_call" | custom-call | flops 1073741824 | bytes 6291456 | tf_op jit(solution)/shard_map/pallas_call | solution.py:247
  100.2 3.3 %collective-permute-start.12 = (bf16[512,512]{1,0:T(8,128)(2,1)}, bf16[512,512]{1,0:T(8,128)(2,1)S(1)}, u32[]{:S(2)}, u32[]{:S(2)}) collective-permute-start(bf16[512,512]{1,0:T(8,128)(2,1)} %get-tuple-element.58), channel_id=1, source_target_pairs={{0,1},{1,2},{2,3},{3,0},{4,5},{5,6},{6,7},{7,4},{8,9},{9,10},{10,1... | collective-permute-start | bytes 1572872 | tf_op jit(solution)/shard_map/ppermute | solution.py:230
  103.5 4.3 %collective-permute-start.13 = (bf16[512,512]{1,0:T(8,128)(2,1)}, bf16[512,512]{1,0:T(8,128)(2,1)S(1)}, u32[]{:S(2)}, u32[]{:S(2)}) collective-permute-start(bf16[512,512]{1,0:T(8,128)(2,1)} %get-tuple-element.59), channel_id=1, source_target_pairs={{0,2},{1,3},{2,0},{3,1},{4,6},{5,7},{6,4},{7,5},{8,10},{9,11},{10,... | collective-permute-start | bytes 1572872 | tf_op jit(solution)/shard_map/ppermute | solution.py:230
  107.9 2.9 %collective-permute-start.14 = (bf16[512,512]{1,0:T(8,128)(2,1)}, bf16[512,512]{1,0:T(8,128)(2,1)S(1)}, u32[]{:S(2)}, u32[]{:S(2)}) collective-permute-start(bf16[512,512]{1,0:T(8,128)(2,1)} %get-tuple-element.60), channel_id=1, source_target_pairs={{0,3},{1,0},{2,1},{3,2},{4,7},{5,4},{6,5},{7,6},{8,11},{9,8},{10,9... | collective-permute-start | bytes 1572872 | tf_op jit(solution)/shard_map/ppermute | solution.py:230
  110.8 5.1 %collective-permute-done.12.refs_1_ = bf16[512,512]{1,0:T(8,128)(2,1)S(1)} collective-permute-done((bf16[512,512]{1,0:T(8,128)(2,1)}, bf16[512,512]{1,0:T(8,128)(2,1)S(1)}, u32[]{:S(2)}, u32[]{:S(2)}) %collective-permute-start.12) | collective-permute-done | bytes 524320 | tf_op jit(solution)/shard_map/ppermute | solution.py:230
  115.9 12.7 %collective-permute-done.13.refs_2_ = bf16[512,512]{1,0:T(8,128)(2,1)S(1)} collective-permute-done((bf16[512,512]{1,0:T(8,128)(2,1)}, bf16[512,512]{1,0:T(8,128)(2,1)S(1)}, u32[]{:S(2)}, u32[]{:S(2)}) %collective-permute-start.13) | collective-permute-done | bytes 524320 | tf_op jit(solution)/shard_map/ppermute | solution.py:230
  132.3 6.6 %all-to-all-start.6 = ((bf16[8,64,512]{2,1,0:T(8,128)(2,1)}), bf16[8,64,512]{2,1,0:T(8,128)(2,1)S(1)}, u32[]{:S(2)}, u32[]{:S(2)}) async-start(bf16[8,64,512]{2,1,0:T(8,128)(2,1)} %bitcast.16), calls=%async_computation.6 | async-start | bytes 1048576 | tf_op jit(solution)/shard_map/all_to_all | solution.py:234
  139.1 5.0 %collective-permute-start.15 = (bf16[64,256]{1,0:T(8,128)(2,1)S(1)}, bf16[64,256]{1,0:T(8,128)(2,1)S(1)}, u32[]{:S(2)}, u32[]{:S(2)}) collective-permute-start(bf16[64,256]{1,0:T(8,128)(2,1)S(1)} %get-tuple-element.65), channel_id=1, source_target_pairs={{0,1},{1,2},{2,3},{3,0},{4,5},{5,6},{6,7},{7,4},{8,9},{9,10},{10,1... | collective-permute-start | bytes 98312 | tf_op jit(solution)/shard_map/ppermute | solution.py:230
  144.1 3.3 %collective-permute-start.16 = (bf16[64,256]{1,0:T(8,128)(2,1)S(1)}, bf16[64,256]{1,0:T(8,128)(2,1)S(1)}, u32[]{:S(2)}, u32[]{:S(2)}) collective-permute-start(bf16[64,256]{1,0:T(8,128)(2,1)S(1)} %get-tuple-element.66), channel_id=1, source_target_pairs={{0,2},{1,3},{2,0},{3,1},{4,6},{5,7},{6,4},{7,5},{8,10},{9,11},{10,... | collective-permute-start | bytes 98312 | tf_op jit(solution)/shard_map/ppermute | solution.py:230
  155.3 14.1 %all_to_all.40.refs_0_ = bf16[16,32,128]{2,1,0:T(8,128)(2,1)S(1)} all-to-all(bf16[16,32,128]{2,1,0:T(8,128)(2,1)S(1)} %shard_map.122), channel_id=1, replica_groups=mesh['expert'=16,'tensor'=8,'dp'=4] {'expert'}, dimensions={0} | all-to-all | bytes 262144 | tf_op jit(solution)/shard_map/all_to_all | solution.py:409
  (54 shorter events, 29.5 us)
Async XLA Ops:
  2.6 20.6 %all-to-all-start.2 = ((bf16[16,48,128]{2,1,0:T(8,128)(2,1)}), bf16[16,48,128]{2,1,0:T(8,128)(2,1)S(1)}, u32[]{:S(2)}, u32[]{:S(2)}) async-start(bf16[16,48,128]{2,1,0:T(8,128)(2,1)} %get-tuple-element.49), calls=%async_computation.2 | async-start | bytes 393216 | tf_op jit(solution)/shard_map/all_to_all | solution.py:368
  16.2 7.0 %copy-start.4 = (bf16[16,128]{1,0:T(8,128)(2,1)S(1)}, bf16[16,128]{1,0:T(8,128)(2,1)}, u32[]{:S(2)}) copy-start(bf16[16,128]{1,0:T(8,128)(2,1)} %get-tuple-element.50.refs_1_) | copy-start | bytes 12292
  25.6 26.5 %all-to-all-start.3 = ((bf16[8,64,512]{2,1,0:T(8,128)(2,1)}), bf16[8,64,512]{2,1,0:T(8,128)(2,1)S(1)}, u32[]{:S(2)}, u32[]{:S(2)}) async-start(bf16[8,64,512]{2,1,0:T(8,128)(2,1)} %get-tuple-element.53), calls=%async_computation.3 | async-start | bytes 1048576 | tf_op jit(solution)/shard_map/all_to_all | solution.py:234
  34.0 10.6 %collective-permute-start.6 = (bf16[64,256]{1,0:T(8,128)(2,1)S(1)}, bf16[64,256]{1,0:T(8,128)(2,1)S(1)}, u32[]{:S(2)}, u32[]{:S(2)}) collective-permute-start(bf16[64,256]{1,0:T(8,128)(2,1)S(1)} %get-tuple-element.52.refs_0_), channel_id=1, source_target_pairs={{0,1},{1,2},{2,3},{3,0},{4,5},{5,6},{6,7},{7,4},{8,9},{9,10},{10,1... | collective-permute-start | bytes 98312 | tf_op jit(solution)/shard_map/ppermute | solution.py:230
  37.1 7.4 %collective-permute-start.7 = (bf16[64,256]{1,0:T(8,128)(2,1)S(1)}, bf16[64,256]{1,0:T(8,128)(2,1)S(1)}, u32[]{:S(2)}, u32[]{:S(2)}) collective-permute-start(bf16[64,256]{1,0:T(8,128)(2,1)S(1)} %get-tuple-element.52.refs_0_), channel_id=1, source_target_pairs={{0,2},{1,3},{2,0},{3,1},{4,6},{5,7},{6,4},{7,5},{8,10},{9,11},{10,... | collective-permute-start | bytes 98312 | tf_op jit(solution)/shard_map/ppermute | solution.py:230
  41.5 5.0 %collective-permute-start.8 = (bf16[64,256]{1,0:T(8,128)(2,1)S(1)}, bf16[64,256]{1,0:T(8,128)(2,1)S(1)}, u32[]{:S(2)}, u32[]{:S(2)}) collective-permute-start(bf16[64,256]{1,0:T(8,128)(2,1)S(1)} %get-tuple-element.52.refs_0_), channel_id=1, source_target_pairs={{0,3},{1,0},{2,1},{3,2},{4,7},{5,4},{6,5},{7,6},{8,11},{9,8},{10,9... | collective-permute-start | bytes 98312 | tf_op jit(solution)/shard_map/ppermute | solution.py:230
  52.1 11.0 %copy-start.12 = (bf16[8,64,512]{2,1,0:T(8,128)(2,1)}, bf16[8,64,512]{2,1,0:T(8,128)(2,1)S(1)}, u32[]{:S(2)}) copy-start(bf16[8,64,512]{2,1,0:T(8,128)(2,1)S(1)} %all-to-all-done.3) | copy-start | bytes 1572868
  52.1 32.7 %all-to-all-start.4 = ((bf16[8,4,64,256]{3,2,1,0:T(8,128)(2,1)}), bf16[8,4,64,256]{3,2,1,0:T(8,128)(2,1)S(1)}, u32[]{:S(2)}, u32[]{:S(2)}) async-start(bf16[8,4,64,256]{3,2,1,0:T(8,128)(2,1)} %shard_map.117), calls=%async_computation.4 | async-start | bytes 2097152 | tf_op jit(solution)/shard_map/all_to_all | solution.py:234
  55.7 16.4 %collective-permute-start.10 = (bf16[512,512]{1,0:T(8,128)(2,1)S(1)}, bf16[512,512]{1,0:T(8,128)(2,1)S(1)}, u32[]{:S(2)}, u32[]{:S(2)}) collective-permute-start(bf16[512,512]{1,0:T(8,128)(2,1)S(1)} %bitcast.33), channel_id=1, source_target_pairs={{0,2},{1,3},{2,0},{3,1},{4,6},{5,7},{6,4},{7,5},{8,10},{9,11},{10,... | collective-permute-start | bytes 1572872 | tf_op jit(solution)/shard_map/ppermute | solution.py:230
  60.3 23.2 %collective-permute-start.11 = (bf16[512,512]{1,0:T(8,128)(2,1)S(1)}, bf16[512,512]{1,0:T(8,128)(2,1)S(1)}, u32[]{:S(2)}, u32[]{:S(2)}) collective-permute-start(bf16[512,512]{1,0:T(8,128)(2,1)S(1)} %bitcast.34), channel_id=1, source_target_pairs={{0,3},{1,0},{2,1},{3,2},{4,7},{5,4},{6,5},{7,6},{8,11},{9,8},{10,9... | collective-permute-start | bytes 1572872 | tf_op jit(solution)/shard_map/ppermute | solution.py:230
  63.1 21.0 %collective-permute-start.9 = (bf16[512,512]{1,0:T(8,128)(2,1)S(1)}, bf16[512,512]{1,0:T(8,128)(2,1)S(1)}, u32[]{:S(2)}, u32[]{:S(2)}) collective-permute-start(bf16[512,512]{1,0:T(8,128)(2,1)S(1)} %bitcast.35), channel_id=1, source_target_pairs={{0,1},{1,2},{2,3},{3,0},{4,5},{5,6},{6,7},{7,4},{8,9},{9,10},{10,1... | collective-permute-start | bytes 1572872 | tf_op jit(solution)/shard_map/ppermute | solution.py:230
  72.1 12.7 %copy-start.13 = (bf16[512,512]{1,0:T(8,128)(2,1)}, bf16[512,512]{1,0:T(8,128)(2,1)S(1)}, u32[]{:S(2)}) copy-start(bf16[512,512]{1,0:T(8,128)(2,1)S(1)} %collective-permute-done.10.refs_3_.refs_4_) | copy-start | bytes 1572868
  89.9 40.4 %all-to-all-start.5 = ((bf16[8,4,64,256]{3,2,1,0:T(8,128)(2,1)}), bf16[8,4,64,256]{3,2,1,0:T(8,128)(2,1)S(1)}, u32[]{:S(2)}, u32[]{:S(2)}) async-start(bf16[8,4,64,256]{3,2,1,0:T(8,128)(2,1)} %bitcast.31), calls=%async_computation.5 | async-start | bytes 2097152 | tf_op jit(solution)/shard_map/all_to_all | solution.py:234
  100.2 15.7 %collective-permute-start.12 = (bf16[512,512]{1,0:T(8,128)(2,1)}, bf16[512,512]{1,0:T(8,128)(2,1)S(1)}, u32[]{:S(2)}, u32[]{:S(2)}) collective-permute-start(bf16[512,512]{1,0:T(8,128)(2,1)} %get-tuple-element.58), channel_id=1, source_target_pairs={{0,1},{1,2},{2,3},{3,0},{4,5},{5,6},{6,7},{7,4},{8,9},{9,10},{10,1... | collective-permute-start | bytes 1572872 | tf_op jit(solution)/shard_map/ppermute | solution.py:230
  103.5 25.0 %collective-permute-start.13 = (bf16[512,512]{1,0:T(8,128)(2,1)}, bf16[512,512]{1,0:T(8,128)(2,1)S(1)}, u32[]{:S(2)}, u32[]{:S(2)}) collective-permute-start(bf16[512,512]{1,0:T(8,128)(2,1)} %get-tuple-element.59), channel_id=1, source_target_pairs={{0,2},{1,3},{2,0},{3,1},{4,6},{5,7},{6,4},{7,5},{8,10},{9,11},{10,... | collective-permute-start | bytes 1572872 | tf_op jit(solution)/shard_map/ppermute | solution.py:230
  107.9 22.3 %collective-permute-start.14 = (bf16[512,512]{1,0:T(8,128)(2,1)}, bf16[512,512]{1,0:T(8,128)(2,1)S(1)}, u32[]{:S(2)}, u32[]{:S(2)}) collective-permute-start(bf16[512,512]{1,0:T(8,128)(2,1)} %get-tuple-element.60), channel_id=1, source_target_pairs={{0,3},{1,0},{2,1},{3,2},{4,7},{5,4},{6,5},{7,6},{8,11},{9,8},{10,9... | collective-permute-start | bytes 1572872 | tf_op jit(solution)/shard_map/ppermute | solution.py:230
  132.3 22.6 %all-to-all-start.6 = ((bf16[8,64,512]{2,1,0:T(8,128)(2,1)}), bf16[8,64,512]{2,1,0:T(8,128)(2,1)S(1)}, u32[]{:S(2)}, u32[]{:S(2)}) async-start(bf16[8,64,512]{2,1,0:T(8,128)(2,1)} %bitcast.16), calls=%async_computation.6 | async-start | bytes 1048576 | tf_op jit(solution)/shard_map/all_to_all | solution.py:234
  139.1 11.2 %collective-permute-start.15 = (bf16[64,256]{1,0:T(8,128)(2,1)S(1)}, bf16[64,256]{1,0:T(8,128)(2,1)S(1)}, u32[]{:S(2)}, u32[]{:S(2)}) collective-permute-start(bf16[64,256]{1,0:T(8,128)(2,1)S(1)} %get-tuple-element.65), channel_id=1, source_target_pairs={{0,1},{1,2},{2,3},{3,0},{4,5},{5,6},{6,7},{7,4},{8,9},{9,10},{10,1... | collective-permute-start | bytes 98312 | tf_op jit(solution)/shard_map/ppermute | solution.py:230
  144.1 6.5 %collective-permute-start.16 = (bf16[64,256]{1,0:T(8,128)(2,1)S(1)}, bf16[64,256]{1,0:T(8,128)(2,1)S(1)}, u32[]{:S(2)}, u32[]{:S(2)}) collective-permute-start(bf16[64,256]{1,0:T(8,128)(2,1)S(1)} %get-tuple-element.66), channel_id=1, source_target_pairs={{0,2},{1,3},{2,0},{3,1},{4,6},{5,7},{6,4},{7,5},{8,10},{9,11},{10,... | collective-permute-start | bytes 98312 | tf_op jit(solution)/shard_map/ppermute | solution.py:230
  147.4 4.8 %collective-permute-start.17 = (bf16[64,256]{1,0:T(8,128)(2,1)S(1)}, bf16[64,256]{1,0:T(8,128)(2,1)S(1)}, u32[]{:S(2)}, u32[]{:S(2)}) collective-permute-start(bf16[64,256]{1,0:T(8,128)(2,1)S(1)} %get-tuple-element.67), channel_id=1, source_target_pairs={{0,3},{1,0},{2,1},{3,2},{4,7},{5,4},{6,5},{7,6},{8,11},{9,8},{10,9... | collective-permute-start | bytes 98312 | tf_op jit(solution)/shard_map/ppermute | solution.py:230
  154.9 14.5 %copy-start.3 = (bf16[128,64]{0,1:T(8,128)(2,1)S(1)}, bf16[128,64]{0,1:T(8,128)(2,1)}, u32[]{:S(2)}) copy-start(bf16[128,64]{0,1:T(8,128)(2,1)} %param.12) | copy-start | bytes 49156
  154.9 14.5 %copy-start.7 = (s32[2,128]{1,0:T(2,128)S(1)}, s32[2,128]{1,0:T(2,128)}, u32[]{:S(2)}) copy-start(s32[2,128]{1,0:T(2,128)} %get-tuple-element.71.refs_1_) | copy-start | bytes 3076
  154.9 14.5 %copy-start.8 = (s32[1,144]{1,0:T(1,128)S(1)}, s32[1,144]{1,0:T(1,128)}, u32[]{:S(2)}) copy-start(s32[1,144]{1,0:T(1,128)} %get-tuple-element.72.refs_2_) | copy-start | bytes 1732
  155.2 14.1 %copy-start.2 = (bf16[144,64]{0,1:T(8,128)(2,1)S(1)}, bf16[144,64]{0,1:T(8,128)(2,1)}, u32[]{:S(2)}) copy-start(bf16[144,64]{0,1:T(8,128)(2,1)} %param.17) | copy-start | bytes 55300
  (8 other events, 12.3 us)

commit v6 on v5

--- a/solution.py
+++ b/solution.py
@@ -381,11 +381,12 @@
         1,
         smem_out=(4,),
         moved=1 << 20,
-        after=2,
-    )(got, enc_ready, dec_ready)
+    )(got)
 
     near_x = [dec_block] + [shift(dec_block, k) for k in (1, 2, 3)]
-    dec_x = call(copies_body, shape((T, DP, FEATS, HELD)), 4, moved=1 << 20)(*near_x)
+    dec_x = call(copies_body, shape((T, DP, FEATS, HELD)), 4, moved=1 << 20, after=2)(
+        *near_x, enc_ready, dec_ready
+    )
     enc_t = over_tensor(enc_block)
     (dec_x,), (enc_t,) = tie([dec_x], [enc_t])
     enc_x = gather(enc_t)

time: 173 us -> 177 us (1.023)
  waiting for transfers between devices: 54.7 us -> 61.9 us
  starting transfers between devices: 77.1 us -> 74.5 us
    ppermute x12, waiting for transfers between devices: 41.7 us -> 47.2 us  [shift(): return lax.ppermute(value, 'dp', [(i, (i + k) % DP) for i in range(DP)])]
    all_to_all x1, waiting for transfers between devices: 5.09 us -> 10.4 us  [shards(): lax.all_to_all(sent, 'expert', split_axis=0, concat_axis=0, tiled=True)]
    ppermute x12, starting transfers between devices: 42.2 us -> 37.6 us  [shift(): return lax.ppermute(value, 'dp', [(i, (i + k) % DP) for i in range(DP)])]
    all_to_all x4, waiting for transfers between devices: 7.91 us -> 4.36 us  [over_tensor(): lax.all_to_all(block, 'tensor', split_axis=0, concat_axis=0, tiled=True)]
    all_to_all x4, starting transfers between devices: 24.7 us -> 26.7 us  [over_tensor(): lax.all_to_all(block, 'tensor', split_axis=0, concat_axis=0, tiled=True)]
  transfers between devices with their start and end apart: 17 -> 17, of which waited for: 13 -> 9; matrix products, arithmetic and copies ran while one was open for 0% -> 0% of each run, Pallas kernels for 6% -> 6%
where the time goes in v6:
time: 177 us; the launch traced here: 176 us
  starting transfers between devices  74.5 us (42%)
  waiting for transfers between devices  61.9 us (35%)
  Pallas kernels  20.1 us (11%)
  blocking collectives  14.1 us (8%)
  local copies, waits for them, and re-layouts  3.58 us (2%)
    ppermute x12, waiting for transfers between devices, shift(): return lax.ppermute(value, 'dp', [(i, (i + k) % DP) for i in range(DP)])  47.2 us
    ppermute x12, starting transfers between devices, shift(): return lax.ppermute(value, 'dp', [(i, (i + k) % DP) for i in range(DP)])  37.6 us
    all_to_all x4, starting transfers between devices, over_tensor(): lax.all_to_all(block, 'tensor', split_axis=0, concat_axis=0, tiled=True)  26.7 us
    all_to_all x1, blocking collectives, shards(): lax.all_to_all(back, 'expert', split_axis=0, concat_axis=0, tiled=True)  14.1 us
    all_to_all x1, waiting for transfers between devices, shards(): lax.all_to_all(sent, 'expert', split_axis=0, concat_axis=0, tiled=True)  10.4 us
    all_to_all x1, starting transfers between devices, shards(): lax.all_to_all(sent, 'expert', split_axis=0, concat_axis=0, tiled=True)  10.2 us
    all_to_all x4, waiting for transfers between devices, over_tensor(): lax.all_to_all(block, 'tensor', split_axis=0, concat_axis=0, tiled=True)  4.36 us
    pallas_call x1, Pallas kernels, expert(): call(expert_body, [part] * 4, 7, smem=(0,), far=range(1, 7), far_out=True...  4.29 us
  transfers between devices with their start and end apart: 17, of which 9 were waited for; matrix products, arithmetic and copies ran while one was open for 0% of the time, Pallas kernels for 6%

profile of v6, /device:TPU:1, one launch (start us, length us, event | category | flops | bytes accessed | tf_op | source)
XLA Modules:
  0.0 175.8 jit_solution(12572669776800384954)
XLA Ops:
  2.6 10.2 %all-to-all-start.2 = ((bf16[16,48,128]{2,1,0:T(8,128)(2,1)}), bf16[16,48,128]{2,1,0:T(8,128)(2,1)S(1)}, u32[]{:S(2)}, u32[]{:S(2)}) async-start(bf16[16,48,128]{2,1,0:T(8,128)(2,1)} %get-tuple-element.49), calls=%async_computation.2 | async-start | bytes 393216 | tf_op jit(solution)/shard_map/all_to_all | solution.py:368
  12.8 10.4 %all-to-all-done.2.refs_0_ = bf16[16,48,128]{2,1,0:T(8,128)(2,1)S(1)} async-done(((bf16[16,48,128]{2,1,0:T(8,128)(2,1)}), bf16[16,48,128]{2,1,0:T(8,128)(2,1)S(1)}, u32[]{:S(2)}, u32[]{:S(2)}) %all-to-all-start.2) | async-done | bytes 196640 | tf_op jit(solution)/shard_map/all_to_all | solution.py:368
  24.9 8.4 %all-to-all-start.3 = ((bf16[8,64,512]{2,1,0:T(8,128)(2,1)}), bf16[8,64,512]{2,1,0:T(8,128)(2,1)S(1)}, u32[]{:S(2)}, u32[]{:S(2)}) async-start(bf16[8,64,512]{2,1,0:T(8,128)(2,1)} %get-tuple-element.53), calls=%async_computation.3 | async-start | bytes 1048576 | tf_op jit(solution)/shard_map/all_to_all | solution.py:234
  33.3 4.4 %collective-permute-start.8 = (bf16[64,256]{1,0:T(8,128)(2,1)S(1)}, bf16[64,256]{1,0:T(8,128)(2,1)S(1)}, u32[]{:S(2)}, u32[]{:S(2)}) collective-permute-start(bf16[64,256]{1,0:T(8,128)(2,1)S(1)} %get-tuple-element.50.refs_0_), channel_id=1, source_target_pairs={{0,3},{1,0},{2,1},{3,2},{4,7},{5,4},{6,5},{7,6},{8,11},{9,8},{10,9... | collective-permute-start | bytes 98312 | tf_op jit(solution)/shard_map/ppermute | solution.py:230
  42.7 3.4 %shard_map.115 = (bf16[4,256,512]{2,1,0:T(8,128)(2,1)}, bf16[4,512,256]{2,1,0:T(8,128)(2,1)}, bf16[16,128]{1,0:T(8,128)(2,1)}) custom-call(bf16[2048,256]{1,0:T(8,128)(2,1)} %bitcast.37, bf16[256,2048]{1,0:T(8,128)(2,1)} %bitcast.38), custom_call_target="tpu_custom_call" | custom-call | bytes 4194304 | tf_op jit(solution)/shard_map/pallas_call | solution.py:372
  51.4 5.0 %all-to-all-start.4 = ((bf16[8,4,64,256]{3,2,1,0:T(8,128)(2,1)}), bf16[8,4,64,256]{3,2,1,0:T(8,128)(2,1)S(1)}, u32[]{:S(2)}, u32[]{:S(2)}) async-start(bf16[8,4,64,256]{3,2,1,0:T(8,128)(2,1)} %shard_map.117), calls=%async_computation.4 | async-start | bytes 2097152 | tf_op jit(solution)/shard_map/all_to_all | solution.py:234
  56.4 4.0 %collective-permute-start.11 = (bf16[512,512]{1,0:T(8,128)(2,1)S(1)}, bf16[512,512]{1,0:T(8,128)(2,1)S(1)}, u32[]{:S(2)}, u32[]{:S(2)}) collective-permute-start(bf16[512,512]{1,0:T(8,128)(2,1)S(1)} %bitcast.33), channel_id=1, source_target_pairs={{0,3},{1,0},{2,1},{3,2},{4,7},{5,4},{6,5},{7,6},{8,11},{9,8},{10,9... | collective-permute-start | bytes 1572872 | tf_op jit(solution)/shard_map/ppermute | solution.py:230
  60.4 3.1 %collective-permute-start.10 = (bf16[512,512]{1,0:T(8,128)(2,1)S(1)}, bf16[512,512]{1,0:T(8,128)(2,1)S(1)}, u32[]{:S(2)}, u32[]{:S(2)}) collective-permute-start(bf16[512,512]{1,0:T(8,128)(2,1)S(1)} %bitcast.34), channel_id=1, source_target_pairs={{0,2},{1,3},{2,0},{3,1},{4,6},{5,7},{6,4},{7,5},{8,10},{9,11},{10,... | collective-permute-start | bytes 1572872 | tf_op jit(solution)/shard_map/ppermute | solution.py:230
  65.4 5.0 %collective-permute-done.11.refs_4_.refs_5_ = bf16[512,512]{1,0:T(8,128)(2,1)S(1)} collective-permute-done((bf16[512,512]{1,0:T(8,128)(2,1)S(1)}, bf16[512,512]{1,0:T(8,128)(2,1)S(1)}, u32[]{:S(2)}, u32[]{:S(2)}) %collective-permute-start.11) | collective-permute-done | bytes 524320 | tf_op jit(solution)/shard_map/ppermute | solution.py:230
  70.4 5.1 %collective-permute-done.10.refs_3_.refs_4_ = bf16[512,512]{1,0:T(8,128)(2,1)S(1)} collective-permute-done((bf16[512,512]{1,0:T(8,128)(2,1)S(1)}, bf16[512,512]{1,0:T(8,128)(2,1)S(1)}, u32[]{:S(2)}, u32[]{:S(2)}) %collective-permute-start.10) | collective-permute-done | bytes 524320 | tf_op jit(solution)/shard_map/ppermute | solution.py:230
  75.5 13.3 %collective-permute-done.9.refs_2_.refs_3_ = bf16[512,512]{1,0:T(8,128)(2,1)S(1)} collective-permute-done((bf16[512,512]{1,0:T(8,128)(2,1)S(1)}, bf16[512,512]{1,0:T(8,128)(2,1)S(1)}, u32[]{:S(2)}, u32[]{:S(2)}) %collective-permute-start.9) | collective-permute-done | bytes 524320 | tf_op jit(solution)/shard_map/ppermute | solution.py:230
  90.0 4.1 %shard_map.119 = bf16[2048,256]{1,0:T(8,128)(2,1)} custom-call(bf16[2048,256]{1,0:T(8,128)(2,1)} %bitcast.32, bf16[256,2048]{1,0:T(8,128)(2,1)} %get-tuple-element.62.refs_1_, bf16[2048,256]{1,0:T(8,128)(2,1)} %get-tuple-element.63.refs_2_, bf16[512,512]{1,0:T(8,128)(2,1)} %copy-done.15, bf16[512,512]{1,0:T(8,128)(2,1)} %copy-done.14, ...), custom_call_target="tpu_custom_call" | custom-call | flops 536870912 | bytes 4194304 | tf_op jit(solution)/shard_map/pallas_call | solution.py:330
  94.1 6.7 %all-to-all-start.5 = ((bf16[8,4,64,256]{3,2,1,0:T(8,128)(2,1)}), bf16[8,4,64,256]{3,2,1,0:T(8,128)(2,1)S(1)}, u32[]{:S(2)}, u32[]{:S(2)}) async-start(bf16[8,4,64,256]{3,2,1,0:T(8,128)(2,1)} %bitcast.31), calls=%async_computation.5 | async-start | bytes 2097152 | tf_op jit(solution)/shard_map/all_to_all | solution.py:234
  100.7 4.3 %shard_map.118 = (bf16[512,512]{1,0:T(8,128)(2,1)}, bf16[512,512]{1,0:T(8,128)(2,1)}, bf16[512,512]{1,0:T(8,128)(2,1)}, bf16[512,512]{1,0:T(8,128)(2,1)}) custom-call(s32[1]{0:T(128)} %bitcast.4.refs_0_, bf16[512,512]{1,0:T(8,128)(2,1)} %bitcast.36, bf16[512,512]{1,0:T(8,128)(2,1)} %copy-done.15, bf16[512,512]{1,0:T(8,128)(2,1)} %copy-done.14, ...), custom_call_target="tpu_custom_call" | custom-call | flops 1073741824 | bytes 6291456 | tf_op jit(solution)/shard_map/pallas_call | solution.py:247
  106.9 3.1 %collective-permute-start.13 = (bf16[512,512]{1,0:T(8,128)(2,1)}, bf16[512,512]{1,0:T(8,128)(2,1)S(1)}, u32[]{:S(2)}, u32[]{:S(2)}) collective-permute-start(bf16[512,512]{1,0:T(8,128)(2,1)} %get-tuple-element.59), channel_id=1, source_target_pairs={{0,2},{1,3},{2,0},{3,1},{4,6},{5,7},{6,4},{7,5},{8,10},{9,11},{10,... | collective-permute-start | bytes 1572872 | tf_op jit(solution)/shard_map/ppermute | solution.py:230
  110.1 4.0 %collective-permute-start.14 = (bf16[512,512]{1,0:T(8,128)(2,1)}, bf16[512,512]{1,0:T(8,128)(2,1)S(1)}, u32[]{:S(2)}, u32[]{:S(2)}) collective-permute-start(bf16[512,512]{1,0:T(8,128)(2,1)} %get-tuple-element.60), channel_id=1, source_target_pairs={{0,3},{1,0},{2,1},{3,2},{4,7},{5,4},{6,5},{7,6},{8,11},{9,8},{10,9... | collective-permute-start | bytes 1572872 | tf_op jit(solution)/shard_map/ppermute | solution.py:230
  114.1 18.2 %collective-permute-done.12.refs_1_ = bf16[512,512]{1,0:T(8,128)(2,1)S(1)} collective-permute-done((bf16[512,512]{1,0:T(8,128)(2,1)}, bf16[512,512]{1,0:T(8,128)(2,1)S(1)}, u32[]{:S(2)}, u32[]{:S(2)}) %collective-permute-start.12) | collective-permute-done | bytes 524320 | tf_op jit(solution)/shard_map/ppermute | solution.py:230
  132.2 2.8 %collective-permute-done.14.refs_3_ = bf16[512,512]{1,0:T(8,128)(2,1)S(1)} collective-permute-done((bf16[512,512]{1,0:T(8,128)(2,1)}, bf16[512,512]{1,0:T(8,128)(2,1)S(1)}, u32[]{:S(2)}, u32[]{:S(2)}) %collective-permute-start.14) | collective-permute-done | bytes 524320 | tf_op jit(solution)/shard_map/ppermute | solution.py:230
  137.1 6.6 %all-to-all-start.6 = ((bf16[8,64,512]{2,1,0:T(8,128)(2,1)}), bf16[8,64,512]{2,1,0:T(8,128)(2,1)S(1)}, u32[]{:S(2)}, u32[]{:S(2)}) async-start(bf16[8,64,512]{2,1,0:T(8,128)(2,1)} %bitcast.16), calls=%async_computation.6 | async-start | bytes 1048576 | tf_op jit(solution)/shard_map/all_to_all | solution.py:234
  143.9 3.5 %collective-permute-start.15 = (bf16[64,256]{1,0:T(8,128)(2,1)S(1)}, bf16[64,256]{1,0:T(8,128)(2,1)S(1)}, u32[]{:S(2)}, u32[]{:S(2)}) collective-permute-start(bf16[64,256]{1,0:T(8,128)(2,1)S(1)} %get-tuple-element.65), channel_id=1, source_target_pairs={{0,1},{1,2},{2,3},{3,0},{4,5},{5,6},{6,7},{7,4},{8,9},{9,10},{10,1... | collective-permute-start | bytes 98312 | tf_op jit(solution)/shard_map/ppermute | solution.py:230
  147.3 4.8 %collective-permute-start.16 = (bf16[64,256]{1,0:T(8,128)(2,1)S(1)}, bf16[64,256]{1,0:T(8,128)(2,1)S(1)}, u32[]{:S(2)}, u32[]{:S(2)}) collective-permute-start(bf16[64,256]{1,0:T(8,128)(2,1)S(1)} %get-tuple-element.66), channel_id=1, source_target_pairs={{0,2},{1,3},{2,0},{3,1},{4,6},{5,7},{6,4},{7,5},{8,10},{9,11},{10,... | collective-permute-start | bytes 98312 | tf_op jit(solution)/shard_map/ppermute | solution.py:230
  154.1 2.9 %collective-permute-done.17.refs_4_ = bf16[64,256]{1,0:T(8,128)(2,1)S(1)} collective-permute-done((bf16[64,256]{1,0:T(8,128)(2,1)S(1)}, bf16[64,256]{1,0:T(8,128)(2,1)S(1)}, u32[]{:S(2)}, u32[]{:S(2)}) %collective-permute-start.17) | collective-permute-done | bytes 32800 | tf_op jit(solution)/shard_map/ppermute | solution.py:230
  157.0 2.7 %all-to-all-done.6.refs_0_ = bf16[8,64,512]{2,1,0:T(8,128)(2,1)S(1)} async-done(((bf16[8,64,512]{2,1,0:T(8,128)(2,1)}), bf16[8,64,512]{2,1,0:T(8,128)(2,1)S(1)}, u32[]{:S(2)}, u32[]{:S(2)}) %all-to-all-start.6) | async-done | bytes 524320 | tf_op jit(solution)/shard_map/all_to_all | solution.py:234
  160.0 14.1 %all_to_all.40.refs_0_ = bf16[16,32,128]{2,1,0:T(8,128)(2,1)S(1)} all-to-all(bf16[16,32,128]{2,1,0:T(8,128)(2,1)S(1)} %shard_map.122), channel_id=1, replica_groups=mesh['expert'=16,'tensor'=8,'dp'=4] {'expert'}, dimensions={0} | all-to-all | bytes 262144 | tf_op jit(solution)/shard_map/all_to_all | solution.py:410
  (54 shorter events, 24.4 us)
Async XLA Ops:
  2.6 20.6 %all-to-all-start.2 = ((bf16[16,48,128]{2,1,0:T(8,128)(2,1)}), bf16[16,48,128]{2,1,0:T(8,128)(2,1)S(1)}, u32[]{:S(2)}, u32[]{:S(2)}) async-start(bf16[16,48,128]{2,1,0:T(8,128)(2,1)} %get-tuple-element.49), calls=%async_computation.2 | async-start | bytes 393216 | tf_op jit(solution)/shard_map/all_to_all | solution.py:368
  24.9 26.5 %all-to-all-start.3 = ((bf16[8,64,512]{2,1,0:T(8,128)(2,1)}), bf16[8,64,512]{2,1,0:T(8,128)(2,1)S(1)}, u32[]{:S(2)}, u32[]{:S(2)}) async-start(bf16[8,64,512]{2,1,0:T(8,128)(2,1)} %get-tuple-element.53), calls=%async_computation.3 | async-start | bytes 1048576 | tf_op jit(solution)/shard_map/all_to_all | solution.py:234
  33.3 14.6 %collective-permute-start.8 = (bf16[64,256]{1,0:T(8,128)(2,1)S(1)}, bf16[64,256]{1,0:T(8,128)(2,1)S(1)}, u32[]{:S(2)}, u32[]{:S(2)}) collective-permute-start(bf16[64,256]{1,0:T(8,128)(2,1)S(1)} %get-tuple-element.50.refs_0_), channel_id=1, source_target_pairs={{0,3},{1,0},{2,1},{3,2},{4,7},{5,4},{6,5},{7,6},{8,11},{9,8},{10,9... | collective-permute-start | bytes 98312 | tf_op jit(solution)/shard_map/ppermute | solution.py:230
  37.7 10.2 %collective-permute-start.7 = (bf16[64,256]{1,0:T(8,128)(2,1)S(1)}, bf16[64,256]{1,0:T(8,128)(2,1)S(1)}, u32[]{:S(2)}, u32[]{:S(2)}) collective-permute-start(bf16[64,256]{1,0:T(8,128)(2,1)S(1)} %get-tuple-element.50.refs_0_), channel_id=1, source_target_pairs={{0,2},{1,3},{2,0},{3,1},{4,6},{5,7},{6,4},{7,5},{8,10},{9,11},{10,... | collective-permute-start | bytes 98312 | tf_op jit(solution)/shard_map/ppermute | solution.py:230
  40.2 7.8 %collective-permute-start.6 = (bf16[64,256]{1,0:T(8,128)(2,1)S(1)}, bf16[64,256]{1,0:T(8,128)(2,1)S(1)}, u32[]{:S(2)}, u32[]{:S(2)}) collective-permute-start(bf16[64,256]{1,0:T(8,128)(2,1)S(1)} %get-tuple-element.50.refs_0_), channel_id=1, source_target_pairs={{0,1},{1,2},{2,3},{3,0},{4,5},{5,6},{6,7},{7,4},{8,9},{9,10},{10,1... | collective-permute-start | bytes 98312 | tf_op jit(solution)/shard_map/ppermute | solution.py:230
  51.4 12.1 %copy-start.12 = (bf16[8,64,512]{2,1,0:T(8,128)(2,1)}, bf16[8,64,512]{2,1,0:T(8,128)(2,1)S(1)}, u32[]{:S(2)}) copy-start(bf16[8,64,512]{2,1,0:T(8,128)(2,1)S(1)} %all-to-all-done.3) | copy-start | bytes 1572868
  51.4 37.4 %all-to-all-start.4 = ((bf16[8,4,64,256]{3,2,1,0:T(8,128)(2,1)}), bf16[8,4,64,256]{3,2,1,0:T(8,128)(2,1)S(1)}, u32[]{:S(2)}, u32[]{:S(2)}) async-start(bf16[8,4,64,256]{3,2,1,0:T(8,128)(2,1)} %shard_map.117), calls=%async_computation.4 | async-start | bytes 2097152 | tf_op jit(solution)/shard_map/all_to_all | solution.py:234
  56.4 14.0 %collective-permute-start.11 = (bf16[512,512]{1,0:T(8,128)(2,1)S(1)}, bf16[512,512]{1,0:T(8,128)(2,1)S(1)}, u32[]{:S(2)}, u32[]{:S(2)}) collective-permute-start(bf16[512,512]{1,0:T(8,128)(2,1)S(1)} %bitcast.33), channel_id=1, source_target_pairs={{0,3},{1,0},{2,1},{3,2},{4,7},{5,4},{6,5},{7,6},{8,11},{9,8},{10,9... | collective-permute-start | bytes 1572872 | tf_op jit(solution)/shard_map/ppermute | solution.py:230
  60.4 15.2 %collective-permute-start.10 = (bf16[512,512]{1,0:T(8,128)(2,1)S(1)}, bf16[512,512]{1,0:T(8,128)(2,1)S(1)}, u32[]{:S(2)}, u32[]{:S(2)}) collective-permute-start(bf16[512,512]{1,0:T(8,128)(2,1)S(1)} %bitcast.34), channel_id=1, source_target_pairs={{0,2},{1,3},{2,0},{3,1},{4,6},{5,7},{6,4},{7,5},{8,10},{9,11},{10,... | collective-permute-start | bytes 1572872 | tf_op jit(solution)/shard_map/ppermute | solution.py:230
  63.5 25.3 %collective-permute-start.9 = (bf16[512,512]{1,0:T(8,128)(2,1)S(1)}, bf16[512,512]{1,0:T(8,128)(2,1)S(1)}, u32[]{:S(2)}, u32[]{:S(2)}) collective-permute-start(bf16[512,512]{1,0:T(8,128)(2,1)S(1)} %bitcast.35), channel_id=1, source_target_pairs={{0,1},{1,2},{2,3},{3,0},{4,5},{5,6},{6,7},{7,4},{8,9},{9,10},{10,1... | collective-permute-start | bytes 1572872 | tf_op jit(solution)/shard_map/ppermute | solution.py:230
  70.4 18.4 %copy-start.13 = (bf16[512,512]{1,0:T(8,128)(2,1)}, bf16[512,512]{1,0:T(8,128)(2,1)S(1)}, u32[]{:S(2)}) copy-start(bf16[512,512]{1,0:T(8,128)(2,1)S(1)} %collective-permute-done.11.refs_4_.refs_5_) | copy-start | bytes 1572868
  75.5 13.3 %copy-start.14 = (bf16[512,512]{1,0:T(8,128)(2,1)}, bf16[512,512]{1,0:T(8,128)(2,1)S(1)}, u32[]{:S(2)}) copy-start(bf16[512,512]{1,0:T(8,128)(2,1)S(1)} %collective-permute-done.10.refs_3_.refs_4_) | copy-start | bytes 1572868
  94.1 40.9 %all-to-all-start.5 = ((bf16[8,4,64,256]{3,2,1,0:T(8,128)(2,1)}), bf16[8,4,64,256]{3,2,1,0:T(8,128)(2,1)S(1)}, u32[]{:S(2)}, u32[]{:S(2)}) async-start(bf16[8,4,64,256]{3,2,1,0:T(8,128)(2,1)} %bitcast.31), calls=%async_computation.5 | async-start | bytes 2097152 | tf_op jit(solution)/shard_map/all_to_all | solution.py:234
  105.0 27.2 %collective-permute-start.12 = (bf16[512,512]{1,0:T(8,128)(2,1)}, bf16[512,512]{1,0:T(8,128)(2,1)S(1)}, u32[]{:S(2)}, u32[]{:S(2)}) collective-permute-start(bf16[512,512]{1,0:T(8,128)(2,1)} %get-tuple-element.58), channel_id=1, source_target_pairs={{0,1},{1,2},{2,3},{3,0},{4,5},{5,6},{6,7},{7,4},{8,9},{9,10},{10,1... | collective-permute-start | bytes 1572872 | tf_op jit(solution)/shard_map/ppermute | solution.py:230
  106.9 25.3 %collective-permute-start.13 = (bf16[512,512]{1,0:T(8,128)(2,1)}, bf16[512,512]{1,0:T(8,128)(2,1)S(1)}, u32[]{:S(2)}, u32[]{:S(2)}) collective-permute-start(bf16[512,512]{1,0:T(8,128)(2,1)} %get-tuple-element.59), channel_id=1, source_target_pairs={{0,2},{1,3},{2,0},{3,1},{4,6},{5,7},{6,4},{7,5},{8,10},{9,11},{10,... | collective-permute-start | bytes 1572872 | tf_op jit(solution)/shard_map/ppermute | solution.py:230
  110.1 24.9 %collective-permute-start.14 = (bf16[512,512]{1,0:T(8,128)(2,1)}, bf16[512,512]{1,0:T(8,128)(2,1)S(1)}, u32[]{:S(2)}, u32[]{:S(2)}) collective-permute-start(bf16[512,512]{1,0:T(8,128)(2,1)} %get-tuple-element.60), channel_id=1, source_target_pairs={{0,3},{1,0},{2,1},{3,2},{4,7},{5,4},{6,5},{7,6},{8,11},{9,8},{10,9... | collective-permute-start | bytes 1572872 | tf_op jit(solution)/shard_map/ppermute | solution.py:230
  137.1 22.6 %all-to-all-start.6 = ((bf16[8,64,512]{2,1,0:T(8,128)(2,1)}), bf16[8,64,512]{2,1,0:T(8,128)(2,1)S(1)}, u32[]{:S(2)}, u32[]{:S(2)}) async-start(bf16[8,64,512]{2,1,0:T(8,128)(2,1)} %bitcast.16), calls=%async_computation.6 | async-start | bytes 1048576 | tf_op jit(solution)/shard_map/all_to_all | solution.py:234
  143.9 10.3 %collective-permute-start.15 = (bf16[64,256]{1,0:T(8,128)(2,1)S(1)}, bf16[64,256]{1,0:T(8,128)(2,1)S(1)}, u32[]{:S(2)}, u32[]{:S(2)}) collective-permute-start(bf16[64,256]{1,0:T(8,128)(2,1)S(1)} %get-tuple-element.65), channel_id=1, source_target_pairs={{0,1},{1,2},{2,3},{3,0},{4,5},{5,6},{6,7},{7,4},{8,9},{9,10},{10,1... | collective-permute-start | bytes 98312 | tf_op jit(solution)/shard_map/ppermute | solution.py:230
  147.3 6.8 %collective-permute-start.16 = (bf16[64,256]{1,0:T(8,128)(2,1)S(1)}, bf16[64,256]{1,0:T(8,128)(2,1)S(1)}, u32[]{:S(2)}, u32[]{:S(2)}) collective-permute-start(bf16[64,256]{1,0:T(8,128)(2,1)S(1)} %get-tuple-element.66), channel_id=1, source_target_pairs={{0,2},{1,3},{2,0},{3,1},{4,6},{5,7},{6,4},{7,5},{8,10},{9,11},{10,... | collective-permute-start | bytes 98312 | tf_op jit(solution)/shard_map/ppermute | solution.py:230
  152.2 4.8 %collective-permute-start.17 = (bf16[64,256]{1,0:T(8,128)(2,1)S(1)}, bf16[64,256]{1,0:T(8,128)(2,1)S(1)}, u32[]{:S(2)}, u32[]{:S(2)}) collective-permute-start(bf16[64,256]{1,0:T(8,128)(2,1)S(1)} %get-tuple-element.67), channel_id=1, source_target_pairs={{0,3},{1,0},{2,1},{3,2},{4,7},{5,4},{6,5},{7,6},{8,11},{9,8},{10,9... | collective-permute-start | bytes 98312 | tf_op jit(solution)/shard_map/ppermute | solution.py:230
  159.7 14.5 %copy-start.3 = (bf16[128,64]{0,1:T(8,128)(2,1)S(1)}, bf16[128,64]{0,1:T(8,128)(2,1)}, u32[]{:S(2)}) copy-start(bf16[128,64]{0,1:T(8,128)(2,1)} %param.12) | copy-start | bytes 49156
  159.7 14.5 %copy-start.7 = (s32[2,128]{1,0:T(2,128)S(1)}, s32[2,128]{1,0:T(2,128)}, u32[]{:S(2)}) copy-start(s32[2,128]{1,0:T(2,128)} %get-tuple-element.71.refs_1_) | copy-start | bytes 3076
  159.7 14.5 %copy-start.8 = (s32[1,144]{1,0:T(1,128)S(1)}, s32[1,144]{1,0:T(1,128)}, u32[]{:S(2)}) copy-start(s32[1,144]{1,0:T(1,128)} %get-tuple-element.72.refs_2_) | copy-start | bytes 1732
  160.0 14.1 %copy-start.2 = (bf16[144,64]{0,1:T(8,128)(2,1)S(1)}, bf16[144,64]{0,1:T(8,128)(2,1)}, u32[]{:S(2)}) copy-start(bf16[144,64]{0,1:T(8,128)(2,1)} %param.17) | copy-start | bytes 55300
  (8 other events, 13.0 us)

commit v7 on v5

--- a/solution.py
+++ b/solution.py
@@ -163,7 +163,7 @@
             out_turned[pl.ds(to, FEATS), :] = block[k * FEATS : (k + 1) * FEATS]
 
 
-def expert_body(me, x0, x1, x2, x3, w_in, w_out, p0, p1, p2, p3, xs, ins, outs, ps, sems):
+def expert_steps(me, x0, x1, x2, x3, w_in, w_out, p0, p1, p2, p3, xs, ins, outs, ps, sems):
     d = me[0]
     near = []
     for k, x in enumerate((x0, x1, x2, x3)):
@@ -176,6 +176,7 @@
         far[k] = pltpu.make_async_copy(w_out.at[goal], outs.at[k], sems.at[2 * DP + k])
     for copy in near + list(far.values()):
         copy.start()
+    yield
     hidden = None
     for k in range(DP):
         near[2 * k].wait()
@@ -189,8 +190,22 @@
         ps[k] = nn(outs[k], hidden).astype(BF)
         gone.append(pltpu.make_async_copy(ps.at[k], (p0, p1, p2, p3)[k], sems.at[3 * DP + k]))
         gone[-1].start()
+    yield
     for copy in gone:
         copy.wait()
+
+
+def expert_body(*refs):
+    for _ in expert_steps(*refs):
+        pass
+
+
+def both_body(me, x0, x1, x2, x3, e_in, e_out, x, d_in, d_out, p0, p1, p2, p3, part, *held):
+    near = crossed_steps(x, d_in, d_out, part, *held[5:])
+    far = expert_steps(me, x0, x1, x2, x3, e_in, e_out, p0, p1, p2, p3, *held[:5])
+    for _ in zip(near, far):
+        pass
+    next(far, None)
 
 
 def add_body(a, b, c, d, out):
@@ -239,11 +254,14 @@
     return [own] + [shift(own, k) for k in (1, 2, 3)]
 
 
+def held_for(rows, turned, sems):
+    held = pltpu.VMEM((DP, T * FEATS, rows), BF)
+    return [held, *(pltpu.VMEM(w.shape, BF) for w in turned), held, pltpu.SemaphoreType.DMA((sems,))]
+
+
 def expert(blocks, turned, me):
     rows = blocks[0].shape[1]
     part = shape((T * FEATS, rows))
-    work = 4 * rows * UNITS * T * DP * FEATS
-    held = pltpu.VMEM((DP, T * FEATS, rows), BF)
     return call(
         expert_body,
         [part] * 4,
@@ -251,11 +269,32 @@
         smem=(0,),
         far=range(1, 7),
         far_out=True,
-        scratch=[held, *(pltpu.VMEM(w.shape, BF) for w in turned), held, pltpu.SemaphoreType.DMA((4 * DP,))],
+        scratch=held_for(rows, turned, 4 * DP),
         limit=60,
-        flops=work,
+        flops=4 * rows * UNITS * T * DP * FEATS,
         moved=6 << 20,
     )(me, *blocks, *turned)
+
+
+def both_experts(blocks, turned, x, near_turned, me):
+    rows, near_rows = blocks[0].shape[1], x.shape[3]
+    flat = x.reshape(T * DP * FEATS, near_rows)
+    near = [pltpu.VMEM(flat.shape, BF), *(pltpu.VMEM(w.shape, BF) for w in near_turned)]
+    *parts, part = call(
+        both_body,
+        [shape((T * FEATS, rows))] * 4 + [shape(flat.shape)],
+        10,
+        smem=(0,),
+        far=range(1, 10),
+        far_out=True,
+        scratch=held_for(rows, turned, 4 * DP)
+        + near
+        + [pltpu.VMEM(flat.shape, BF), pltpu.SemaphoreType.DMA((1 + 3 * DP,))],
+        limit=60,
+        flops=4 * (rows + near_rows) * UNITS * T * DP * FEATS,
+        moved=10 << 20,
+    )(me, *blocks, *turned, flat, *near_turned)
+    return parts, part.reshape(x.shape)
 
 
 def arrive(parts):
@@ -285,7 +324,7 @@
             out[t, k] = ref[...]
 
 
-def crossed_body(x, w_in, w_out, part, xs, ins, outs, ps, sems):
+def crossed_steps(x, w_in, w_out, part, xs, ins, outs, ps, sems):
     span = T * FEATS
     first = pltpu.make_async_copy(w_in, ins, sems.at[0])
     near = []
@@ -296,6 +335,7 @@
         far.append(pltpu.make_async_copy(w_out.at[cut], outs.at[cut], sems.at[1 + DP + k]))
     for copy in [first] + near + far:
         copy.start()
+    yield
     first.wait()
     hidden = None
     for k in range(DP):
@@ -310,6 +350,7 @@
         ps[k * span : (k + 1) * span, :] = nn(outs[k * span : (k + 1) * span, :], hidden).astype(BF)
         gone.append(pltpu.make_async_copy(ps.at[cut], part.at[cut], sems.at[1 + 2 * DP + k]))
         gone[-1].start()
+    yield
     for copy in gone:
         copy.wait()
 
@@ -320,26 +361,6 @@
         for t in range(1, T):
             acc = acc + got[t, k].astype(F32)
         ref[...] = acc.astype(BF)
-
-
-def expert_crossed(x, turned, later):
-    rows = x.shape[3]
-    flat = x.reshape(T * DP * FEATS, rows)
-    work = 4 * rows * UNITS * T * DP * FEATS
-    held = pltpu.VMEM(flat.shape, BF)
-    part = call(
-        crossed_body,
-        shape(flat.shape),
-        3,
-        far=range(3),
-        far_out=True,
-        scratch=[held, *(pltpu.VMEM(w.shape, BF) for w in turned), held, pltpu.SemaphoreType.DMA((1 + 3 * DP,))],
-        limit=60,
-        flops=work,
-        moved=4 << 20,
-        after=len(later),
-    )(flat, *turned, *later)
-    return part.reshape(x.shape)
 
 
 def shards(
@@ -381,8 +402,8 @@
         1,
         smem_out=(4,),
         moved=1 << 20,
-        after=2,
-    )(got, enc_ready, dec_ready)
+        after=1,
+    )(got, enc_ready)
 
     near_x = [dec_block] + [shift(dec_block, k) for k in (1, 2, 3)]
     dec_x = call(copies_body, shape((T, DP, FEATS, HELD)), 4, moved=1 << 20)(*near_x)
@@ -390,8 +411,8 @@
     (dec_x,), (enc_t,) = tie([dec_x], [enc_t])
     enc_x = gather(enc_t)
     dec_x = over_tensor(dec_x)
-    dec_parts = expert_crossed(dec_x, near_turned, enc_x[1:])
-    enc_got = arrive(expert(enc_x, enc_turned, me))
+    enc_parts, dec_parts = both_experts(enc_x, enc_turned, dec_x, near_turned, me)
+    enc_got = arrive(enc_parts)
     dec_parts = over_tensor(dec_parts)
     dec_halves = call(crossed_sum_body, [shape((FEATS, HELD))] * 4, 1, moved=1 << 20)(dec_parts)
     dec_sums = arrive(dec_halves)

time: 173 us -> 174 us (level)
  waiting for transfers between devices: 54.7 us -> 62.6 us
  starting transfers between devices: 77.1 us -> 73.5 us
    ppermute x12, waiting for transfers between devices: 41.7 us -> 48.6 us  [shift(): return lax.ppermute(value, 'dp', [(i, (i + k) % DP) for i in range(DP)])]
    ppermute x12, starting transfers between devices: 42.2 us -> 37.3 us  [shift(): return lax.ppermute(value, 'dp', [(i, (i + k) % DP) for i in range(DP)])]
    all_to_all x1, waiting for transfers between devices: 5.09 us -> 7 us  [shards(): lax.all_to_all(sent, 'expert', split_axis=0, concat_axis=0, tiled=True)]
    pallas_call x2 -> x1, Pallas kernels: 8.37 us -> 6.89 us  [both_experts(): call(both_body, [shape((T * FEATS, rows))] * 4 + [shape(flat.shape)], 10,...]
  transfers between devices with their start and end apart: 17 -> 17, of which waited for: 13 -> 11; matrix products, arithmetic and copies ran while one was open for 0% -> 0% of each run, Pallas kernels for 6% -> 4%
where the time goes in v7:
time: 174 us; the launch traced here: 173 us
  starting transfers between devices  73.5 us (42%)
  waiting for transfers between devices  62.6 us (36%)
  Pallas kernels  18.6 us (11%)
  blocking collectives  14.1 us (8%)
  local copies, waits for them, and re-layouts  2.25 us (1%)
    ppermute x12, waiting for transfers between devices, shift(): return lax.ppermute(value, 'dp', [(i, (i + k) % DP) for i in range(DP)])  48.6 us
    ppermute x12, starting transfers between devices, shift(): return lax.ppermute(value, 'dp', [(i, (i + k) % DP) for i in range(DP)])  37.3 us
    all_to_all x4, starting transfers between devices, over_tensor(): lax.all_to_all(block, 'tensor', split_axis=0, concat_axis=0, tiled=True)  26 us
    all_to_all x1, blocking collectives, shards(): lax.all_to_all(back, 'expert', split_axis=0, concat_axis=0, tiled=True)  14.1 us
    all_to_all x1, starting transfers between devices, shards(): lax.all_to_all(sent, 'expert', split_axis=0, concat_axis=0, tiled=True)  10.2 us
    all_to_all x1, waiting for transfers between devices, shards(): lax.all_to_all(sent, 'expert', split_axis=0, concat_axis=0, tiled=True)  7 us
    all_to_all x4, waiting for transfers between devices, over_tensor(): lax.all_to_all(block, 'tensor', split_axis=0, concat_axis=0, tiled=True)  7 us
    pallas_call x1, Pallas kernels, both_experts(): call(both_body, [shape((T * FEATS, rows))] * 4 + [shape(flat.shape)], 10,...  6.89 us
  transfers between devices with their start and end apart: 17, of which 11 were waited for; matrix products, arithmetic and copies ran while one was open for 0% of the time, Pallas kernels for 4%

profile of v7, /device:TPU:1, one launch (start us, length us, event | category | flops | bytes accessed | tf_op | source)
XLA Modules:
  0.0 172.6 jit_solution(10524946899127694430)
XLA Ops:
  2.6 10.2 %all-to-all-start.2 = ((bf16[16,48,128]{2,1,0:T(8,128)(2,1)}), bf16[16,48,128]{2,1,0:T(8,128)(2,1)S(1)}, u32[]{:S(2)}, u32[]{:S(2)}) async-start(bf16[16,48,128]{2,1,0:T(8,128)(2,1)} %get-tuple-element.49), calls=%async_computation.2 | async-start | bytes 393216 | tf_op jit(solution)/shard_map/all_to_all | solution.py:389
  12.8 3.4 %shard_map.114 = (bf16[4,256,512]{2,1,0:T(8,128)(2,1)}, bf16[4,512,256]{2,1,0:T(8,128)(2,1)}, bf16[16,128]{1,0:T(8,128)(2,1)}) custom-call(bf16[2048,256]{1,0:T(8,128)(2,1)} %bitcast.35, bf16[256,2048]{1,0:T(8,128)(2,1)} %bitcast.36), custom_call_target="tpu_custom_call" | custom-call | bytes 4194304 | tf_op jit(solution)/shard_map/pallas_call | solution.py:393
  16.2 7.0 %all-to-all-done.2.refs_0_ = bf16[16,48,128]{2,1,0:T(8,128)(2,1)S(1)} async-done(((bf16[16,48,128]{2,1,0:T(8,128)(2,1)}), bf16[16,48,128]{2,1,0:T(8,128)(2,1)S(1)}, u32[]{:S(2)}, u32[]{:S(2)}) %all-to-all-start.2) | async-done | bytes 196640 | tf_op jit(solution)/shard_map/all_to_all | solution.py:389
  25.6 8.4 %all-to-all-start.3 = ((bf16[8,64,512]{2,1,0:T(8,128)(2,1)}), bf16[8,64,512]{2,1,0:T(8,128)(2,1)S(1)}, u32[]{:S(2)}, u32[]{:S(2)}) async-start(bf16[8,64,512]{2,1,0:T(8,128)(2,1)} %get-tuple-element.52), calls=%async_computation.3 | async-start | bytes 1048576 | tf_op jit(solution)/shard_map/all_to_all | solution.py:249
  34.0 4.4 %collective-permute-start.8 = (bf16[64,256]{1,0:T(8,128)(2,1)S(1)}, bf16[64,256]{1,0:T(8,128)(2,1)S(1)}, u32[]{:S(2)}, u32[]{:S(2)}) collective-permute-start(bf16[64,256]{1,0:T(8,128)(2,1)S(1)} %get-tuple-element.51.refs_0_), channel_id=1, source_target_pairs={{0,3},{1,0},{2,1},{3,2},{4,7},{5,4},{6,5},{7,6},{8,11},{9,8},{10,9... | collective-permute-start | bytes 98312 | tf_op jit(solution)/shard_map/ppermute | solution.py:245
  40.9 2.5 %collective-permute-start.6 = (bf16[64,256]{1,0:T(8,128)(2,1)S(1)}, bf16[64,256]{1,0:T(8,128)(2,1)S(1)}, u32[]{:S(2)}, u32[]{:S(2)}) collective-permute-start(bf16[64,256]{1,0:T(8,128)(2,1)S(1)} %get-tuple-element.51.refs_0_), channel_id=1, source_target_pairs={{0,1},{1,2},{2,3},{3,0},{4,5},{5,6},{6,7},{7,4},{8,9},{9,10},{10,1... | collective-permute-start | bytes 98312 | tf_op jit(solution)/shard_map/ppermute | solution.py:245
  47.8 4.3 %all-to-all-done.3 = bf16[8,64,512]{2,1,0:T(8,128)(2,1)S(1)} async-done(((bf16[8,64,512]{2,1,0:T(8,128)(2,1)}), bf16[8,64,512]{2,1,0:T(8,128)(2,1)S(1)}, u32[]{:S(2)}, u32[]{:S(2)}) %all-to-all-start.3) | async-done | bytes 524320 | tf_op jit(solution)/shard_map/all_to_all | solution.py:249
  52.1 4.2 %all-to-all-start.4 = ((bf16[8,4,64,256]{3,2,1,0:T(8,128)(2,1)}), bf16[8,4,64,256]{3,2,1,0:T(8,128)(2,1)}, u32[]{:S(2)}, u32[]{:S(2)}) async-start(bf16[8,4,64,256]{3,2,1,0:T(8,128)(2,1)} %shard_map.116), calls=%async_computation.4 | async-start | bytes 2097152 | tf_op jit(solution)/shard_map/all_to_all | solution.py:249
  56.3 4.4 %collective-permute-start.11 = (bf16[512,512]{1,0:T(8,128)(2,1)S(1)}, bf16[512,512]{1,0:T(8,128)(2,1)S(1)}, u32[]{:S(2)}, u32[]{:S(2)}) collective-permute-start(bf16[512,512]{1,0:T(8,128)(2,1)S(1)} %bitcast.31), channel_id=1, source_target_pairs={{0,3},{1,0},{2,1},{3,2},{4,7},{5,4},{6,5},{7,6},{8,11},{9,8},{10,9... | collective-permute-start | bytes 1572872 | tf_op jit(solution)/shard_map/ppermute | solution.py:245
  63.2 2.5 %collective-permute-start.9 = (bf16[512,512]{1,0:T(8,128)(2,1)S(1)}, bf16[512,512]{1,0:T(8,128)(2,1)}, u32[]{:S(2)}, u32[]{:S(2)}) collective-permute-start(bf16[512,512]{1,0:T(8,128)(2,1)S(1)} %bitcast.33), channel_id=1, source_target_pairs={{0,1},{1,2},{2,3},{3,0},{4,5},{5,6},{6,7},{7,4},{8,9},{9,10},{10,1... | collective-permute-start | bytes 1572872 | tf_op jit(solution)/shard_map/ppermute | solution.py:245
  67.6 4.7 %collective-permute-done.11.refs_4_ = bf16[512,512]{1,0:T(8,128)(2,1)S(1)} collective-permute-done((bf16[512,512]{1,0:T(8,128)(2,1)S(1)}, bf16[512,512]{1,0:T(8,128)(2,1)S(1)}, u32[]{:S(2)}, u32[]{:S(2)}) %collective-permute-start.11) | collective-permute-done | bytes 524320 | tf_op jit(solution)/shard_map/ppermute | solution.py:245
  72.3 4.6 %collective-permute-done.10.refs_3_ = bf16[512,512]{1,0:T(8,128)(2,1)S(1)} collective-permute-done((bf16[512,512]{1,0:T(8,128)(2,1)S(1)}, bf16[512,512]{1,0:T(8,128)(2,1)S(1)}, u32[]{:S(2)}, u32[]{:S(2)}) %collective-permute-start.10) | collective-permute-done | bytes 524320 | tf_op jit(solution)/shard_map/ppermute | solution.py:245
  77.8 11.6 %collective-permute-done.9.refs_2_ = bf16[512,512]{1,0:T(8,128)(2,1)} collective-permute-done((bf16[512,512]{1,0:T(8,128)(2,1)S(1)}, bf16[512,512]{1,0:T(8,128)(2,1)}, u32[]{:S(2)}, u32[]{:S(2)}) %collective-permute-start.9) | collective-permute-done | bytes 524320 | tf_op jit(solution)/shard_map/ppermute | solution.py:245
  89.3 6.9 %shard_map.118 = (bf16[512,512]{1,0:T(8,128)(2,1)}, bf16[512,512]{1,0:T(8,128)(2,1)}, bf16[512,512]{1,0:T(8,128)(2,1)}, bf16[512,512]{1,0:T(8,128)(2,1)}, bf16[2048,256]{1,0:T(8,128)(2,1)}) custom-call(s32[1]{0:T(128)} %bitcast.4.refs_0_, bf16[512,512]{1,0:T(8,128)(2,1)} %bitcast.34, bf16[512,512]{1,0:T(8,128)(2,1)} %collective-permute-done.9.refs_2_, ...), custom_call_target="tpu_custom_call" | custom-call | flops 1610612736 | bytes 10485760 | tf_op jit(solution)/shard_map/pallas_call | solution.py:283
  96.2 6.7 %all-to-all-start.5 = ((bf16[8,4,64,256]{3,2,1,0:T(8,128)(2,1)}), bf16[8,4,64,256]{3,2,1,0:T(8,128)(2,1)S(1)}, u32[]{:S(2)}, u32[]{:S(2)}) async-start(bf16[8,4,64,256]{3,2,1,0:T(8,128)(2,1)} %bitcast.37), calls=%async_computation.5 | async-start | bytes 2097152 | tf_op jit(solution)/shard_map/all_to_all | solution.py:249
  107.3 4.1 %collective-permute-start.14 = (bf16[512,512]{1,0:T(8,128)(2,1)}, bf16[512,512]{1,0:T(8,128)(2,1)S(1)}, u32[]{:S(2)}, u32[]{:S(2)}) collective-permute-start(bf16[512,512]{1,0:T(8,128)(2,1)} %get-tuple-element.62), channel_id=1, source_target_pairs={{0,3},{1,0},{2,1},{3,2},{4,7},{5,4},{6,5},{7,6},{8,11},{9,8},{10,9... | collective-permute-start | bytes 1572872 | tf_op jit(solution)/shard_map/ppermute | solution.py:245
  111.4 18.8 %collective-permute-done.12.refs_1_ = bf16[512,512]{1,0:T(8,128)(2,1)S(1)} collective-permute-done((bf16[512,512]{1,0:T(8,128)(2,1)}, bf16[512,512]{1,0:T(8,128)(2,1)S(1)}, u32[]{:S(2)}, u32[]{:S(2)}) %collective-permute-start.12) | collective-permute-done | bytes 524320 | tf_op jit(solution)/shard_map/ppermute | solution.py:245
  130.2 2.7 %collective-permute-done.14.refs_3_ = bf16[512,512]{1,0:T(8,128)(2,1)S(1)} collective-permute-done((bf16[512,512]{1,0:T(8,128)(2,1)}, bf16[512,512]{1,0:T(8,128)(2,1)S(1)}, u32[]{:S(2)}, u32[]{:S(2)}) %collective-permute-start.14) | collective-permute-done | bytes 524320 | tf_op jit(solution)/shard_map/ppermute | solution.py:245
  133.9 6.6 %all-to-all-start.6 = ((bf16[8,64,512]{2,1,0:T(8,128)(2,1)}), bf16[8,64,512]{2,1,0:T(8,128)(2,1)S(1)}, u32[]{:S(2)}, u32[]{:S(2)}) async-start(bf16[8,64,512]{2,1,0:T(8,128)(2,1)} %bitcast.16), calls=%async_computation.6 | async-start | bytes 1048576 | tf_op jit(solution)/shard_map/all_to_all | solution.py:249
  140.7 2.8 %collective-permute-start.15 = (bf16[64,256]{1,0:T(8,128)(2,1)S(1)}, bf16[64,256]{1,0:T(8,128)(2,1)S(1)}, u32[]{:S(2)}, u32[]{:S(2)}) collective-permute-start(bf16[64,256]{1,0:T(8,128)(2,1)S(1)} %get-tuple-element.65), channel_id=1, source_target_pairs={{0,1},{1,2},{2,3},{3,0},{4,5},{5,6},{6,7},{7,4},{8,9},{9,10},{10,1... | collective-permute-start | bytes 98312 | tf_op jit(solution)/shard_map/ppermute | solution.py:245
  143.6 5.5 %collective-permute-start.16 = (bf16[64,256]{1,0:T(8,128)(2,1)S(1)}, bf16[64,256]{1,0:T(8,128)(2,1)S(1)}, u32[]{:S(2)}, u32[]{:S(2)}) collective-permute-start(bf16[64,256]{1,0:T(8,128)(2,1)S(1)} %get-tuple-element.66), channel_id=1, source_target_pairs={{0,2},{1,3},{2,0},{3,1},{4,6},{5,7},{6,4},{7,5},{8,10},{9,11},{10,... | collective-permute-start | bytes 98312 | tf_op jit(solution)/shard_map/ppermute | solution.py:245
  151.0 2.9 %collective-permute-done.17.refs_4_ = bf16[64,256]{1,0:T(8,128)(2,1)S(1)} collective-permute-done((bf16[64,256]{1,0:T(8,128)(2,1)S(1)}, bf16[64,256]{1,0:T(8,128)(2,1)S(1)}, u32[]{:S(2)}, u32[]{:S(2)}) %collective-permute-start.17) | collective-permute-done | bytes 32800 | tf_op jit(solution)/shard_map/ppermute | solution.py:245
  153.9 2.7 %all-to-all-done.6.refs_0_ = bf16[8,64,512]{2,1,0:T(8,128)(2,1)S(1)} async-done(((bf16[8,64,512]{2,1,0:T(8,128)(2,1)}), bf16[8,64,512]{2,1,0:T(8,128)(2,1)S(1)}, u32[]{:S(2)}, u32[]{:S(2)}) %all-to-all-start.6) | async-done | bytes 524320 | tf_op jit(solution)/shard_map/all_to_all | solution.py:249
  156.9 14.1 %all_to_all.40.refs_0_ = bf16[16,32,128]{2,1,0:T(8,128)(2,1)S(1)} all-to-all(bf16[16,32,128]{2,1,0:T(8,128)(2,1)S(1)} %shard_map.121), channel_id=1, replica_groups=mesh['expert'=16,'tensor'=8,'dp'=4] {'expert'}, dimensions={0} | all-to-all | bytes 262144 | tf_op jit(solution)/shard_map/all_to_all | solution.py:430
  (47 shorter events, 25.1 us)
Async XLA Ops:
  2.6 20.6 %all-to-all-start.2 = ((bf16[16,48,128]{2,1,0:T(8,128)(2,1)}), bf16[16,48,128]{2,1,0:T(8,128)(2,1)S(1)}, u32[]{:S(2)}, u32[]{:S(2)}) async-start(bf16[16,48,128]{2,1,0:T(8,128)(2,1)} %get-tuple-element.49), calls=%async_computation.2 | async-start | bytes 393216 | tf_op jit(solution)/shard_map/all_to_all | solution.py:389
  12.8 12.7 %copy-start.9 = (bf16[1,256,2048]{2,1,0:T(8,128)(2,1)S(1)}, bf16[1,256,2048]{2,1,0:T(8,128)(2,1)}, u32[]{:S(2)}) copy-start(bf16[1,256,2048]{2,1,0:T(8,128)(2,1)} %param.21) | copy-start | bytes 3145732
  25.6 26.5 %all-to-all-start.3 = ((bf16[8,64,512]{2,1,0:T(8,128)(2,1)}), bf16[8,64,512]{2,1,0:T(8,128)(2,1)S(1)}, u32[]{:S(2)}, u32[]{:S(2)}) async-start(bf16[8,64,512]{2,1,0:T(8,128)(2,1)} %get-tuple-element.52), calls=%async_computation.3 | async-start | bytes 1048576 | tf_op jit(solution)/shard_map/all_to_all | solution.py:249
  34.0 9.3 %collective-permute-start.8 = (bf16[64,256]{1,0:T(8,128)(2,1)S(1)}, bf16[64,256]{1,0:T(8,128)(2,1)S(1)}, u32[]{:S(2)}, u32[]{:S(2)}) collective-permute-start(bf16[64,256]{1,0:T(8,128)(2,1)S(1)} %get-tuple-element.51.refs_0_), channel_id=1, source_target_pairs={{0,3},{1,0},{2,1},{3,2},{4,7},{5,4},{6,5},{7,6},{8,11},{9,8},{10,9... | collective-permute-start | bytes 98312 | tf_op jit(solution)/shard_map/ppermute | solution.py:245
  38.4 6.5 %collective-permute-start.7 = (bf16[64,256]{1,0:T(8,128)(2,1)S(1)}, bf16[64,256]{1,0:T(8,128)(2,1)S(1)}, u32[]{:S(2)}, u32[]{:S(2)}) collective-permute-start(bf16[64,256]{1,0:T(8,128)(2,1)S(1)} %get-tuple-element.51.refs_0_), channel_id=1, source_target_pairs={{0,2},{1,3},{2,0},{3,1},{4,6},{5,7},{6,4},{7,5},{8,10},{9,11},{10,... | collective-permute-start | bytes 98312 | tf_op jit(solution)/shard_map/ppermute | solution.py:245
  40.9 5.9 %collective-permute-start.6 = (bf16[64,256]{1,0:T(8,128)(2,1)S(1)}, bf16[64,256]{1,0:T(8,128)(2,1)S(1)}, u32[]{:S(2)}, u32[]{:S(2)}) collective-permute-start(bf16[64,256]{1,0:T(8,128)(2,1)S(1)} %get-tuple-element.51.refs_0_), channel_id=1, source_target_pairs={{0,1},{1,2},{2,3},{3,0},{4,5},{5,6},{6,7},{7,4},{8,9},{9,10},{10,1... | collective-permute-start | bytes 98312 | tf_op jit(solution)/shard_map/ppermute | solution.py:245
  52.1 37.2 %all-to-all-start.4 = ((bf16[8,4,64,256]{3,2,1,0:T(8,128)(2,1)}), bf16[8,4,64,256]{3,2,1,0:T(8,128)(2,1)}, u32[]{:S(2)}, u32[]{:S(2)}) async-start(bf16[8,4,64,256]{3,2,1,0:T(8,128)(2,1)} %shard_map.116), calls=%async_computation.4 | async-start | bytes 2097152 | tf_op jit(solution)/shard_map/all_to_all | solution.py:249
  56.3 16.0 %collective-permute-start.11 = (bf16[512,512]{1,0:T(8,128)(2,1)S(1)}, bf16[512,512]{1,0:T(8,128)(2,1)S(1)}, u32[]{:S(2)}, u32[]{:S(2)}) collective-permute-start(bf16[512,512]{1,0:T(8,128)(2,1)S(1)} %bitcast.31), channel_id=1, source_target_pairs={{0,3},{1,0},{2,1},{3,2},{4,7},{5,4},{6,5},{7,6},{8,11},{9,8},{10,9... | collective-permute-start | bytes 1572872 | tf_op jit(solution)/shard_map/ppermute | solution.py:245
  60.7 16.2 %collective-permute-start.10 = (bf16[512,512]{1,0:T(8,128)(2,1)S(1)}, bf16[512,512]{1,0:T(8,128)(2,1)S(1)}, u32[]{:S(2)}, u32[]{:S(2)}) collective-permute-start(bf16[512,512]{1,0:T(8,128)(2,1)S(1)} %bitcast.32), channel_id=1, source_target_pairs={{0,2},{1,3},{2,0},{3,1},{4,6},{5,7},{6,4},{7,5},{8,10},{9,11},{10,... | collective-permute-start | bytes 1572872 | tf_op jit(solution)/shard_map/ppermute | solution.py:245
  63.2 26.1 %collective-permute-start.9 = (bf16[512,512]{1,0:T(8,128)(2,1)S(1)}, bf16[512,512]{1,0:T(8,128)(2,1)}, u32[]{:S(2)}, u32[]{:S(2)}) collective-permute-start(bf16[512,512]{1,0:T(8,128)(2,1)S(1)} %bitcast.33), channel_id=1, source_target_pairs={{0,1},{1,2},{2,3},{3,0},{4,5},{5,6},{6,7},{7,4},{8,9},{9,10},{10,1... | collective-permute-start | bytes 1572872 | tf_op jit(solution)/shard_map/ppermute | solution.py:245
  72.3 17.0 %copy-start.12 = (bf16[512,512]{1,0:T(8,128)(2,1)}, bf16[512,512]{1,0:T(8,128)(2,1)S(1)}, u32[]{:S(2)}) copy-start(bf16[512,512]{1,0:T(8,128)(2,1)S(1)} %collective-permute-done.11.refs_4_) | copy-start | bytes 1572868
  96.2 36.7 %copy-start = (bf16[512,512]{1,0:T(8,128)(2,1)S(1)}, bf16[512,512]{1,0:T(8,128)(2,1)}, u32[]{:S(2)}) copy-start(bf16[512,512]{1,0:T(8,128)(2,1)} %get-tuple-element.59.refs_0_) | copy-start | bytes 1572868
  96.2 36.7 %all-to-all-start.5 = ((bf16[8,4,64,256]{3,2,1,0:T(8,128)(2,1)}), bf16[8,4,64,256]{3,2,1,0:T(8,128)(2,1)S(1)}, u32[]{:S(2)}, u32[]{:S(2)}) async-start(bf16[8,4,64,256]{3,2,1,0:T(8,128)(2,1)} %bitcast.37), calls=%async_computation.5 | async-start | bytes 2097152 | tf_op jit(solution)/shard_map/all_to_all | solution.py:249
  102.9 27.2 %collective-permute-start.12 = (bf16[512,512]{1,0:T(8,128)(2,1)}, bf16[512,512]{1,0:T(8,128)(2,1)S(1)}, u32[]{:S(2)}, u32[]{:S(2)}) collective-permute-start(bf16[512,512]{1,0:T(8,128)(2,1)} %get-tuple-element.60), channel_id=1, source_target_pairs={{0,1},{1,2},{2,3},{3,0},{4,5},{5,6},{6,7},{7,4},{8,9},{9,10},{10,1... | collective-permute-start | bytes 1572872 | tf_op jit(solution)/shard_map/ppermute | solution.py:245
  104.8 25.3 %collective-permute-start.13 = (bf16[512,512]{1,0:T(8,128)(2,1)}, bf16[512,512]{1,0:T(8,128)(2,1)S(1)}, u32[]{:S(2)}, u32[]{:S(2)}) collective-permute-start(bf16[512,512]{1,0:T(8,128)(2,1)} %get-tuple-element.61), channel_id=1, source_target_pairs={{0,2},{1,3},{2,0},{3,1},{4,6},{5,7},{6,4},{7,5},{8,10},{9,11},{10,... | collective-permute-start | bytes 1572872 | tf_op jit(solution)/shard_map/ppermute | solution.py:245
  107.3 25.6 %collective-permute-start.14 = (bf16[512,512]{1,0:T(8,128)(2,1)}, bf16[512,512]{1,0:T(8,128)(2,1)S(1)}, u32[]{:S(2)}, u32[]{:S(2)}) collective-permute-start(bf16[512,512]{1,0:T(8,128)(2,1)} %get-tuple-element.62), channel_id=1, source_target_pairs={{0,3},{1,0},{2,1},{3,2},{4,7},{5,4},{6,5},{7,6},{8,11},{9,8},{10,9... | collective-permute-start | bytes 1572872 | tf_op jit(solution)/shard_map/ppermute | solution.py:245
  133.9 22.6 %all-to-all-start.6 = ((bf16[8,64,512]{2,1,0:T(8,128)(2,1)}), bf16[8,64,512]{2,1,0:T(8,128)(2,1)S(1)}, u32[]{:S(2)}, u32[]{:S(2)}) async-start(bf16[8,64,512]{2,1,0:T(8,128)(2,1)} %bitcast.16), calls=%async_computation.6 | async-start | bytes 1048576 | tf_op jit(solution)/shard_map/all_to_all | solution.py:249
  140.7 10.3 %collective-permute-start.15 = (bf16[64,256]{1,0:T(8,128)(2,1)S(1)}, bf16[64,256]{1,0:T(8,128)(2,1)S(1)}, u32[]{:S(2)}, u32[]{:S(2)}) collective-permute-start(bf16[64,256]{1,0:T(8,128)(2,1)S(1)} %get-tuple-element.65), channel_id=1, source_target_pairs={{0,1},{1,2},{2,3},{3,0},{4,5},{5,6},{6,7},{7,4},{8,9},{9,10},{10,1... | collective-permute-start | bytes 98312 | tf_op jit(solution)/shard_map/ppermute | solution.py:245
  143.6 7.4 %collective-permute-start.16 = (bf16[64,256]{1,0:T(8,128)(2,1)S(1)}, bf16[64,256]{1,0:T(8,128)(2,1)S(1)}, u32[]{:S(2)}, u32[]{:S(2)}) collective-permute-start(bf16[64,256]{1,0:T(8,128)(2,1)S(1)} %get-tuple-element.66), channel_id=1, source_target_pairs={{0,2},{1,3},{2,0},{3,1},{4,6},{5,7},{6,4},{7,5},{8,10},{9,11},{10,... | collective-permute-start | bytes 98312 | tf_op jit(solution)/shard_map/ppermute | solution.py:245
  149.1 4.8 %collective-permute-start.17 = (bf16[64,256]{1,0:T(8,128)(2,1)S(1)}, bf16[64,256]{1,0:T(8,128)(2,1)S(1)}, u32[]{:S(2)}, u32[]{:S(2)}) collective-permute-start(bf16[64,256]{1,0:T(8,128)(2,1)S(1)} %get-tuple-element.67), channel_id=1, source_target_pairs={{0,3},{1,0},{2,1},{3,2},{4,7},{5,4},{6,5},{7,6},{8,11},{9,8},{10,9... | collective-permute-start | bytes 98312 | tf_op jit(solution)/shard_map/ppermute | solution.py:245
  156.6 14.5 %copy-start.3 = (bf16[128,64]{0,1:T(8,128)(2,1)S(1)}, bf16[128,64]{0,1:T(8,128)(2,1)}, u32[]{:S(2)}) copy-start(bf16[128,64]{0,1:T(8,128)(2,1)} %param.12) | copy-start | bytes 49156
  156.6 14.5 %copy-start.6 = (s32[2,128]{1,0:T(2,128)S(1)}, s32[2,128]{1,0:T(2,128)}, u32[]{:S(2)}) copy-start(s32[2,128]{1,0:T(2,128)} %get-tuple-element.71.refs_1_) | copy-start | bytes 3076
  156.6 14.5 %copy-start.7 = (s32[1,144]{1,0:T(1,128)S(1)}, s32[1,144]{1,0:T(1,128)}, u32[]{:S(2)}) copy-start(s32[1,144]{1,0:T(1,128)} %get-tuple-element.72.refs_2_) | copy-start | bytes 1732
  156.9 14.1 %copy-start.2 = (bf16[144,64]{0,1:T(8,128)(2,1)S(1)}, bf16[144,64]{0,1:T(8,128)(2,1)}, u32[]{:S(2)}) copy-start(bf16[144,64]{0,1:T(8,128)(2,1)} %param.17) | copy-start | bytes 55300
  (5 other events, 26.0 us)
